TPU v7x, 256 devices: a whole 4x4x8 slice. The times are simulated.
256 devices in a mesh: lat: 64 (over x_lo, y, z), head: 4 (over x_hi, core).
Axes of the slice: x: 4 (x_hi: 2, x_lo: 2; x = x_hi * 2 + x_lo), y: 4, z: 8, core: 2. Of those that a mesh axis runs over, the one named last changes fastest.
Arguments:
- tokens: bfloat16 [384, 2, 48, 1024], P('lat', None, 'head'), may hold values from -6 to 6
- output_grad: bfloat16 [384, 2, 48, 1024], P('lat', None, 'head'), may hold values from -6 to 6
- region_labels: int32 [384, 2, 48], P('lat', None, 'head'), may hold values from 0 to 3
- qkv_weight: bfloat16 [3, 1024, 1024], P(None, None, 'head'), may hold values from -0.1875 to 0.1875
- out_weight: bfloat16 [1024, 1024], P('head'), may hold values from -0.1875 to 0.1875
- bias_table: float32 [759, 16], P(None, 'head'), may hold values from -5 to 326
- bias_index: int32 [144, 144], replicated, may hold values from 0 to 758
Outputs:
- input_grad: float32 [384, 2, 48, 1024], P('lat', None, 'head')
- qkv_weight_grad: float32 [3, 1024, 1024], P(None, 'lat', 'head')
- out_weight_grad: float32 [1024, 1024], P('head', 'lat')
- bias_grad: float32 [759, 16], P(None, 'head')
All inputs are finite; a program needn't handle non-finite values.
Results may differ from a plain program's by a relative error of at most 0.0065.
Values may be sent and summed in bfloat16 or wider, within the bound.
No kernel may reach another device: no remote copies, remote signals or barrier semaphores. Data moves between devices by JAX's collectives and lax.ppermute only.
A program may use at most 64 MiB of HBM per device.

v0:
```python
import functools

import jax
import jax.numpy as jnp
import numpy as np
from jax import lax
from jax.experimental import pallas as pl
from jax.experimental.pallas import tpu as pltpu
from jax.sharding import PartitionSpec as P

D = 1024
HD = 64
HEADS = 4
WIDTH = 256
WT = 144
NB = 759
ROWS = 80
BLOCKS = 8
ALL = BLOCKS * ROWS
BAND = 576
NY = 4
NZ = 8
F32 = jnp.float32
BF16 = jnp.bfloat16
NT = (((1,), (1,)), ((), ()))
TN = (((0,), (0,)), ((), ()))


def sent(x, axis, to):
    size = lax.axis_size(axis)
    return lax.ppermute(x, axis, [(i, to(i)) for i in range(size)])


def lat_of(x, y, z):
    return (x * NY + y % NY) * NZ + z % NZ


def moved(dx, dy, dz):
    def to(i):
        x, y, z = i // (NY * NZ), i // NZ % NY, i % NZ
        return lat_of(x ^ dx, y + dy, z + dz)

    return to


def paired(dx, dz):
    def to(i):
        x, y, z = i // (NY * NZ), i // NZ % NY, i % NZ
        return lat_of(x ^ dx, y, z ^ dz)

    return to


def call(kernel, out, args, flops, moved_bytes, vmem=16):
    return pl.pallas_call(
        kernel,
        out_shape=out,
        scratch_shapes=args,
        compiler_params=pltpu.CompilerParams(vmem_limit_bytes=vmem * 2**20),
        cost_estimate=pl.CostEstimate(flops=flops, bytes_accessed=moved_bytes, transcendentals=0),
    )


def shape(dims, dtype):
    return jax.ShapeDtypeStruct(dims, dtype)


def window_order():
    order = np.zeros((WT, WT), np.float32)
    for row in range(6):
        for half in range(2):
            for lon in range(6):
                for lev in range(2):
                    n = row * 24 + half * 12 + lon * 2 + lev
                    order[n, row * 24 + (1 - lev) * 12 + (1 - half) * 6 + lon] = 1
    return order


def turned(x, fill):
    x = jnp.concatenate([x[:, 128:], jnp.full((WT, 112), fill, F32)], axis=1)
    x = jnp.concatenate([x, jnp.full((112, 128), fill, F32)], axis=0)
    return jnp.transpose(x)[:16]


def bias_kernel(table, index, order, bias, places, places_end):
    idx = index[...].astype(F32)
    high = jnp.floor(idx * (1.0 / 32.0))
    low = idx - high * 32.0
    perm = order[...]

    def reordered(x):
        y = jnp.dot(perm, x.astype(BF16), preferred_element_type=F32).astype(BF16)
        return lax.dot_general(y, perm, NT, preferred_element_type=F32)

    own_f = reordered(high) * 32.0 + reordered(low)
    own = own_f.astype(jnp.int32)
    places[...] = own[:, :128]
    places_end[...] = turned(own_f, -1.0).astype(jnp.int32)
    for start, stop in ((0, 128), (128, WT)):
        part = own[:, start:stop]
        if stop - start < 128:
            part = jnp.concatenate([part, jnp.zeros((WT, 128 - stop + start), jnp.int32)], axis=1)
        chunk = lax.shift_right_logical(part, 7)
        lane = lax.bitwise_and(part, 127)
        for head in range(HEADS):
            found = jnp.zeros((WT, 128), F32)
            for c in range(6):
                row = jnp.broadcast_to(table[head : head + 1, c * 128 : (c + 1) * 128], (WT, 128))
                got = jnp.take_along_axis(row, lane, axis=1, mode="promise_in_bounds")
                found = jnp.where(chunk == c, got, found)
            bias[head, :, start:stop] = found[:, : stop - start]


def eastern(width):
    row = lax.broadcasted_iota(jnp.int32, (72, width), 0)
    return lax.rem(row, 24) < 12


def to_windows(rows, wins, own, step):
    first = eastern(rows.shape[1])
    for w in range(4):
        near = lax.bitwise_xor(own, w) * (2 * step)
        east = lax.bitwise_xor(own, (w + 1) % 4) * (2 * step)
        for r in range(2):
            a = rows[pl.ds(pl.multiple_of(near + r * step, 8), 72), :]
            b = rows[pl.ds(pl.multiple_of(east + r * step, 8), 72), :]
            wins[w, r * 72 : (r + 1) * 72, :] = jnp.where(first, b, a)


def from_windows(wins, rows, own, step):
    first = eastern(rows.shape[1])
    for s in range(4):
        start = lax.bitwise_xor(own, s) * (2 * step)
        for r in range(2):
            a = wins[s, r * 72 : (r + 1) * 72, :]
            b = wins[(s + 3) % 4, r * 72 : (r + 1) * 72, :]
            at = pl.multiple_of(start + r * step, 8)
            rows[pl.ds(at, 72), :] = jnp.where(first, b, a)
            if step > 72:
                rows[pl.ds(pl.multiple_of(at + 72, 8), step - 72), :] = jnp.zeros((step - 72, rows.shape[1]), F32)


def head_mask(head, rows):
    lane = lax.broadcasted_iota(jnp.int32, (rows, WIDTH), 1)
    return lax.shift_right_logical(lane, 6) == head


def only(head, x):
    return jnp.where(head_mask(head, x.shape[0]), x, 0.0).astype(BF16)


def forward_kernel(t0, t1, t2, t3, t4, t5, t6, t7, weight, bias, tall, qkv, probs, att, rows, wins, labels):
    own = lax.axis_index("head")
    pieces = (t0, t1, t2, t3, t4, t5, t6, t7)
    labels[...] = jnp.zeros_like(labels)
    row = lax.broadcasted_iota(jnp.int32, (8, WIDTH), 0)
    for p in range(4):
        shard = lax.bitwise_xor(own, p)
        before = lax.rem(shard + 3, 4)
        for r in range(2):
            tall[pl.ds((p * 2 + r) * ROWS, ROWS), :] = pieces[p * 2 + r][...]
            marks = pieces[p * 2 + r][64:80, :WIDTH].astype(F32)[8:16]
            labels[shard] += jnp.where(row < 4, marks, 0.0)
            labels[before] += jnp.where(row < 4, pltpu.roll(marks, 4, 0), 0.0)
    for m in range(3):
        rows[...] = jnp.dot(tall[...], weight[m], preferred_element_type=F32).astype(BF16).astype(F32)
        to_windows(rows, wins, own, ROWS)
        qkv[m] = wins[...].astype(BF16)

    def window(w, _):
        marks = labels[w].astype(BF16)
        same = lax.dot_general(marks, marks, TN, preferred_element_type=F32)[:WT, :WT] > 0.5
        q = qkv[0, w].astype(F32)
        k = qkv[1, w]
        v = qkv[2, w].astype(F32)
        total = jnp.zeros((WT, WIDTH), F32)
        for head in range(HEADS):
            s = lax.dot_general(only(head, q), k, NT, preferred_element_type=F32)
            s = s * 0.125 + bias[head]
            s = jnp.where(same, s, -jnp.inf)
            e = jnp.exp(s - jnp.max(s, axis=1, keepdims=True))
            pr = e / jnp.sum(e, axis=1, keepdims=True)
            probs[w, head] = pr
            total += jnp.dot(pr.astype(BF16), only(head, v), preferred_element_type=F32)
        wins[w] = total
        return 0

    lax.fori_loop(0, 4, window, 0)
    band = rows.at[pl.ds(0, BAND), :]
    from_windows(wins, band, own, 72)
    att[...] = band[...].astype(BF16)


def segment_sums(sums, ends, places, places_end):
    low_row = lax.broadcasted_iota(jnp.int32, (128, 256), 0)

    def terms(idx, values):
        high = jnp.right_shift(idx, 7)
        low = lax.bitwise_and(idx, 127)
        a = jnp.concatenate([jnp.where(high == c, values, 0.0) for c in range(6)], axis=0)
        return a.astype(BF16), (low_row == low).astype(F32).astype(BF16)

    def added(acc, pairs):
        a = jnp.concatenate([p[0] for p in pairs], axis=1)
        b = jnp.concatenate([p[1] for p in pairs], axis=1)
        return acc + lax.dot_general(a, b, NT, preferred_element_type=F32)

    def split(block):
        top = block.astype(BF16).astype(F32)
        return top, block - top

    def rows_of(blocks, i):
        return jnp.concatenate([b[0][i : i + 1] for b in blocks] + [b[1][i : i + 1] for b in blocks], axis=0)

    def step(i, acc):
        at = pl.ds(pl.multiple_of(i * 8, 8), 8)
        idx = places[at, :]
        blocks = [split(sums[head, at, :128]) for head in range(HEADS)]
        pairs = []
        for j in range(0, 8, 2):
            both = jnp.concatenate([idx[j : j + 1], idx[j + 1 : j + 2]], axis=1)
            pairs.append(terms(both, jnp.concatenate([rows_of(blocks, j), rows_of(blocks, j + 1)], axis=1)))
        return added(acc, pairs)

    acc = lax.fori_loop(0, 18, step, jnp.zeros((48, 128), F32))

    def last(i, acc):
        at = pl.ds(pl.multiple_of(i * 8, 8), 8)
        idx = places_end[at, :]
        blocks = [split(ends[head, at, :]) for head in range(HEADS)]
        for j in range(0, 8, 4):
            acc = added(acc, [terms(idx[n : n + 1], rows_of(blocks, n)) for n in range(j, j + 4)])
        return acc

    acc = lax.fori_loop(0, 2, last, acc)
    return jnp.concatenate([acc[c * 8 : (c + 1) * 8] for c in range(6)], axis=1)


def bias_total(s):
    return s + pltpu.roll(s, 4, 0)


def bias_rows(total):
    top = total.astype(BF16).astype(F32)
    row = lax.broadcasted_iota(jnp.int32, total.shape, 0)
    both = jnp.where(row < 4, top, total - top)
    return jnp.concatenate([both, jnp.zeros_like(both)], axis=0).astype(BF16)


def backward_kernel(g0, g1, g2, g3, wo, qkv, probs, tall, att, places, places_end, grads, r0, r1, r2, r3, gall, rows, wins, outs, sums, ends):
    own = lax.axis_index("head")
    for p, piece in enumerate((g0, g1, g2, g3)):
        gall[p * WT : (p + 1) * WT, :] = piece[...]
    band = rows.at[pl.ds(0, BAND), :]
    delta = lax.dot_general(gall[...], wo[...], NT, preferred_element_type=F32)
    band[...] = delta.astype(BF16).astype(F32)
    to_windows(band, wins, own, 72)
    sums[...] = jnp.zeros_like(sums)

    def window(w, _):
        d = wins[w]
        q = qkv[0, w].astype(F32)
        k = qkv[1, w].astype(F32)
        v = qkv[2, w]
        dq = jnp.zeros((WT, WIDTH), F32)
        dk = jnp.zeros((WT, WIDTH), F32)
        dv = jnp.zeros((WT, WIDTH), F32)
        for head in range(HEADS):
            pr = probs[w, head]
            dh = only(head, d)
            dp = lax.dot_general(dh, v, NT, preferred_element_type=F32)
            ds = pr * (dp - jnp.sum(pr * dp, axis=1, keepdims=True))
            sums[head] += ds
            dsb = ds.astype(BF16)
            dv += lax.dot_general(pr.astype(BF16), dh, TN, preferred_element_type=F32)
            dq += jnp.dot(dsb, only(head, k), preferred_element_type=F32)
            dk += lax.dot_general(dsb, only(head, q), TN, preferred_element_type=F32)
        outs[0, w] = dq * 0.125
        outs[1, w] = dk * 0.125
        outs[2, w] = dv
        return 0

    lax.fori_loop(0, 4, window, 0)
    for m in range(3):
        from_windows(outs.at[m], rows, own, ROWS)
        grads[:, m * WIDTH : (m + 1) * WIDTH] = rows[...].astype(BF16)

    for head in range(HEADS):
        ends[head] = turned(sums[head], 0.0)
    found = bias_total(segment_sums(sums, ends, places, places_end))
    found = bias_rows(jnp.concatenate([found, jnp.zeros((8, 256), F32)], axis=1))

    y = lax.rem(lax.axis_index("lat") // NZ, NY)
    for d, out in enumerate((r0, r1, r2, r3)):
        to = lax.rem(y + d, NY)
        out[256:272, :] = found
        for x in range(2):
            lanes = pl.ds(pl.multiple_of(x * 512 + to * 128, 128), 128)
            out[x * 128 : (x + 1) * 128, : 3 * WIDTH] = lax.dot_general(
                tall[:, lanes], grads[...], TN, preferred_element_type=F32
            ).astype(BF16)
            out[x * 128 : (x + 1) * 128, 3 * WIDTH :] = lax.dot_general(
                gall[:, lanes], att[...], TN, preferred_element_type=F32
            ).astype(BF16)


def input_kernel(grads, weight, near, far, given):
    total = jnp.zeros((ALL, D), F32)
    for m in range(3):
        total += lax.dot_general(
            grads[:, m * WIDTH : (m + 1) * WIDTH], weight[m], NT, preferred_element_type=F32
        )
    for p, out in enumerate((near.at[...], given.at[:WT, :], far.at[...], given.at[WT:, :])):
        start = p * 2 * ROWS
        both = jnp.concatenate([total[start : start + 72], total[start + ROWS : start + ROWS + 72]], axis=0)
        out[...] = both.astype(BF16)


def stage_rows(parts, rows):
    total = parts[0][rows, :].astype(F32)
    for part in parts[1:]:
        total += part[rows, :].astype(F32)
    return total


def y_sum_kernel(a, b, c, d, *outs):
    parts = (a, b, c, d)
    lat = lax.axis_index("lat")
    x, z = lat // (NY * NZ), lax.rem(lat, 2)
    found = bias_rows(bias_total(stage_rows(parts, pl.ds(256, 16))[:8]))
    for dx in range(2):
        for dz in range(2):
            out = outs[dx * 2 + dz]
            start = lax.bitwise_xor(x, dx) * 128 + lax.bitwise_xor(z, dz) * 16
            for k in range(4):
                rows = pl.ds(pl.multiple_of(start + k * 32, 16), 16)
                out[k * 16 : (k + 1) * 16, :] = stage_rows(parts, rows).astype(BF16)
            out[64:80, :] = found


def pair_sum_kernel(a, b, c, d, *outs):
    parts = (a, b, c, d)
    z = lax.rem(lax.axis_index("lat"), NZ) // 2
    found = bias_rows(bias_total(stage_rows(parts, pl.ds(64, 16))[:8]))
    for e in range(4):
        rows = pl.ds(pl.multiple_of(lax.rem(z + e, 4) * 16, 16), 16)
        outs[e][:16, :] = stage_rows(parts, rows).astype(BF16)
        outs[e][16:, :] = found


def last_sum_kernel(a, b, c, d, qkv, out, bias):
    parts = (a, b, c, d)
    total = stage_rows(parts, pl.ds(0, 16))
    for m in range(3):
        qkv[m] = total[:, m * WIDTH : (m + 1) * WIDTH]
    out[...] = total[:, 3 * WIDTH :]
    bias[...] = bias_total(stage_rows(parts, pl.ds(16, 16))[:8])[:4, :NB]


def halves(source):
    x = source.transpose(0, 2, 1, 3).reshape(2, 72, source.shape[-1])
    return x[0], x[1]


def label_rows(labels, first):
    row = lax.broadcasted_iota(jnp.int32, (8, 72), 0)
    col = lax.broadcasted_iota(jnp.int32, (8, 72), 1)
    hit = (row % 4 == labels[None]) & ((row >= 4) == (col % 24 < 12))
    return jnp.pad(hit.astype(BF16), ((0, 0), (first, D - 72 - first)))


def shards(tokens, output_grad, region_labels, qkv_weight, out_weight, bias_table, bias_index):
    core = functools.partial(sent, axis="head", to=lambda i: i ^ 1)
    across = functools.partial(sent, axis="head", to=lambda i: i ^ 2)
    back = functools.partial(sent, axis="lat", to=lambda i: (i - 1) % 64)
    onward = functools.partial(sent, axis="lat", to=lambda i: (i + 1) % 64)

    t_low, t_high = halves(tokens)
    l_low, l_high = halves(region_labels[..., None])
    t_low = back(jnp.concatenate([t_low, label_rows(l_low[:, 0], 72)]))
    t_high = jnp.concatenate([t_high, label_rows(l_high[:, 0], 0)])
    g_low, g_high = halves(output_grad)
    g = jnp.concatenate([g_high, back(g_low)])

    far_high, far_low, far_g = across(t_high), across(t_low), across(g)
    t_pieces = (t_high, t_low, core(t_high), core(t_low), far_high, far_low, core(far_high), core(far_low))
    g_pieces = (g, core(g), far_g, core(far_g))

    table = jnp.pad(bias_table.T, ((0, 0), (0, 9)))
    bias, places, places_end = call(
        bias_kernel,
        (shape((HEADS, WT, WT), F32), shape((WT, 128), jnp.int32), shape((16, 256), jnp.int32)),
        (),
        2 * 10**7,
        10**6,
    )(table, bias_index, jnp.asarray(window_order(), BF16))

    tall, qkv, probs, att = call(
        forward_kernel,
        (
            shape((ALL, D), BF16),
            shape((3, 4, WT, WIDTH), BF16),
            shape((4, HEADS, WT, WT), F32),
            shape((BAND, WIDTH), BF16),
        ),
        [pltpu.VMEM((ALL, WIDTH), F32), pltpu.VMEM((4, WT, WIDTH), F32), pltpu.VMEM((4, 8, WIDTH), F32)],
        2 * 10**9,
        10**7,
    )(*t_pieces, qkv_weight, bias)

    grads, *blocks = call(
        backward_kernel,
        (shape((ALL, 3 * WIDTH), BF16),) + (shape((272, D), BF16),) * NY,
        [
            pltpu.VMEM((BAND, D), BF16),
            pltpu.VMEM((ALL, WIDTH), F32),
            pltpu.VMEM((4, WT, WIDTH), F32),
            pltpu.VMEM((3, 4, WT, WIDTH), F32),
            pltpu.VMEM((HEADS, WT, WT), F32),
            pltpu.VMEM((HEADS, 16, 256), F32),
        ],
        3 * 10**9,
        10**7,
    )(*g_pieces, out_weight, qkv, probs, tall, att, places, places_end)

    got = [blocks[0]] + [sent(blocks[d], "lat", moved(0, d, 0)) for d in range(1, NY)]
    parts = call(y_sum_kernel, (shape((80, D), BF16),) * 4, (), 10**6, 3 * 10**6, 8)(*got)
    got = [parts[0]] + [sent(parts[d], "lat", paired(d // 2, d % 2)) for d in range(1, 4)]
    parts = call(pair_sum_kernel, (shape((32, D), BF16),) * 4, (), 10**6, 10**6, 8)(*got)
    got = [parts[0]] + [sent(parts[e], "lat", moved(0, 0, 2 * e)) for e in range(1, 4)]
    qkv_grad, out_grad, bias_grad = call(
        last_sum_kernel,
        (shape((3, 16, WIDTH), F32), shape((16, WIDTH), F32), shape((HEADS, NB), F32)),
        (),
        10**6,
        10**6,
        8,
    )(*got)

    near, far, given = call(
        input_kernel, (shape((WT, D), BF16), shape((WT, D), BF16), shape((2 * WT, D), BF16)), (), 10**9, 5 * 10**6
    )(grads, qkv_weight)
    given = core(given)
    far = (far.astype(F32) + given[WT:].astype(F32)).astype(BF16)
    near = near.astype(F32) + given[:WT].astype(F32) + across(far).astype(F32)
    low = onward(near[72:].astype(BF16)).astype(F32)
    input_grad = jnp.concatenate([low, near[:72]]).reshape(6, 12, 2, D).transpose(0, 2, 1, 3)
    return input_grad, qkv_grad, out_grad.T, bias_grad.T


def solution(mesh):
    return jax.shard_map(
        shards,
        mesh=mesh,
        in_specs=(
            P("lat", None, "head", None),
            P("lat", None, "head", None),
            P("lat", None, "head"),
            P(None, None, "head"),
            P("head", None),
            P(None, "head"),
            P(),
        ),
        out_specs=(
            P("lat", None, "head", None),
            P(None, "lat", "head"),
            P("head", "lat"),
            P(None, "head"),
        ),
        check_vma=False,
    )
```

profile of v0, /device:TPU:2, one launch (start us, length us, event | category | flops | bytes accessed | tf_op | source)
XLA Modules:
  0.0 110.1 jit_solution(12508822218735384446)
XLA Ops:
  2.0 1.2 %fusion.3 = (bf16[3,12,2,1024]{3,2,1,0:T(2,128)(2,1)S(1)}, bf16[3,12,2,1024]{3,2,1,0:T(2,128)(2,1)S(1)}) fusion(bf16[6,12,2,1024]{3,2,1,0:T(2,128)(2,1)} %bitcast.14), kind=kLoop, calls=%fused_computation.23 | loop fusion | bytes 589824 | tf_op jit(solution)/shard_map/slice | solution.py:362
  3.4 8.4 %collective-permute-start.4 = (bf16[80,1024]{1,0:T(8,128)(2,1)S(1)}, bf16[80,1024]{1,0:T(8,128)(2,1)S(1)}, u32[]{:S(2)}, u32[]{:S(2)}) collective-permute-start(bf16[80,1024]{1,0:T(8,128)(2,1)S(1)} %pad_maximum_fusion.2), channel_id=1, source_target_pairs={{0,252},{4,0},{8,4},{12,8},{16,12},{20,16},{24,20},{28,24},{32,28}... | collective-permute-start | bytes 491528 | tf_op jit(solution)/shard_map/ppermute | solution.py:31
  13.2 5.1 %collective-permute-done = bf16[72,1024]{1,0:T(8,128)(2,1)S(1)} collective-permute-done((bf16[72,1024]{1,0:T(8,128)(2,1)S(1)}, bf16[72,1024]{1,0:T(8,128)(2,1)S(1)}, u32[]{:S(2)}, u32[]{:S(2)}) %collective-permute-start) | collective-permute-done | bytes 147488 | tf_op jit(solution)/shard_map/ppermute | solution.py:31
  18.3 2.5 %collective-permute-start.2 = (bf16[144,1024]{1,0:T(8,128)(2,1)S(1)}, bf16[144,1024]{1,0:T(8,128)(2,1)S(1)}, u32[]{:S(2)}, u32[]{:S(2)}) collective-permute-start(bf16[144,1024]{1,0:T(8,128)(2,1)S(1)} %constant_dynamic-update-slice_fusion.g0), channel_id=1, source_target_pairs={{0,2},{1,3},{2,0},{3,1},{4,6},{5,7},{6,4},{7,5},{8,10},{9,11},{10,... | collective-permute-start | bytes 884744 | tf_op jit(solution)/shard_map/ppermute | solution.py:31
  20.9 1.2 %collective-permute-start.7 = (bf16[80,1024]{1,0:T(8,128)(2,1)S(1)}, bf16[80,1024]{1,0:T(8,128)(2,1)S(1)}, u32[]{:S(2)}, u32[]{:S(2)}) collective-permute-start(bf16[80,1024]{1,0:T(8,128)(2,1)S(1)} %pad_maximum_fusion.1.t0), channel_id=1, source_target_pairs={{0,2},{1,3},{2,0},{3,1},{4,6},{5,7},{6,4},{7,5},{8,10},{9,11},{10,... | collective-permute-start | bytes 491528 | tf_op jit(solution)/shard_map/ppermute | solution.py:31
  22.1 2.4 %collective-permute-start.8 = (bf16[80,1024]{1,0:T(8,128)(2,1)S(1)}, bf16[80,1024]{1,0:T(8,128)(2,1)S(1)}, u32[]{:S(2)}, u32[]{:S(2)}) collective-permute-start(bf16[80,1024]{1,0:T(8,128)(2,1)S(1)} %collective-permute-done.4.t1), channel_id=1, source_target_pairs={{0,2},{1,3},{2,0},{3,1},{4,6},{5,7},{6,4},{7,5},{8,10},{9,11},{10,... | collective-permute-start | bytes 491528 | tf_op jit(solution)/shard_map/ppermute | solution.py:31
  25.0 8.1 %collective-permute-done.7.t4 = bf16[80,1024]{1,0:T(8,128)(2,1)S(1)} collective-permute-done((bf16[80,1024]{1,0:T(8,128)(2,1)S(1)}, bf16[80,1024]{1,0:T(8,128)(2,1)S(1)}, u32[]{:S(2)}, u32[]{:S(2)}) %collective-permute-start.7) | collective-permute-done | bytes 163872 | tf_op jit(solution)/shard_map/ppermute | solution.py:31
  33.1 1.8 %collective-permute-done.8.t5 = bf16[80,1024]{1,0:T(8,128)(2,1)S(1)} collective-permute-done((bf16[80,1024]{1,0:T(8,128)(2,1)S(1)}, bf16[80,1024]{1,0:T(8,128)(2,1)S(1)}, u32[]{:S(2)}, u32[]{:S(2)}) %collective-permute-start.8) | collective-permute-done | bytes 163872 | tf_op jit(solution)/shard_map/ppermute | solution.py:31
  35.7 2.6 %shard_map.111 = (f32[4,144,144]{2,1,0:T(8,128)S(1)}, s32[144,128]{1,0:T(8,128)S(1)}, s32[16,256]{1,0:T(8,128)S(1)}) custom-call(f32[4,768]{1,0:T(4,128)S(1)} %pad.22.table, s32[144,144]{1,0:T(8,128)S(1)} %copy-done, bf16[144,144]{1,0:T(8,128)(2,1)S(1)} %copy-done.1), custom_call_target="tpu_custom_call" | custom-call | flops 20000000 | bytes 1000000 | tf_op jit(solution)/shard_map/pallas_call | solution.py:390
  38.3 4.4 %shard_map.112 = (bf16[640,1024]{1,0:T(8,128)(2,1)S(1)}, bf16[3,4,144,256]{3,2,1,0:T(8,128)(2,1)S(1)}, f32[4,4,144,144]{3,2,1,0:T(8,128)S(1)}, bf16[576,256]{1,0:T(8,128)(2,1)S(1)}) custom-call(bf16[80,1024]{1,0:T(8,128)(2,1)S(1)} %pad_maximum_fusion.1.t0, bf16[80,1024]{1,0:T(8,128)(2,1)S(1)} %collective-permute-done.4.t1, ...), custom_call_target="tpu_custom_call" | custom-call | flops 2000000000 | bytes 10000000 | tf_op jit(solution)/shard_map/pallas_call | solution.py:398
  42.7 12.1 %shard_map.113 = (bf16[640,768]{1,0:T(8,128)(2,1)S(1)}, bf16[272,1024]{1,0:T(8,128)(2,1)S(1)}, bf16[272,1024]{1,0:T(8,128)(2,1)S(1)}, bf16[272,1024]{1,0:T(8,128)(2,1)S(1)}, bf16[272,1024]{1,0:T(8,128)(2,1)S(1)}) custom-call(bf16[144,1024]{1,0:T(8,128)(2,1)S(1)} %constant_dynamic-update-slice_fusion.g0, bf16[144,1024]{1,0:T(8,128)(2,1)S(1)} %collective-permute-done.1.g1, ...), custom_call_target="tpu_custom_call" | custom-call | flops 3000000000 | bytes 10000000 | tf_op jit(solution)/shard_map/pallas_call | solution.py:411
  54.8 1.2 %shard_map.114 = (bf16[144,1024]{1,0:T(8,128)(2,1)S(1)}, bf16[144,1024]{1,0:T(8,128)(2,1)S(1)}, bf16[288,1024]{1,0:T(8,128)(2,1)S(1)}) custom-call(bf16[640,768]{1,0:T(8,128)(2,1)S(1)} %get-tuple-element.37.grads, bf16[3,1024,256]{2,1,0:T(8,128)(2,1)S(1)} %copy-done.2), custom_call_target="tpu_custom_call" | custom-call | flops 1000000000 | bytes 5000000 | tf_op jit(solution)/shard_map/pallas_call | solution.py:440
  56.4 2.2 %collective-permute-start.15 = (bf16[272,1024]{1,0:T(8,128)(2,1)S(1)}, bf16[272,1024]{1,0:T(8,128)(2,1)S(1)}, u32[]{:S(2)}, u32[]{:S(2)}) collective-permute-start(bf16[272,1024]{1,0:T(8,128)(2,1)S(1)} %get-tuple-element.43), channel_id=1, source_target_pairs={{0,64},{4,68},{8,72},{12,76},{16,80},{20,84},{24,88},{28,92},{32,9... | collective-permute-start | bytes 1671176 | tf_op jit(solution)/shard_map/ppermute | solution.py:31
  59.8 2.4 %collective-permute-start.12 = (bf16[144,1024]{1,0:T(8,128)(2,1)S(1)}, bf16[144,1024]{1,0:T(8,128)(2,1)S(1)}, u32[]{:S(2)}, u32[]{:S(2)}) collective-permute-start(bf16[144,1024]{1,0:T(8,128)(2,1)S(1)} %add_convert_fusion), channel_id=1, source_target_pairs={{0,2},{1,3},{2,0},{3,1},{4,6},{5,7},{6,4},{7,5},{8,10},{9,11},{10,... | collective-permute-start | bytes 884744 | tf_op jit(solution)/shard_map/ppermute | solution.py:31
  62.2 22.1 %collective-permute-done.14.b = bf16[272,1024]{1,0:T(8,128)(2,1)S(1)} collective-permute-done((bf16[272,1024]{1,0:T(8,128)(2,1)S(1)}, bf16[272,1024]{1,0:T(8,128)(2,1)S(1)}, u32[]{:S(2)}, u32[]{:S(2)}) %collective-permute-start.14) | collective-permute-done | bytes 557088 | tf_op jit(solution)/shard_map/ppermute | solution.py:31
  85.3 1.8 %collective-permute-start.18 = (bf16[80,1024]{1,0:T(8,128)(2,1)S(1)}, bf16[80,1024]{1,0:T(8,128)(2,1)S(1)}, u32[]{:S(2)}, u32[]{:S(2)}) collective-permute-start(bf16[80,1024]{1,0:T(8,128)(2,1)S(1)} %get-tuple-element.47), channel_id=1, source_target_pairs={{0,128},{4,132},{8,136},{12,140},{16,144},{20,148},{24,152},{28,15... | collective-permute-start | bytes 491528 | tf_op jit(solution)/shard_map/ppermute | solution.py:31
  87.1 1.7 %collective-permute-start.19 = (bf16[80,1024]{1,0:T(8,128)(2,1)S(1)}, bf16[80,1024]{1,0:T(8,128)(2,1)S(1)}, u32[]{:S(2)}, u32[]{:S(2)}) collective-permute-start(bf16[80,1024]{1,0:T(8,128)(2,1)S(1)} %get-tuple-element.48), channel_id=1, source_target_pairs={{0,132},{4,128},{8,140},{12,136},{16,148},{20,144},{24,156},{28,15... | collective-permute-start | bytes 491528 | tf_op jit(solution)/shard_map/ppermute | solution.py:31
  89.4 3.0 %collective-permute-done.17.b = bf16[80,1024]{1,0:T(8,128)(2,1)S(1)} collective-permute-done((bf16[80,1024]{1,0:T(8,128)(2,1)S(1)}, bf16[80,1024]{1,0:T(8,128)(2,1)S(1)}, u32[]{:S(2)}, u32[]{:S(2)}) %collective-permute-start.17) | collective-permute-done | bytes 163872 | tf_op jit(solution)/shard_map/ppermute | solution.py:31
  92.3 1.1 %collective-permute-done.18.c = bf16[80,1024]{1,0:T(8,128)(2,1)S(1)} collective-permute-done((bf16[80,1024]{1,0:T(8,128)(2,1)S(1)}, bf16[80,1024]{1,0:T(8,128)(2,1)S(1)}, u32[]{:S(2)}, u32[]{:S(2)}) %collective-permute-start.18) | collective-permute-done | bytes 163872 | tf_op jit(solution)/shard_map/ppermute | solution.py:31
  93.4 1.6 %collective-permute-done.19.d = bf16[80,1024]{1,0:T(8,128)(2,1)S(1)} collective-permute-done((bf16[80,1024]{1,0:T(8,128)(2,1)S(1)}, bf16[80,1024]{1,0:T(8,128)(2,1)S(1)}, u32[]{:S(2)}, u32[]{:S(2)}) %collective-permute-start.19) | collective-permute-done | bytes 163872 | tf_op jit(solution)/shard_map/ppermute | solution.py:31
  95.9 7.1 %collective-permute-start.21 = (bf16[32,1024]{1,0:T(8,128)(2,1)S(1)}, bf16[32,1024]{1,0:T(8,128)(2,1)S(1)}, u32[]{:S(2)}, u32[]{:S(2)}) collective-permute-start(bf16[32,1024]{1,0:T(8,128)(2,1)S(1)} %get-tuple-element.51), channel_id=1, source_target_pairs={{0,16},{4,20},{8,24},{12,28},{16,0},{20,4},{24,8},{28,12},{32,48},... | collective-permute-start | bytes 196616 | tf_op jit(solution)/shard_map/ppermute | solution.py:31
  103.0 2.4 %collective-permute-done.20.b = bf16[32,1024]{1,0:T(8,128)(2,1)S(1)} collective-permute-done((bf16[32,1024]{1,0:T(8,128)(2,1)S(1)}, bf16[32,1024]{1,0:T(8,128)(2,1)S(1)}, u32[]{:S(2)}, u32[]{:S(2)}) %collective-permute-start.20) | collective-permute-done | bytes 65568 | tf_op jit(solution)/shard_map/ppermute | solution.py:31
  106.5 1.7 %collective-permute-done.22.d = bf16[32,1024]{1,0:T(8,128)(2,1)S(1)} collective-permute-done((bf16[32,1024]{1,0:T(8,128)(2,1)S(1)}, bf16[32,1024]{1,0:T(8,128)(2,1)S(1)}, u32[]{:S(2)}, u32[]{:S(2)}) %collective-permute-start.22) | collective-permute-done | bytes 65568 | tf_op jit(solution)/shard_map/ppermute | solution.py:31
  108.9 1.2 %reshape.28 = f32[6,12,2,1024]{3,2,1,0:T(2,128)} reshape(f32[144,1024]{1,0:T(8,128)S(1)} %pad_maximum_fusion) | data formatting | bytes 1179648 | tf_op jit(solution)/shard_map/reshape | solution.py:447
  (71 shorter events, 10.0 us)
Async XLA Ops:
  3.3 34.9 %copy-start.2 = (bf16[3,1024,256]{2,1,0:T(8,128)(2,1)S(1)}, bf16[3,1024,256]{2,1,0:T(8,128)(2,1)}, u32[]{:S(2)}) copy-start(bf16[3,1024,256]{2,1,0:T(8,128)(2,1)} %weight.3) | copy-start | bytes 4718596
  3.4 18.7 %collective-permute-start.4 = (bf16[80,1024]{1,0:T(8,128)(2,1)S(1)}, bf16[80,1024]{1,0:T(8,128)(2,1)S(1)}, u32[]{:S(2)}, u32[]{:S(2)}) collective-permute-start(bf16[80,1024]{1,0:T(8,128)(2,1)S(1)} %pad_maximum_fusion.2), channel_id=1, source_target_pairs={{0,252},{4,0},{8,4},{12,8},{16,12},{20,16},{24,20},{28,24},{32,28}... | collective-permute-start | bytes 491528 | tf_op jit(solution)/shard_map/ppermute | solution.py:31
  12.0 6.3 %collective-permute-start = (bf16[72,1024]{1,0:T(8,128)(2,1)S(1)}, bf16[72,1024]{1,0:T(8,128)(2,1)S(1)}, u32[]{:S(2)}, u32[]{:S(2)}) collective-permute-start(bf16[72,1024]{1,0:T(8,128)(2,1)S(1)} %squeeze.13), channel_id=1, source_target_pairs={{0,252},{4,0},{8,4},{12,8},{16,12},{20,16},{24,20},{28,24},{32,28}... | collective-permute-start | bytes 442376 | tf_op jit(solution)/shard_map/ppermute | solution.py:31
  18.3 17.0 %collective-permute-start.2 = (bf16[144,1024]{1,0:T(8,128)(2,1)S(1)}, bf16[144,1024]{1,0:T(8,128)(2,1)S(1)}, u32[]{:S(2)}, u32[]{:S(2)}) collective-permute-start(bf16[144,1024]{1,0:T(8,128)(2,1)S(1)} %constant_dynamic-update-slice_fusion.g0), channel_id=1, source_target_pairs={{0,2},{1,3},{2,0},{3,1},{4,6},{5,7},{6,4},{7,5},{8,10},{9,11},{10,... | collective-permute-start | bytes 884744 | tf_op jit(solution)/shard_map/ppermute | solution.py:31
  20.9 12.2 %collective-permute-start.7 = (bf16[80,1024]{1,0:T(8,128)(2,1)S(1)}, bf16[80,1024]{1,0:T(8,128)(2,1)S(1)}, u32[]{:S(2)}, u32[]{:S(2)}) collective-permute-start(bf16[80,1024]{1,0:T(8,128)(2,1)S(1)} %pad_maximum_fusion.1.t0), channel_id=1, source_target_pairs={{0,2},{1,3},{2,0},{3,1},{4,6},{5,7},{6,4},{7,5},{8,10},{9,11},{10,... | collective-permute-start | bytes 491528 | tf_op jit(solution)/shard_map/ppermute | solution.py:31
  22.1 12.8 %collective-permute-start.8 = (bf16[80,1024]{1,0:T(8,128)(2,1)S(1)}, bf16[80,1024]{1,0:T(8,128)(2,1)S(1)}, u32[]{:S(2)}, u32[]{:S(2)}) collective-permute-start(bf16[80,1024]{1,0:T(8,128)(2,1)S(1)} %collective-permute-done.4.t1), channel_id=1, source_target_pairs={{0,2},{1,3},{2,0},{3,1},{4,6},{5,7},{6,4},{7,5},{8,10},{9,11},{10,... | collective-permute-start | bytes 491528 | tf_op jit(solution)/shard_map/ppermute | solution.py:31
  24.5 10.4 %collective-permute-start.5 = (bf16[80,1024]{1,0:T(8,128)(2,1)S(1)}, bf16[80,1024]{1,0:T(8,128)(2,1)S(1)}, u32[]{:S(2)}, u32[]{:S(2)}) collective-permute-start(bf16[80,1024]{1,0:T(8,128)(2,1)S(1)} %pad_maximum_fusion.1.t0), channel_id=1, source_target_pairs={{0,1},{1,0},{2,3},{3,2},{4,5},{5,4},{6,7},{7,6},{8,9},{9,8},{10,11... | collective-permute-start | bytes 491528 | tf_op jit(solution)/shard_map/ppermute | solution.py:31
  24.5 13.8 %collective-permute-start.6 = (bf16[80,1024]{1,0:T(8,128)(2,1)S(1)}, bf16[80,1024]{1,0:T(8,128)(2,1)S(1)}, u32[]{:S(2)}, u32[]{:S(2)}) collective-permute-start(bf16[80,1024]{1,0:T(8,128)(2,1)S(1)} %collective-permute-done.4.t1), channel_id=1, source_target_pairs={{0,1},{1,0},{2,3},{3,2},{4,5},{5,4},{6,7},{7,6},{8,9},{9,8},{10,11... | collective-permute-start | bytes 491528 | tf_op jit(solution)/shard_map/ppermute | solution.py:31
  33.1 5.2 %collective-permute-start.9 = (bf16[80,1024]{1,0:T(8,128)(2,1)S(1)}, bf16[80,1024]{1,0:T(8,128)(2,1)S(1)}, u32[]{:S(2)}, u32[]{:S(2)}) collective-permute-start(bf16[80,1024]{1,0:T(8,128)(2,1)S(1)} %collective-permute-done.7.t4), channel_id=1, source_target_pairs={{0,1},{1,0},{2,3},{3,2},{4,5},{5,4},{6,7},{7,6},{8,9},{9,8},{10,11... | collective-permute-start | bytes 491528 | tf_op jit(solution)/shard_map/ppermute | solution.py:31
  34.8 3.4 %collective-permute-start.10 = (bf16[80,1024]{1,0:T(8,128)(2,1)S(1)}, bf16[80,1024]{1,0:T(8,128)(2,1)S(1)}, u32[]{:S(2)}, u32[]{:S(2)}) collective-permute-start(bf16[80,1024]{1,0:T(8,128)(2,1)S(1)} %collective-permute-done.8.t5), channel_id=1, source_target_pairs={{0,1},{1,0},{2,3},{3,2},{4,5},{5,4},{6,7},{7,6},{8,9},{9,8},{10,11... | collective-permute-start | bytes 491528 | tf_op jit(solution)/shard_map/ppermute | solution.py:31
  34.8 7.9 %collective-permute-start.1 = (bf16[144,1024]{1,0:T(8,128)(2,1)S(1)}, bf16[144,1024]{1,0:T(8,128)(2,1)S(1)}, u32[]{:S(2)}, u32[]{:S(2)}) collective-permute-start(bf16[144,1024]{1,0:T(8,128)(2,1)S(1)} %constant_dynamic-update-slice_fusion.g0), channel_id=1, source_target_pairs={{0,1},{1,0},{2,3},{3,2},{4,5},{5,4},{6,7},{7,6},{8,9},{9,8},{10,11... | collective-permute-start | bytes 884744 | tf_op jit(solution)/shard_map/ppermute | solution.py:31
  35.4 7.4 %collective-permute-start.3 = (bf16[144,1024]{1,0:T(8,128)(2,1)S(1)}, bf16[144,1024]{1,0:T(8,128)(2,1)S(1)}, u32[]{:S(2)}, u32[]{:S(2)}) collective-permute-start(bf16[144,1024]{1,0:T(8,128)(2,1)S(1)} %collective-permute-done.2.g2), channel_id=1, source_target_pairs={{0,1},{1,0},{2,3},{3,2},{4,5},{5,4},{6,7},{7,6},{8,9},{9,8},{10,11... | collective-permute-start | bytes 884744 | tf_op jit(solution)/shard_map/ppermute | solution.py:31
  56.0 3.6 %collective-permute-start.11 = (bf16[288,1024]{1,0:T(8,128)(2,1)S(1)}, bf16[288,1024]{1,0:T(8,128)(2,1)S(1)}, u32[]{:S(2)}, u32[]{:S(2)}) collective-permute-start(bf16[288,1024]{1,0:T(8,128)(2,1)S(1)} %get-tuple-element.39), channel_id=1, source_target_pairs={{0,1},{1,0},{2,3},{3,2},{4,5},{5,4},{6,7},{7,6},{8,9},{9,8},{10,11... | collective-permute-start | bytes 1769480 | tf_op jit(solution)/shard_map/ppermute | solution.py:31
  56.4 27.9 %collective-permute-start.14 = (bf16[272,1024]{1,0:T(8,128)(2,1)S(1)}, bf16[272,1024]{1,0:T(8,128)(2,1)S(1)}, u32[]{:S(2)}, u32[]{:S(2)}) collective-permute-start(bf16[272,1024]{1,0:T(8,128)(2,1)S(1)} %get-tuple-element.42), channel_id=1, source_target_pairs={{0,32},{4,36},{8,40},{12,44},{16,48},{20,52},{24,56},{28,60},{32,6... | collective-permute-start | bytes 1671176 | tf_op jit(solution)/shard_map/ppermute | solution.py:31
  56.4 27.9 %collective-permute-start.15 = (bf16[272,1024]{1,0:T(8,128)(2,1)S(1)}, bf16[272,1024]{1,0:T(8,128)(2,1)S(1)}, u32[]{:S(2)}, u32[]{:S(2)}) collective-permute-start(bf16[272,1024]{1,0:T(8,128)(2,1)S(1)} %get-tuple-element.43), channel_id=1, source_target_pairs={{0,64},{4,68},{8,72},{12,76},{16,80},{20,84},{24,88},{28,92},{32,9... | collective-permute-start | bytes 1671176 | tf_op jit(solution)/shard_map/ppermute | solution.py:31
  58.6 26.4 %collective-permute-start.16 = (bf16[272,1024]{1,0:T(8,128)(2,1)S(1)}, bf16[272,1024]{1,0:T(8,128)(2,1)S(1)}, u32[]{:S(2)}, u32[]{:S(2)}) collective-permute-start(bf16[272,1024]{1,0:T(8,128)(2,1)S(1)} %get-tuple-element.44), channel_id=1, source_target_pairs={{0,96},{4,100},{8,104},{12,108},{16,112},{20,116},{24,120},{28,124... | collective-permute-start | bytes 1671176 | tf_op jit(solution)/shard_map/ppermute | solution.py:31
  59.8 29.0 %collective-permute-start.12 = (bf16[144,1024]{1,0:T(8,128)(2,1)S(1)}, bf16[144,1024]{1,0:T(8,128)(2,1)S(1)}, u32[]{:S(2)}, u32[]{:S(2)}) collective-permute-start(bf16[144,1024]{1,0:T(8,128)(2,1)S(1)} %add_convert_fusion), channel_id=1, source_target_pairs={{0,2},{1,3},{2,0},{3,1},{4,6},{5,7},{6,4},{7,5},{8,10},{9,11},{10,... | collective-permute-start | bytes 884744 | tf_op jit(solution)/shard_map/ppermute | solution.py:31
  85.2 7.1 %collective-permute-start.17 = (bf16[80,1024]{1,0:T(8,128)(2,1)S(1)}, bf16[80,1024]{1,0:T(8,128)(2,1)S(1)}, u32[]{:S(2)}, u32[]{:S(2)}) collective-permute-start(bf16[80,1024]{1,0:T(8,128)(2,1)S(1)} %get-tuple-element.46), channel_id=1, source_target_pairs={{0,4},{4,0},{8,12},{12,8},{16,20},{20,16},{24,28},{28,24},{32,36},... | collective-permute-start | bytes 491528 | tf_op jit(solution)/shard_map/ppermute | solution.py:31
  85.3 8.1 %collective-permute-start.18 = (bf16[80,1024]{1,0:T(8,128)(2,1)S(1)}, bf16[80,1024]{1,0:T(8,128)(2,1)S(1)}, u32[]{:S(2)}, u32[]{:S(2)}) collective-permute-start(bf16[80,1024]{1,0:T(8,128)(2,1)S(1)} %get-tuple-element.47), channel_id=1, source_target_pairs={{0,128},{4,132},{8,136},{12,140},{16,144},{20,148},{24,152},{28,15... | collective-permute-start | bytes 491528 | tf_op jit(solution)/shard_map/ppermute | solution.py:31
  87.1 7.9 %collective-permute-start.19 = (bf16[80,1024]{1,0:T(8,128)(2,1)S(1)}, bf16[80,1024]{1,0:T(8,128)(2,1)S(1)}, u32[]{:S(2)}, u32[]{:S(2)}) collective-permute-start(bf16[80,1024]{1,0:T(8,128)(2,1)S(1)} %get-tuple-element.48), channel_id=1, source_target_pairs={{0,132},{4,128},{8,140},{12,136},{16,148},{20,144},{24,156},{28,15... | collective-permute-start | bytes 491528 | tf_op jit(solution)/shard_map/ppermute | solution.py:31
  89.0 19.8 %collective-permute-start.13 = (bf16[72,1024]{1,0:T(8,128)(2,1)S(1)}, bf16[72,1024]{1,0:T(8,128)(2,1)S(1)}, u32[]{:S(2)}, u32[]{:S(2)}) collective-permute-start(bf16[72,1024]{1,0:T(8,128)(2,1)S(1)} %slice.60), channel_id=1, source_target_pairs={{0,4},{4,8},{8,12},{12,16},{16,20},{20,24},{24,28},{28,32},{32,36}... | collective-permute-start | bytes 442376 | tf_op jit(solution)/shard_map/ppermute | solution.py:31
  95.1 10.3 %collective-permute-start.20 = (bf16[32,1024]{1,0:T(8,128)(2,1)S(1)}, bf16[32,1024]{1,0:T(8,128)(2,1)S(1)}, u32[]{:S(2)}, u32[]{:S(2)}) collective-permute-start(bf16[32,1024]{1,0:T(8,128)(2,1)S(1)} %get-tuple-element.50), channel_id=1, source_target_pairs={{0,8},{4,12},{8,16},{12,20},{16,24},{20,28},{24,0},{28,4},{32,40},... | collective-permute-start | bytes 196616 | tf_op jit(solution)/shard_map/ppermute | solution.py:31
  95.9 10.6 %collective-permute-start.21 = (bf16[32,1024]{1,0:T(8,128)(2,1)S(1)}, bf16[32,1024]{1,0:T(8,128)(2,1)S(1)}, u32[]{:S(2)}, u32[]{:S(2)}) collective-permute-start(bf16[32,1024]{1,0:T(8,128)(2,1)S(1)} %get-tuple-element.51), channel_id=1, source_target_pairs={{0,16},{4,20},{8,24},{12,28},{16,0},{20,4},{24,8},{28,12},{32,48},... | collective-permute-start | bytes 196616 | tf_op jit(solution)/shard_map/ppermute | solution.py:31
  103.0 5.2 %collective-permute-start.22 = (bf16[32,1024]{1,0:T(8,128)(2,1)S(1)}, bf16[32,1024]{1,0:T(8,128)(2,1)S(1)}, u32[]{:S(2)}, u32[]{:S(2)}) collective-permute-start(bf16[32,1024]{1,0:T(8,128)(2,1)S(1)} %get-tuple-element.52), channel_id=1, source_target_pairs={{0,24},{4,28},{8,0},{12,4},{16,8},{20,12},{24,16},{28,20},{32,56},... | collective-permute-start | bytes 196616 | tf_op jit(solution)/shard_map/ppermute | solution.py:31
  (5 other events, 112.8 us)
where the time goes:
time: 111 us; the launch traced here: 110 us
  waiting for transfers between devices  48.5 us (44%)
  starting transfers between devices  34.8 us (31%)
  Pallas kernels  21.3 us (19%)
  local copies, waits for them, and re-layouts  4.06 us (4%)
    ppermute x23, waiting for transfers between devices, sent(): return lax.ppermute(x, axis, [(i, to(i)) for i in range(size)])  48.5 us
    ppermute x23, starting transfers between devices, sent(): return lax.ppermute(x, axis, [(i, to(i)) for i in range(size)])  34.8 us
    pallas_call x1, Pallas kernels, shards(): call(backward_kernel, (shape((ALL, 3 * WIDTH), BF16),) + (shape((272, D),...  12.1 us
    pallas_call x1, Pallas kernels, shards(): call(forward_kernel, (shape((ALL, D), BF16), shape((3, 4, WT, WIDTH), BF1...  4.43 us
    pallas_call x1, Pallas kernels, shards(): call(bias_kernel, (shape((HEADS, WT, WT), F32), shape((WT, 128), jnp.int3...  2.56 us
    slice x5, local copies, waits for them, and re-layouts, halves(): return (x[0], x[1])  2.35 us
  transfers between devices with their start and end apart: 23, of which 11 were waited for; matrix products, arithmetic and copies ran while one was open for 1% of the time, Pallas kernels for 7%

commit v1 on v0

v1 whole, which is shorter than its diff:
```python
import functools

import jax
import jax.numpy as jnp
import numpy as np
from jax import lax
from jax.experimental import pallas as pl
from jax.experimental.pallas import tpu as pltpu
from jax.sharding import PartitionSpec as P

D = 1024
HD = 64
HEADS = 4
WIDTH = 256
WT = 144
NB = 759
ROWS = 80
BLOCKS = 8
ALL = BLOCKS * ROWS
HALF = 320
NY = 4
NZ = 8
F32 = jnp.float32
BF16 = jnp.bfloat16
NT = (((1,), (1,)), ((), ()))
TN = (((0,), (0,)), ((), ()))


def sent(x, axis, to):
    size = lax.axis_size(axis)
    return lax.ppermute(x, axis, [(i, to(i)) for i in range(size)])


def lat_of(x, y, z):
    return (x * NY + y % NY) * NZ + z % NZ


def moved(dx, dy, dz):
    def to(i):
        x, y, z = i // (NY * NZ), i // NZ % NY, i % NZ
        return lat_of(x ^ dx, y + dy, z + dz)

    return to


def paired(dx, dz):
    def to(i):
        x, y, z = i // (NY * NZ), i // NZ % NY, i % NZ
        return lat_of(x ^ dx, y, z ^ dz)

    return to


def call(kernel, out, args, flops, moved_bytes, vmem=16):
    return pl.pallas_call(
        kernel,
        out_shape=out,
        scratch_shapes=args,
        compiler_params=pltpu.CompilerParams(vmem_limit_bytes=vmem * 2**20),
        cost_estimate=pl.CostEstimate(flops=flops, bytes_accessed=moved_bytes, transcendentals=0),
    )


def shape(dims, dtype):
    return jax.ShapeDtypeStruct(dims, dtype)


def window_order():
    order = np.zeros((WT, WT), np.float32)
    for row in range(6):
        for half in range(2):
            for lon in range(6):
                for lev in range(2):
                    n = row * 24 + half * 12 + lon * 2 + lev
                    order[n, row * 24 + (1 - lev) * 12 + (1 - half) * 6 + lon] = 1
    return order


def turned(x, fill):
    x = jnp.concatenate([x[:, 128:], jnp.full((WT, 112), fill, F32)], axis=1)
    x = jnp.concatenate([x, jnp.full((112, 128), fill, F32)], axis=0)
    return jnp.transpose(x)[:16]


def bias_kernel(table, index, order, bias, places, places_end):
    idx = index[...].astype(F32)
    high = jnp.floor(idx * (1.0 / 32.0))
    low = idx - high * 32.0
    perm = order[...]

    def reordered(x):
        y = jnp.dot(perm, x.astype(BF16), preferred_element_type=F32).astype(BF16)
        return lax.dot_general(y, perm, NT, preferred_element_type=F32)

    own_f = reordered(high) * 32.0 + reordered(low)
    own = own_f.astype(jnp.int32)
    places[...] = own[:, :128]
    places_end[...] = turned(own_f, -1.0).astype(jnp.int32)
    for start, stop in ((0, 128), (128, WT)):
        part = own[:, start:stop]
        if stop - start < 128:
            part = jnp.concatenate([part, jnp.zeros((WT, 128 - stop + start), jnp.int32)], axis=1)
        chunk = lax.shift_right_logical(part, 7)
        lane = lax.bitwise_and(part, 127)
        for head in range(HEADS):
            found = jnp.zeros((WT, 128), F32)
            for c in range(6):
                row = jnp.broadcast_to(table[head : head + 1, c * 128 : (c + 1) * 128], (WT, 128))
                got = jnp.take_along_axis(row, lane, axis=1, mode="promise_in_bounds")
                found = jnp.where(chunk == c, got, found)
            bias[head, :, start:stop] = found[:, : stop - start]


def eastern(width):
    row = lax.broadcasted_iota(jnp.int32, (72, width), 0)
    return lax.rem(row, 24) < 12


def to_windows(rows, wins, own):
    first = eastern(rows.shape[1])
    for w in range(4):
        near = lax.bitwise_xor(own, w) * ROWS
        east = lax.bitwise_xor(own, (w + 1) % 4) * ROWS
        for r in range(2):
            a = rows[pl.ds(pl.multiple_of(near + r * HALF, 8), 72), :]
            b = rows[pl.ds(pl.multiple_of(east + r * HALF, 8), 72), :]
            wins[w, r * 72 : (r + 1) * 72, :] = jnp.where(first, b, a)


def from_windows(wins, rows, own):
    first = eastern(rows.shape[1])
    for s in range(4):
        start = lax.bitwise_xor(own, s) * ROWS
        for r in range(2):
            a = wins[s, r * 72 : (r + 1) * 72, :]
            b = wins[(s + 3) % 4, r * 72 : (r + 1) * 72, :]
            at = pl.multiple_of(start + r * HALF, 8)
            rows[pl.ds(at, 72), :] = jnp.where(first, b, a)
            rows[pl.ds(pl.multiple_of(at + 72, 8), 8), :] = jnp.zeros((8, rows.shape[1]), F32)


def head_mask(head, rows):
    lane = lax.broadcasted_iota(jnp.int32, (rows, WIDTH), 1)
    return lax.shift_right_logical(lane, 6) == head


def only(head, x):
    return jnp.where(head_mask(head, x.shape[0]), x, 0.0).astype(BF16)


def stacked(pieces, tall, gall):
    for p, piece in enumerate(pieces):
        tall[p * ROWS : (p + 1) * ROWS, :] = piece[:ROWS, :]
        gall[p * ROWS : (p + 1) * ROWS, :] = piece[ROWS:, :]


def projected(m, tall, gall, weight, wo):
    if m < 3:
        y = jnp.dot(tall[...], weight[m], preferred_element_type=F32)
    else:
        y = lax.dot_general(gall[...], wo[...], NT, preferred_element_type=F32)
    return y.astype(BF16)


def early_kernel(m0, m1, m2, m3, weight, wo, proj, tall, gall):
    stacked((m0, m1, m2, m3), tall, gall)
    for m in range(4):
        proj[m] = projected(m, tall, gall, weight, wo)


def segment_sums(sums, ends, places, places_end):
    low_row = lax.broadcasted_iota(jnp.int32, (128, 256), 0)

    def terms(idx, values):
        high = jnp.right_shift(idx, 7)
        low = lax.bitwise_and(idx, 127)
        a = jnp.concatenate([jnp.where(high == c, values, 0.0) for c in range(6)], axis=0)
        return a.astype(BF16), (low_row == low).astype(F32).astype(BF16)

    def added(acc, pairs):
        a = jnp.concatenate([p[0] for p in pairs], axis=1)
        b = jnp.concatenate([p[1] for p in pairs], axis=1)
        return acc + lax.dot_general(a, b, NT, preferred_element_type=F32)

    def split(block):
        top = block.astype(BF16).astype(F32)
        return top, block - top

    def rows_of(blocks, i):
        return jnp.concatenate([b[0][i : i + 1] for b in blocks] + [b[1][i : i + 1] for b in blocks], axis=0)

    def step(i, acc):
        at = pl.ds(pl.multiple_of(i * 8, 8), 8)
        idx = places[at, :]
        blocks = [split(sums[head, at, :128]) for head in range(HEADS)]
        pairs = []
        for j in range(0, 8, 2):
            both = jnp.concatenate([idx[j : j + 1], idx[j + 1 : j + 2]], axis=1)
            pairs.append(terms(both, jnp.concatenate([rows_of(blocks, j), rows_of(blocks, j + 1)], axis=1)))
        return added(acc, pairs)

    acc = lax.fori_loop(0, 18, step, jnp.zeros((48, 128), F32))

    def last(i, acc):
        at = pl.ds(pl.multiple_of(i * 8, 8), 8)
        idx = places_end[at, :]
        blocks = [split(ends[head, at, :]) for head in range(HEADS)]
        for j in range(0, 8, 4):
            acc = added(acc, [terms(idx[n : n + 1], rows_of(blocks, n)) for n in range(j, j + 4)])
        return acc

    acc = lax.fori_loop(0, 2, last, acc)
    return jnp.concatenate([acc[c * 8 : (c + 1) * 8] for c in range(6)], axis=1)


def bias_rows(x):
    top = x.astype(BF16).astype(F32)
    return jnp.concatenate([top, x - top], axis=0).astype(BF16)


def band_kernel(*refs):
    highs, lows = refs[:4], refs[4:8]
    weight, wo, bias, early, places, places_end, grads = refs[8:15]
    ways, pairs = refs[15:19], refs[19:23]
    tall, gall, qkv, rows, wins, outs, sums, ends, att, labels, full = refs[23:]
    own = lax.axis_index("head")
    labels[...] = jnp.zeros_like(labels)
    row = lax.broadcasted_iota(jnp.int32, (8, WIDTH), 0)
    for p in range(4):
        shard = lax.bitwise_xor(own, p)
        before = lax.rem(shard + 3, 4)
        marks = highs[p][64:80, :WIDTH].astype(F32)[8:16] + lows[p][64:80, :WIDTH].astype(F32)[8:16]
        labels[shard] += jnp.where(row < 4, marks, 0.0)
        labels[before] += jnp.where(row < 4, pltpu.roll(marks, 4, 0), 0.0)
    stacked(highs, tall.at[:HALF, :], gall.at[:HALF, :])
    stacked(lows, tall.at[HALF:, :], gall.at[HALF:, :])
    for m in range(4):
        rows[:HALF, :] = early[m].astype(F32)
        rows[HALF:, :] = projected(m, tall.at[HALF:, :], gall.at[HALF:, :], weight, wo).astype(F32)
        to_windows(rows, wins, own)
        if m < 3:
            qkv[m] = wins[...].astype(BF16)
    sums[...] = jnp.zeros_like(sums)

    def window(w, _):
        marks = labels[w].astype(BF16)
        same = lax.dot_general(marks, marks, TN, preferred_element_type=F32)[:WT, :WT] > 0.5
        q = qkv[0, w].astype(F32)
        k = qkv[1, w]
        v = qkv[2, w]
        d = wins[w]
        k_f = k.astype(F32)
        v_f = v.astype(F32)
        total = jnp.zeros((WT, WIDTH), F32)
        dq = jnp.zeros((WT, WIDTH), F32)
        dk = jnp.zeros((WT, WIDTH), F32)
        dv = jnp.zeros((WT, WIDTH), F32)
        for head in range(HEADS):
            qh = only(head, q)
            dh = only(head, d)
            s = lax.dot_general(qh, k, NT, preferred_element_type=F32)
            dp = lax.dot_general(dh, v, NT, preferred_element_type=F32)
            s = s * 0.125 + bias[head]
            s = jnp.where(same, s, -jnp.inf)
            e = jnp.exp(s - jnp.max(s, axis=1, keepdims=True))
            pr = e / jnp.sum(e, axis=1, keepdims=True)
            prb = pr.astype(BF16)
            total += jnp.dot(prb, only(head, v_f), preferred_element_type=F32)
            dv += lax.dot_general(prb, dh, TN, preferred_element_type=F32)
            ds = pr * (dp - jnp.sum(pr * dp, axis=1, keepdims=True))
            sums[head] += ds
            dsb = ds.astype(BF16)
            dq += jnp.dot(dsb, only(head, k_f), preferred_element_type=F32)
            dk += lax.dot_general(dsb, qh, TN, preferred_element_type=F32)
        outs[0, w] = dq * 0.125
        outs[1, w] = dk * 0.125
        outs[2, w] = dv
        outs[3, w] = total
        return 0

    lax.fori_loop(0, 4, window, 0)
    for m in range(4):
        from_windows(outs.at[m], rows, own)
        if m < 3:
            grads[:, m * WIDTH : (m + 1) * WIDTH] = rows[...].astype(BF16)
    att[...] = rows[...].astype(BF16)

    for head in range(HEADS):
        ends[head] = turned(sums[head], 0.0)
    found = segment_sums(sums, ends, places, places_end)
    found = found + pltpu.roll(found, 4, 0)
    rest = jnp.concatenate([found[:, 512:], jnp.zeros((8, 256), F32)], axis=1)
    found = bias_rows(jnp.where(lax.broadcasted_iota(jnp.int32, (8, 512), 0) < 4, found[:, :512], rest))

    full[:, : 3 * WIDTH] = lax.dot_general(tall[...], grads[...], TN, preferred_element_type=F32).astype(BF16)
    full[:, 3 * WIDTH :] = lax.dot_general(gall[...], att[...], TN, preferred_element_type=F32).astype(BF16)
    lat = lax.axis_index("lat")
    x, y, z = lat // (NY * NZ), lax.rem(lat // NZ, NY), lax.rem(lat, 2)
    for d, out in enumerate(ways):
        out[256:272, :] = found
        for half in range(2):
            at = pl.ds(pl.multiple_of(half * 512 + lax.rem(y + d, NY) * 128, 128), 128)
            out[half * 128 : (half + 1) * 128, :] = full[at, :512]
    for i, out in enumerate(pairs):
        start = lax.bitwise_xor(x, i // 2) * 512 + lax.bitwise_xor(z, i % 2) * 16
        for b in range(16):
            at = pl.ds(pl.multiple_of(start + (b // 4) * 128 + (b % 4) * 32, 16), 16)
            out[b * 16 : (b + 1) * 16, :] = full[at, 512:]


def input_kernel(grads, weight, near, far, given):
    total = jnp.zeros((ALL, D), F32)
    for m in range(3):
        total += lax.dot_general(
            grads[:, m * WIDTH : (m + 1) * WIDTH], weight[m], NT, preferred_element_type=F32
        )
    for p, out in enumerate((near.at[...], given.at[:WT, :], far.at[...], given.at[WT:, :])):
        start = p * ROWS
        both = jnp.concatenate([total[start : start + 72], total[start + HALF : start + HALF + 72]], axis=0)
        out[...] = both.astype(BF16)


def stage_rows(parts, rows):
    total = parts[0][rows, :].astype(F32)
    for part in parts[1:]:
        total += part[rows, :].astype(F32)
    return total


def second_kernel(*refs):
    ways, pairs, to_pairs, to_ways = refs[:4], refs[4:8], refs[8:12], refs[12:]
    lat = lax.axis_index("lat")
    x, y, z = lat // (NY * NZ), lax.rem(lat // NZ, NY), lax.rem(lat, 2)
    found = stage_rows(ways, pl.ds(256, 16))
    found = bias_rows(found[:8] + found[8:])
    for i, out in enumerate(to_pairs):
        start = lax.bitwise_xor(x, i // 2) * 128 + lax.bitwise_xor(z, i % 2) * 16
        for k in range(4):
            rows = pl.ds(pl.multiple_of(start + k * 32, 16), 16)
            out[k * 16 : (k + 1) * 16, :] = stage_rows(ways, rows).astype(BF16)
        out[64:80, :] = found
    for d, out in enumerate(to_ways):
        rows = pl.ds(pl.multiple_of(lax.rem(y + d, NY) * 64, 64), 64)
        out[...] = stage_rows(pairs, rows).astype(BF16)


def third_kernel(*refs):
    pairs, ways, outs = refs[:4], refs[4:8], refs[8:]
    z = lax.rem(lax.axis_index("lat"), NZ) // 2
    found = stage_rows(pairs, pl.ds(64, 16))
    found = bias_rows(found[:8] + found[8:])
    for e, out in enumerate(outs):
        rows = pl.ds(pl.multiple_of(lax.rem(z + e, 4) * 16, 16), 16)
        out[:16, :512] = stage_rows(pairs, rows).astype(BF16)
        out[:16, 512:] = stage_rows(ways, rows).astype(BF16)
        out[16:, :512] = found
        out[16:, 512:] = jnp.zeros_like(found)


def last_kernel(a, b, c, d, qkv, out, bias):
    parts = (a, b, c, d)
    total = stage_rows(parts, pl.ds(0, 16))
    for m in range(3):
        qkv[m] = total[:, m * WIDTH : (m + 1) * WIDTH]
    out[...] = total[:, 3 * WIDTH :]
    found = stage_rows(parts, pl.ds(16, 16))
    found = found[:8, :512] + found[8:, :512]
    bias[...] = jnp.concatenate([found[:4], found[4:]], axis=1)[:, :NB]


def label_rows(labels, first):
    row = lax.broadcasted_iota(jnp.int32, (8, 72), 0)
    col = lax.broadcasted_iota(jnp.int32, (8, 72), 1)
    labels = labels.transpose(0, 2, 1).reshape(1, 72)
    hit = (row % 4 == labels) & ((row >= 4) == (col % 24 < 12))
    return jnp.pad(hit.astype(BF16), ((0, 0), (first, D - 72 - first)))


def shards(tokens, output_grad, region_labels, qkv_weight, out_weight, bias_table, bias_index):
    core = functools.partial(sent, axis="head", to=lambda i: i ^ 1)
    across = functools.partial(sent, axis="head", to=lambda i: i ^ 2)
    back = functools.partial(sent, axis="lat", to=lambda i: (i - 1) % 64)
    onward = functools.partial(sent, axis="lat", to=lambda i: (i + 1) % 64)

    def message(r):
        rows = slice(3 - 3 * r, 6 - 3 * r)
        t, g = (x[rows].transpose(0, 2, 1, 3).reshape(72, D) for x in (tokens, output_grad))
        marks = label_rows(region_labels[rows], 72 * r)
        return jnp.concatenate([t, marks, g, jnp.zeros((8, D), BF16)])

    high = message(0)
    low = back(message(1))
    far_high = across(high)
    highs = (high, core(high), far_high, core(far_high))

    table = jnp.pad(bias_table.T, ((0, 0), (0, 9)))
    bias, places, places_end = call(
        bias_kernel,
        (shape((HEADS, WT, WT), F32), shape((WT, 128), jnp.int32), shape((16, 256), jnp.int32)),
        (),
        2 * 10**7,
        10**6,
    )(table, bias_index, jnp.asarray(window_order(), BF16))

    low, bias, places, places_end = lax.optimization_barrier((low, bias, places, places_end))
    far_low = across(low)
    early = call(
        early_kernel,
        shape((4, HALF, WIDTH), BF16),
        [pltpu.VMEM((HALF, D), BF16), pltpu.VMEM((HALF, D), BF16)],
        10**9,
        5 * 10**6,
        8,
    )(*highs, qkv_weight, out_weight)
    far_low, early = lax.optimization_barrier((far_low, early))
    lows = (low, core(low), far_low, core(far_low))

    grads, *blocks = call(
        band_kernel,
        (shape((ALL, 3 * WIDTH), BF16),) + (shape((272, 512), BF16),) * 4 + (shape((256, 512), BF16),) * 4,
        [
            pltpu.VMEM((ALL, D), BF16),
            pltpu.VMEM((ALL, D), BF16),
            pltpu.VMEM((3, 4, WT, WIDTH), BF16),
            pltpu.VMEM((ALL, WIDTH), F32),
            pltpu.VMEM((4, WT, WIDTH), F32),
            pltpu.VMEM((4, 4, WT, WIDTH), F32),
            pltpu.VMEM((HEADS, WT, WT), F32),
            pltpu.VMEM((HEADS, 16, 256), F32),
            pltpu.VMEM((ALL, WIDTH), BF16),
            pltpu.VMEM((4, 8, WIDTH), F32),
            pltpu.VMEM((D, D), BF16),
        ],
        3 * 10**9,
        10**7,
        24,
    )(*highs, *lows, qkv_weight, out_weight, bias, early, places, places_end)

    def by_y(parts):
        return [parts[0]] + [sent(parts[d], "lat", moved(0, d, 0)) for d in range(1, 4)]

    def by_pair(parts):
        return [parts[0]] + [sent(parts[d], "lat", paired(d // 2, d % 2)) for d in range(1, 4)]

    ways, pairs = by_y(blocks[:4]), by_pair(blocks[4:])

    near, far, given = call(
        input_kernel, (shape((WT, D), BF16), shape((WT, D), BF16), shape((2 * WT, D), BF16)), (), 10**9, 5 * 10**6
    )(grads, qkv_weight)
    given = core(given)
    far = (far.astype(F32) + given[WT:].astype(F32)).astype(BF16)
    parts = call(
        second_kernel, (shape((80, 512), BF16),) * 4 + (shape((64, 512), BF16),) * 4, (), 10**6, 3 * 10**6, 8
    )(*ways, *pairs)
    far, parts = lax.optimization_barrier((far, parts))
    more = across(far)
    pairs, ways = by_pair(parts[:4]), by_y(parts[4:])
    pairs, ways, more = lax.optimization_barrier((pairs, ways, more))
    parts = call(third_kernel, (shape((32, D), BF16),) * 4, (), 10**6, 10**6, 8)(*pairs, *ways)
    got = [parts[0]] + [sent(parts[e], "lat", moved(0, 0, 2 * e)) for e in range(1, 4)]
    near = near.astype(F32) + given[:WT].astype(F32) + more.astype(F32)
    low = onward(near[72:].astype(BF16)).astype(F32)
    input_grad = jnp.concatenate([low, near[:72]]).reshape(6, 12, 2, D).transpose(0, 2, 1, 3)
    got, input_grad = lax.optimization_barrier((got, input_grad))
    qkv_grad, out_grad, bias_grad = call(
        last_kernel,
        (shape((3, 16, WIDTH), F32), shape((16, WIDTH), F32), shape((HEADS, NB), F32)),
        (),
        10**6,
        10**6,
        8,
    )(*got)
    return input_grad, qkv_grad, out_grad.T, bias_grad.T


def solution(mesh):
    return jax.shard_map(
        shards,
        mesh=mesh,
        in_specs=(
            P("lat", None, "head", None),
            P("lat", None, "head", None),
            P("lat", None, "head"),
            P(None, None, "head"),
            P("head", None),
            P(None, "head"),
            P(),
        ),
        out_specs=(
            P("lat", None, "head", None),
            P(None, "lat", "head"),
            P("head", "lat"),
            P(None, "head"),
        ),
        check_vma=False,
    )
```

time: 111 us -> 106 us (0.955)
  waiting for transfers between devices: 48.5 us -> 33.3 us
  starting transfers between devices: 34.8 us -> 44.4 us
  local copies, waits for them, and re-layouts: 4.06 us -> 5.2 us
    ppermute x23 -> x25, waiting for transfers between devices: 48.5 us -> 33.3 us  [sent(): return lax.ppermute(x, axis, [(i, to(i)) for i in range(size)])]
    ppermute x23 -> x25, starting transfers between devices: 34.8 us -> 44.4 us  [sent(): return lax.ppermute(x, axis, [(i, to(i)) for i in range(size)])]
    transpose x0 -> x5, local copies, waits for them, and re-layouts: none -> 3.43 us  [the longest x2 2.51 us: message(): x[rows].transpose(0, 2, 1, 3).reshape(72, D)]
    slice x5 -> x0, local copies, waits for them, and re-layouts: 2.35 us -> none  [halves(): return (x[0], x[1])]
  transfers between devices with their start and end apart: 23 -> 25, of which waited for: 11 -> 9; matrix products, arithmetic and copies ran while one was open for 1% -> 1% of each run, Pallas kernels for 7% -> 4%
where the time goes in v1:
time: 106 us
  starting transfers between devices  44.4 us (42%)
  waiting for transfers between devices  33.3 us (31%)
  Pallas kernels  21.7 us (20%)
  local copies, waits for them, and re-layouts  5.2 us (5%)
    ppermute x25, starting transfers between devices, sent(): return lax.ppermute(x, axis, [(i, to(i)) for i in range(size)])  44.4 us
    ppermute x25, waiting for transfers between devices, sent(): return lax.ppermute(x, axis, [(i, to(i)) for i in range(size)])  33.3 us
    pallas_call x1, Pallas kernels, shards(): call(band_kernel, (shape((ALL, 3 * WIDTH), BF16),) + (shape((272, 512), B...  16 us
    pallas_call x1, Pallas kernels, shards(): call(bias_kernel, (shape((HEADS, WT, WT), F32), shape((WT, 128), jnp.int3...  2.56 us
    transpose x2, local copies, waits for them, and re-layouts, message(): x[rows].transpose(0, 2, 1, 3).reshape(72, D)  2.51 us
  transfers between devices with their start and end apart: 25, of which 9 were waited for; matrix products, arithmetic and copies ran while one was open for 1% of the time, Pallas kernels for 4%

profile of v1, /device:TPU:2, one launch (start us, length us, event | category | flops | bytes accessed | tf_op | source)
XLA Modules:
  0.0 106.1 jit_solution(212513067971411445)
XLA Ops:
  1.9 1.2 %slice_bitcast_fusion.1 = (bf16[3,12,2,1024]{3,2,1,0:T(2,128)(2,1)S(1)}, bf16[3,12,2,1024]{3,2,1,0:T(2,128)(2,1)S(1)}) fusion(bf16[6,2,12,1024]{3,1,2,0:T(2,128)(2,1)} %param.8), kind=kLoop, calls=%fused_computation.7 | loop fusion | bytes 589824 | tf_op jit(solution)/shard_map/transpose | solution.py:387
  3.2 1.3 %slice_bitcast_fusion = (bf16[3,12,2,1024]{3,2,1,0:T(2,128)(2,1)S(1)}, bf16[3,12,2,1024]{3,2,1,0:T(2,128)(2,1)S(1)}) fusion(bf16[6,2,12,1024]{3,1,2,0:T(2,128)(2,1)} %param.9), kind=kLoop, calls=%fused_computation.6 | loop fusion | bytes 589824 | tf_op jit(solution)/shard_map/transpose | solution.py:387
  5.1 2.2 %collective-permute-start.1 = (bf16[160,1024]{1,0:T(8,128)(2,1)S(1)}, bf16[160,1024]{1,0:T(8,128)(2,1)S(1)}, u32[]{:S(2)}, u32[]{:S(2)}) collective-permute-start(bf16[160,1024]{1,0:T(8,128)(2,1)S(1)} %get-tuple-element.131.m0.refs_0_), channel_id=1, source_target_pairs={{0,2},{1,3},{2,0},{3,1},{4,6},{5,7},{6,4},{7,5},{8,10},{9,11},{10,... | collective-permute-start | bytes 983048 | tf_op jit(solution)/shard_map/ppermute | solution.py:31
  7.3 9.2 %collective-permute-start.3 = (bf16[160,1024]{1,0:T(8,128)(2,1)S(1)}, bf16[160,1024]{1,0:T(8,128)(2,1)S(1)}, u32[]{:S(2)}, u32[]{:S(2)}) collective-permute-start(bf16[160,1024]{1,0:T(8,128)(2,1)S(1)} %get-tuple-element.130), channel_id=1, source_target_pairs={{0,252},{4,0},{8,4},{12,8},{16,12},{20,16},{24,20},{28,24},{32,28}... | collective-permute-start | bytes 983048 | tf_op jit(solution)/shard_map/ppermute | solution.py:31
  17.1 2.6 %shard_map.111 = (f32[4,144,144]{2,1,0:T(8,128)S(1)}, s32[144,128]{1,0:T(8,128)S(1)}, s32[16,256]{1,0:T(8,128)S(1)}) custom-call(f32[4,768]{1,0:T(4,128)S(1)} %pad.22.table, s32[144,144]{1,0:T(8,128)S(1)} %copy-done.2, bf16[144,144]{1,0:T(8,128)(2,1)S(1)} %copy-done.3), custom_call_target="tpu_custom_call" | custom-call | flops 20000000 | bytes 1000000 | tf_op jit(solution)/shard_map/pallas_call | solution.py:397
  19.6 3.6 %collective-permute-done.3.refs_4_ = bf16[160,1024]{1,0:T(8,128)(2,1)S(1)} collective-permute-done((bf16[160,1024]{1,0:T(8,128)(2,1)S(1)}, bf16[160,1024]{1,0:T(8,128)(2,1)S(1)}, u32[]{:S(2)}, u32[]{:S(2)}) %collective-permute-start.3) | collective-permute-done | bytes 327712 | tf_op jit(solution)/shard_map/ppermute | solution.py:31
  24.2 8.9 %collective-permute-done.5.refs_6_ = bf16[160,1024]{1,0:T(8,128)(2,1)S(1)} collective-permute-done((bf16[160,1024]{1,0:T(8,128)(2,1)S(1)}, bf16[160,1024]{1,0:T(8,128)(2,1)S(1)}, u32[]{:S(2)}, u32[]{:S(2)}) %collective-permute-start.5) | collective-permute-done | bytes 327712 | tf_op jit(solution)/shard_map/ppermute | solution.py:31
  33.0 1.6 %collective-permute-done.6.refs_7_ = bf16[160,1024]{1,0:T(8,128)(2,1)S(1)} collective-permute-done((bf16[160,1024]{1,0:T(8,128)(2,1)S(1)}, bf16[160,1024]{1,0:T(8,128)(2,1)S(1)}, u32[]{:S(2)}, u32[]{:S(2)}) %collective-permute-start.6) | collective-permute-done | bytes 327712 | tf_op jit(solution)/shard_map/ppermute | solution.py:31
  34.6 16.0 %shard_map.113 = (bf16[640,768]{1,0:T(8,128)(2,1)S(1)}, bf16[272,512]{1,0:T(8,128)(2,1)S(1)}, bf16[272,512]{1,0:T(8,128)(2,1)S(1)}, bf16[272,512]{1,0:T(8,128)(2...) custom-call(bf16[160,1024]{1,0:T(8,128)(2,1)S(1)} %get-tuple-element, ...), custom_call_target="tpu_custom_call" | custom-call | flops 3000000000 | bytes 10000000 | tf_op jit(solution)/shard_map/pallas_call | solution.py:418
  50.7 1.2 %shard_map.114 = (bf16[144,1024]{1,0:T(8,128)(2,1)S(1)}, bf16[144,1024]{1,0:T(8,128)(2,1)S(1)}, bf16[288,1024]{1,0:T(8,128)(2,1)S(1)}) custom-call(bf16[640,768]{1,0:T(8,128)(2,1)S(1)} %get-tuple-element.72.grads, bf16[3,1024,256]{2,1,0:T(8,128)(2,1)S(1)} %copy-done), custom_call_target="tpu_custom_call" | custom-call | flops 1000000000 | bytes 5000000 | tf_op jit(solution)/shard_map/pallas_call | solution.py:447
  53.7 2.9 %collective-permute-start.9 = (bf16[272,512]{1,0:T(8,128)(2,1)S(1)}, bf16[272,512]{1,0:T(8,128)(2,1)S(1)}, u32[]{:S(2)}, u32[]{:S(2)}) collective-permute-start(bf16[272,512]{1,0:T(8,128)(2,1)S(1)} %get-tuple-element.77), channel_id=1, source_target_pairs={{0,64},{4,68},{8,72},{12,76},{16,80},{20,84},{24,88},{28,92},{32,9... | collective-permute-start | bytes 835592 | tf_op jit(solution)/shard_map/ppermute | solution.py:31
  56.6 4.1 %collective-permute-done.11.refs_5_ = bf16[256,512]{1,0:T(8,128)(2,1)S(1)} collective-permute-done((bf16[256,512]{1,0:T(8,128)(2,1)S(1)}, bf16[256,512]{1,0:T(8,128)(2,1)S(1)}, u32[]{:S(2)}, u32[]{:S(2)}) %collective-permute-start.11) | collective-permute-done | bytes 262176 | tf_op jit(solution)/shard_map/ppermute | solution.py:31
  61.4 1.7 %collective-permute-start.13 = (bf16[256,512]{1,0:T(8,128)(2,1)S(1)}, bf16[256,512]{1,0:T(8,128)(2,1)S(1)}, u32[]{:S(2)}, u32[]{:S(2)}) collective-permute-start(bf16[256,512]{1,0:T(8,128)(2,1)S(1)} %get-tuple-element.82), channel_id=1, source_target_pairs={{0,132},{4,128},{8,140},{12,136},{16,148},{20,144},{24,156},{28,15... | collective-permute-start | bytes 786440 | tf_op jit(solution)/shard_map/ppermute | solution.py:31
  63.1 6.9 %collective-permute-done.13.refs_7_ = bf16[256,512]{1,0:T(8,128)(2,1)S(1)} collective-permute-done((bf16[256,512]{1,0:T(8,128)(2,1)S(1)}, bf16[256,512]{1,0:T(8,128)(2,1)S(1)}, u32[]{:S(2)}, u32[]{:S(2)}) %collective-permute-start.13) | collective-permute-done | bytes 262176 | tf_op jit(solution)/shard_map/ppermute | solution.py:31
  70.4 2.2 %collective-permute-start.20 = (bf16[144,1024]{1,0:T(8,128)(2,1)S(1)}, bf16[144,1024]{1,0:T(8,128)(2,1)S(1)}, u32[]{:S(2)}, u32[]{:S(2)}) collective-permute-start(bf16[144,1024]{1,0:T(8,128)(2,1)S(1)} %add_convert_fusion), channel_id=1, source_target_pairs={{0,2},{1,3},{2,0},{3,1},{4,6},{5,7},{6,4},{7,5},{8,10},{9,11},{10,... | collective-permute-start | bytes 884744 | tf_op jit(solution)/shard_map/ppermute | solution.py:31
  73.7 2.2 %collective-permute-start.18 = (bf16[64,512]{1,0:T(8,128)(2,1)S(1)}, bf16[64,512]{1,0:T(8,128)(2,1)S(1)}, u32[]{:S(2)}, u32[]{:S(2)}) collective-permute-start(bf16[64,512]{1,0:T(8,128)(2,1)S(1)} %get-tuple-element.97), channel_id=1, source_target_pairs={{0,64},{4,68},{8,72},{12,76},{16,80},{20,84},{24,88},{28,92},{32,9... | collective-permute-start | bytes 196616 | tf_op jit(solution)/shard_map/ppermute | solution.py:31
  75.8 1.6 %collective-permute-start.14 = (bf16[80,512]{1,0:T(8,128)(2,1)S(1)}, bf16[80,512]{1,0:T(8,128)(2,1)S(1)}, u32[]{:S(2)}, u32[]{:S(2)}) collective-permute-start(bf16[80,512]{1,0:T(8,128)(2,1)S(1)} %get-tuple-element.92), channel_id=1, source_target_pairs={{0,4},{4,0},{8,12},{12,8},{16,20},{20,16},{24,28},{28,24},{32,36},... | collective-permute-start | bytes 245768 | tf_op jit(solution)/shard_map/ppermute | solution.py:31
  78.6 2.5 %collective-permute-start.16 = (bf16[80,512]{1,0:T(8,128)(2,1)S(1)}, bf16[80,512]{1,0:T(8,128)(2,1)S(1)}, u32[]{:S(2)}, u32[]{:S(2)}) collective-permute-start(bf16[80,512]{1,0:T(8,128)(2,1)S(1)} %get-tuple-element.94), channel_id=1, source_target_pairs={{0,132},{4,128},{8,140},{12,136},{16,148},{20,144},{24,156},{28,15... | collective-permute-start | bytes 245768 | tf_op jit(solution)/shard_map/ppermute | solution.py:31
  81.6 3.9 %collective-permute-done.19.refs_7_ = bf16[64,512]{1,0:T(8,128)(2,1)S(1)} collective-permute-done((bf16[64,512]{1,0:T(8,128)(2,1)S(1)}, bf16[64,512]{1,0:T(8,128)(2,1)S(1)}, u32[]{:S(2)}, u32[]{:S(2)}) %collective-permute-start.19) | collective-permute-done | bytes 65568 | tf_op jit(solution)/shard_map/ppermute | solution.py:31
  86.1 3.4 %collective-permute-start.21 = (bf16[32,1024]{1,0:T(8,128)(2,1)S(1)}, bf16[32,1024]{1,0:T(8,128)(2,1)S(1)}, u32[]{:S(2)}, u32[]{:S(2)}) collective-permute-start(bf16[32,1024]{1,0:T(8,128)(2,1)S(1)} %get-tuple-element.109), channel_id=1, source_target_pairs={{0,8},{4,12},{8,16},{12,20},{16,24},{20,28},{24,0},{28,4},{32,40},... | collective-permute-start | bytes 196616 | tf_op jit(solution)/shard_map/ppermute | solution.py:31
  89.5 10.6 %collective-permute-start.22 = (bf16[32,1024]{1,0:T(8,128)(2,1)S(1)}, bf16[32,1024]{1,0:T(8,128)(2,1)S(1)}, u32[]{:S(2)}, u32[]{:S(2)}) collective-permute-start(bf16[32,1024]{1,0:T(8,128)(2,1)S(1)} %get-tuple-element.110), channel_id=1, source_target_pairs={{0,16},{4,20},{8,24},{12,28},{16,0},{20,4},{24,8},{28,12},{32,48},... | collective-permute-start | bytes 196616 | tf_op jit(solution)/shard_map/ppermute | solution.py:31
  100.1 2.4 %collective-permute-done.24 = bf16[72,1024]{1,0:T(8,128)(2,1)S(1)} collective-permute-done((bf16[72,1024]{1,0:T(8,128)(2,1)S(1)}, bf16[72,1024]{1,0:T(8,128)(2,1)S(1)}, u32[]{:S(2)}, u32[]{:S(2)}) %collective-permute-start.24) | collective-permute-done | bytes 147488 | tf_op jit(solution)/shard_map/ppermute | solution.py:31
  102.6 1.2 %reshape.31 = f32[6,12,2,1024]{3,2,1,0:T(2,128)} reshape(f32[144,1024]{1,0:T(8,128)S(1)} %pad_maximum_fusion) | data formatting | bytes 1179648 | tf_op jit(solution)/shard_map/reshape | solution.py:463
  103.8 1.7 %collective-permute-done.23.d = bf16[32,1024]{1,0:T(8,128)(2,1)S(1)} collective-permute-done((bf16[32,1024]{1,0:T(8,128)(2,1)S(1)}, bf16[32,1024]{1,0:T(8,128)(2,1)S(1)}, u32[]{:S(2)}, u32[]{:S(2)}) %collective-permute-start.23) | collective-permute-done | bytes 65568 | tf_op jit(solution)/shard_map/ppermute | solution.py:31
  (74 shorter events, 10.0 us)
Async XLA Ops:
  5.1 11.4 %collective-permute-start.1 = (bf16[160,1024]{1,0:T(8,128)(2,1)S(1)}, bf16[160,1024]{1,0:T(8,128)(2,1)S(1)}, u32[]{:S(2)}, u32[]{:S(2)}) collective-permute-start(bf16[160,1024]{1,0:T(8,128)(2,1)S(1)} %get-tuple-element.131.m0.refs_0_), channel_id=1, source_target_pairs={{0,2},{1,3},{2,0},{3,1},{4,6},{5,7},{6,4},{7,5},{8,10},{9,11},{10,... | collective-permute-start | bytes 983048 | tf_op jit(solution)/shard_map/ppermute | solution.py:31
  7.3 15.9 %collective-permute-start.3 = (bf16[160,1024]{1,0:T(8,128)(2,1)S(1)}, bf16[160,1024]{1,0:T(8,128)(2,1)S(1)}, u32[]{:S(2)}, u32[]{:S(2)}) collective-permute-start(bf16[160,1024]{1,0:T(8,128)(2,1)S(1)} %get-tuple-element.130), channel_id=1, source_target_pairs={{0,252},{4,0},{8,4},{12,8},{16,12},{20,16},{24,20},{28,24},{32,28}... | collective-permute-start | bytes 983048 | tf_op jit(solution)/shard_map/ppermute | solution.py:31
  16.5 6.7 %collective-permute-start = (bf16[160,1024]{1,0:T(8,128)(2,1)S(1)}, bf16[160,1024]{1,0:T(8,128)(2,1)S(1)}, u32[]{:S(2)}, u32[]{:S(2)}) collective-permute-start(bf16[160,1024]{1,0:T(8,128)(2,1)S(1)} %get-tuple-element.131.m0.refs_0_), channel_id=1, source_target_pairs={{0,1},{1,0},{2,3},{3,2},{4,5},{5,4},{6,7},{7,6},{8,9},{9,8},{10,11... | collective-permute-start | bytes 983048 | tf_op jit(solution)/shard_map/ppermute | solution.py:31
  16.5 6.7 %collective-permute-start.2 = (bf16[160,1024]{1,0:T(8,128)(2,1)S(1)}, bf16[160,1024]{1,0:T(8,128)(2,1)S(1)}, u32[]{:S(2)}, u32[]{:S(2)}) collective-permute-start(bf16[160,1024]{1,0:T(8,128)(2,1)S(1)} %collective-permute-done.1.m2.refs_2_), channel_id=1, source_target_pairs={{0,1},{1,0},{2,3},{3,2},{4,5},{5,4},{6,7},{7,6},{8,9},{9,8},{10,11... | collective-permute-start | bytes 983048 | tf_op jit(solution)/shard_map/ppermute | solution.py:31
  23.3 9.8 %collective-permute-start.5 = (bf16[160,1024]{1,0:T(8,128)(2,1)S(1)}, bf16[160,1024]{1,0:T(8,128)(2,1)S(1)}, u32[]{:S(2)}, u32[]{:S(2)}) collective-permute-start(bf16[160,1024]{1,0:T(8,128)(2,1)S(1)} %collective-permute-done.3.refs_4_), channel_id=1, source_target_pairs={{0,2},{1,3},{2,0},{3,1},{4,6},{5,7},{6,4},{7,5},{8,10},{9,11},{10,... | collective-permute-start | bytes 983048 | tf_op jit(solution)/shard_map/ppermute | solution.py:31
  23.3 9.8 %collective-permute-start.4 = (bf16[160,1024]{1,0:T(8,128)(2,1)S(1)}, bf16[160,1024]{1,0:T(8,128)(2,1)S(1)}, u32[]{:S(2)}, u32[]{:S(2)}) collective-permute-start(bf16[160,1024]{1,0:T(8,128)(2,1)S(1)} %collective-permute-done.3.refs_4_), channel_id=1, source_target_pairs={{0,1},{1,0},{2,3},{3,2},{4,5},{5,4},{6,7},{7,6},{8,9},{9,8},{10,11... | collective-permute-start | bytes 983048 | tf_op jit(solution)/shard_map/ppermute | solution.py:31
  51.9 18.4 %collective-permute-start.7 = (bf16[288,1024]{1,0:T(8,128)(2,1)S(1)}, bf16[288,1024]{1,0:T(8,128)(2,1)S(1)}, u32[]{:S(2)}, u32[]{:S(2)}) collective-permute-start(bf16[288,1024]{1,0:T(8,128)(2,1)S(1)} %get-tuple-element.74), channel_id=1, source_target_pairs={{0,1},{1,0},{2,3},{3,2},{4,5},{5,4},{6,7},{7,6},{8,9},{9,8},{10,11... | collective-permute-start | bytes 1769480 | tf_op jit(solution)/shard_map/ppermute | solution.py:31
  52.1 8.6 %collective-permute-start.11 = (bf16[256,512]{1,0:T(8,128)(2,1)S(1)}, bf16[256,512]{1,0:T(8,128)(2,1)S(1)}, u32[]{:S(2)}, u32[]{:S(2)}) collective-permute-start(bf16[256,512]{1,0:T(8,128)(2,1)S(1)} %get-tuple-element.80), channel_id=1, source_target_pairs={{0,4},{4,0},{8,12},{12,8},{16,20},{20,16},{24,28},{28,24},{32,36},... | collective-permute-start | bytes 786440 | tf_op jit(solution)/shard_map/ppermute | solution.py:31
  52.1 9.3 %collective-permute-start.12 = (bf16[256,512]{1,0:T(8,128)(2,1)S(1)}, bf16[256,512]{1,0:T(8,128)(2,1)S(1)}, u32[]{:S(2)}, u32[]{:S(2)}) collective-permute-start(bf16[256,512]{1,0:T(8,128)(2,1)S(1)} %get-tuple-element.81), channel_id=1, source_target_pairs={{0,128},{4,132},{8,136},{12,140},{16,144},{20,148},{24,152},{28,15... | collective-permute-start | bytes 786440 | tf_op jit(solution)/shard_map/ppermute | solution.py:31
  52.8 17.2 %collective-permute-start.8 = (bf16[272,512]{1,0:T(8,128)(2,1)S(1)}, bf16[272,512]{1,0:T(8,128)(2,1)S(1)}, u32[]{:S(2)}, u32[]{:S(2)}) collective-permute-start(bf16[272,512]{1,0:T(8,128)(2,1)S(1)} %get-tuple-element.76), channel_id=1, source_target_pairs={{0,32},{4,36},{8,40},{12,44},{16,48},{20,52},{24,56},{28,60},{32,6... | collective-permute-start | bytes 835592 | tf_op jit(solution)/shard_map/ppermute | solution.py:31
  53.7 16.3 %collective-permute-start.9 = (bf16[272,512]{1,0:T(8,128)(2,1)S(1)}, bf16[272,512]{1,0:T(8,128)(2,1)S(1)}, u32[]{:S(2)}, u32[]{:S(2)}) collective-permute-start(bf16[272,512]{1,0:T(8,128)(2,1)S(1)} %get-tuple-element.77), channel_id=1, source_target_pairs={{0,64},{4,68},{8,72},{12,76},{16,80},{20,84},{24,88},{28,92},{32,9... | collective-permute-start | bytes 835592 | tf_op jit(solution)/shard_map/ppermute | solution.py:31
  60.7 9.3 %collective-permute-start.10 = (bf16[272,512]{1,0:T(8,128)(2,1)S(1)}, bf16[272,512]{1,0:T(8,128)(2,1)S(1)}, u32[]{:S(2)}, u32[]{:S(2)}) collective-permute-start(bf16[272,512]{1,0:T(8,128)(2,1)S(1)} %get-tuple-element.78), channel_id=1, source_target_pairs={{0,96},{4,100},{8,104},{12,108},{16,112},{20,116},{24,120},{28,124... | collective-permute-start | bytes 835592 | tf_op jit(solution)/shard_map/ppermute | solution.py:31
  61.4 8.6 %collective-permute-start.13 = (bf16[256,512]{1,0:T(8,128)(2,1)S(1)}, bf16[256,512]{1,0:T(8,128)(2,1)S(1)}, u32[]{:S(2)}, u32[]{:S(2)}) collective-permute-start(bf16[256,512]{1,0:T(8,128)(2,1)S(1)} %get-tuple-element.82), channel_id=1, source_target_pairs={{0,132},{4,128},{8,140},{12,136},{16,148},{20,144},{24,156},{28,15... | collective-permute-start | bytes 786440 | tf_op jit(solution)/shard_map/ppermute | solution.py:31
  70.4 15.1 %collective-permute-start.20 = (bf16[144,1024]{1,0:T(8,128)(2,1)S(1)}, bf16[144,1024]{1,0:T(8,128)(2,1)S(1)}, u32[]{:S(2)}, u32[]{:S(2)}) collective-permute-start(bf16[144,1024]{1,0:T(8,128)(2,1)S(1)} %add_convert_fusion), channel_id=1, source_target_pairs={{0,2},{1,3},{2,0},{3,1},{4,6},{5,7},{6,4},{7,5},{8,10},{9,11},{10,... | collective-permute-start | bytes 884744 | tf_op jit(solution)/shard_map/ppermute | solution.py:31
  72.6 6.1 %collective-permute-start.17 = (bf16[64,512]{1,0:T(8,128)(2,1)S(1)}, bf16[64,512]{1,0:T(8,128)(2,1)S(1)}, u32[]{:S(2)}, u32[]{:S(2)}) collective-permute-start(bf16[64,512]{1,0:T(8,128)(2,1)S(1)} %get-tuple-element.96), channel_id=1, source_target_pairs={{0,32},{4,36},{8,40},{12,44},{16,48},{20,52},{24,56},{28,60},{32,6... | collective-permute-start | bytes 196616 | tf_op jit(solution)/shard_map/ppermute | solution.py:31
  73.7 7.5 %collective-permute-start.18 = (bf16[64,512]{1,0:T(8,128)(2,1)S(1)}, bf16[64,512]{1,0:T(8,128)(2,1)S(1)}, u32[]{:S(2)}, u32[]{:S(2)}) collective-permute-start(bf16[64,512]{1,0:T(8,128)(2,1)S(1)} %get-tuple-element.97), channel_id=1, source_target_pairs={{0,64},{4,68},{8,72},{12,76},{16,80},{20,84},{24,88},{28,92},{32,9... | collective-permute-start | bytes 196616 | tf_op jit(solution)/shard_map/ppermute | solution.py:31
  75.8 9.6 %collective-permute-start.14 = (bf16[80,512]{1,0:T(8,128)(2,1)S(1)}, bf16[80,512]{1,0:T(8,128)(2,1)S(1)}, u32[]{:S(2)}, u32[]{:S(2)}) collective-permute-start(bf16[80,512]{1,0:T(8,128)(2,1)S(1)} %get-tuple-element.92), channel_id=1, source_target_pairs={{0,4},{4,0},{8,12},{12,8},{16,20},{20,16},{24,28},{28,24},{32,36},... | collective-permute-start | bytes 245768 | tf_op jit(solution)/shard_map/ppermute | solution.py:31
  77.4 8.0 %collective-permute-start.15 = (bf16[80,512]{1,0:T(8,128)(2,1)S(1)}, bf16[80,512]{1,0:T(8,128)(2,1)S(1)}, u32[]{:S(2)}, u32[]{:S(2)}) collective-permute-start(bf16[80,512]{1,0:T(8,128)(2,1)S(1)} %get-tuple-element.93), channel_id=1, source_target_pairs={{0,128},{4,132},{8,136},{12,140},{16,144},{20,148},{24,152},{28,15... | collective-permute-start | bytes 245768 | tf_op jit(solution)/shard_map/ppermute | solution.py:31
  78.6 6.8 %collective-permute-start.16 = (bf16[80,512]{1,0:T(8,128)(2,1)S(1)}, bf16[80,512]{1,0:T(8,128)(2,1)S(1)}, u32[]{:S(2)}, u32[]{:S(2)}) collective-permute-start(bf16[80,512]{1,0:T(8,128)(2,1)S(1)} %get-tuple-element.94), channel_id=1, source_target_pairs={{0,132},{4,128},{8,140},{12,136},{16,148},{20,144},{24,156},{28,15... | collective-permute-start | bytes 245768 | tf_op jit(solution)/shard_map/ppermute | solution.py:31
  81.2 4.3 %collective-permute-start.19 = (bf16[64,512]{1,0:T(8,128)(2,1)S(1)}, bf16[64,512]{1,0:T(8,128)(2,1)S(1)}, u32[]{:S(2)}, u32[]{:S(2)}) collective-permute-start(bf16[64,512]{1,0:T(8,128)(2,1)S(1)} %get-tuple-element.98), channel_id=1, source_target_pairs={{0,96},{4,100},{8,104},{12,108},{16,112},{20,116},{24,120},{28,124... | collective-permute-start | bytes 196616 | tf_op jit(solution)/shard_map/ppermute | solution.py:31
  85.6 16.9 %collective-permute-start.24 = (bf16[72,1024]{1,0:T(8,128)(2,1)S(1)}, bf16[72,1024]{1,0:T(8,128)(2,1)S(1)}, u32[]{:S(2)}, u32[]{:S(2)}) collective-permute-start(bf16[72,1024]{1,0:T(8,128)(2,1)S(1)} %slice.54), channel_id=1, source_target_pairs={{0,4},{4,8},{8,12},{12,16},{16,20},{20,24},{24,28},{28,32},{32,36}... | collective-permute-start | bytes 442376 | tf_op jit(solution)/shard_map/ppermute | solution.py:31
  86.1 17.7 %collective-permute-start.21 = (bf16[32,1024]{1,0:T(8,128)(2,1)S(1)}, bf16[32,1024]{1,0:T(8,128)(2,1)S(1)}, u32[]{:S(2)}, u32[]{:S(2)}) collective-permute-start(bf16[32,1024]{1,0:T(8,128)(2,1)S(1)} %get-tuple-element.109), channel_id=1, source_target_pairs={{0,8},{4,12},{8,16},{12,20},{16,24},{20,28},{24,0},{28,4},{32,40},... | collective-permute-start | bytes 196616 | tf_op jit(solution)/shard_map/ppermute | solution.py:31
  89.5 14.3 %collective-permute-start.22 = (bf16[32,1024]{1,0:T(8,128)(2,1)S(1)}, bf16[32,1024]{1,0:T(8,128)(2,1)S(1)}, u32[]{:S(2)}, u32[]{:S(2)}) collective-permute-start(bf16[32,1024]{1,0:T(8,128)(2,1)S(1)} %get-tuple-element.110), channel_id=1, source_target_pairs={{0,16},{4,20},{8,24},{12,28},{16,0},{20,4},{24,8},{28,12},{32,48},... | collective-permute-start | bytes 196616 | tf_op jit(solution)/shard_map/ppermute | solution.py:31
  100.1 5.4 %collective-permute-start.23 = (bf16[32,1024]{1,0:T(8,128)(2,1)S(1)}, bf16[32,1024]{1,0:T(8,128)(2,1)S(1)}, u32[]{:S(2)}, u32[]{:S(2)}) collective-permute-start(bf16[32,1024]{1,0:T(8,128)(2,1)S(1)} %get-tuple-element.111), channel_id=1, source_target_pairs={{0,24},{4,28},{8,0},{12,4},{16,8},{20,12},{24,16},{28,20},{32,56},... | collective-permute-start | bytes 196616 | tf_op jit(solution)/shard_map/ppermute | solution.py:31
  (6 other events, 83.8 us)

commit v2 on v1

--- a/solution.py
+++ b/solution.py
@@ -82,7 +82,7 @@
     return jnp.transpose(x)[:16]
 
 
-def bias_kernel(table, index, order, bias, places, places_end):
+def bias_kernel(table, index, order, bias, highs, lows):
     idx = index[...].astype(F32)
     high = jnp.floor(idx * (1.0 / 32.0))
     low = idx - high * 32.0
@@ -94,21 +94,34 @@
 
     own_f = reordered(high) * 32.0 + reordered(low)
     own = own_f.astype(jnp.int32)
-    places[...] = own[:, :128]
-    places_end[...] = turned(own_f, -1.0).astype(jnp.int32)
-    for start, stop in ((0, 128), (128, WT)):
-        part = own[:, start:stop]
-        if stop - start < 128:
-            part = jnp.concatenate([part, jnp.zeros((WT, 128 - stop + start), jnp.int32)], axis=1)
-        chunk = lax.shift_right_logical(part, 7)
-        lane = lax.bitwise_and(part, 127)
-        for head in range(HEADS):
-            found = jnp.zeros((WT, 128), F32)
-            for c in range(6):
-                row = jnp.broadcast_to(table[head : head + 1, c * 128 : (c + 1) * 128], (WT, 128))
-                got = jnp.take_along_axis(row, lane, axis=1, mode="promise_in_bounds")
-                found = jnp.where(chunk == c, got, found)
-            bias[head, :, start:stop] = found[:, : stop - start]
+    ends = turned(own_f, -1.0).astype(jnp.int32)
+
+    def found(head, places):
+        chunk = lax.shift_right_logical(places, 7)
+        lane = lax.bitwise_and(places, 127)
+        total = jnp.zeros(places.shape, F32)
+        for c in range(6):
+            row = jnp.broadcast_to(table[head : head + 1, c * 128 : (c + 1) * 128], places.shape)
+            got = jnp.take_along_axis(row, lane, axis=1, mode="promise_in_bounds")
+            total = jnp.where(chunk == c, got, total)
+        return total
+
+    for head in range(HEADS):
+        bias[head, :, :128] = found(head, own[:, :128])
+        rest = jnp.concatenate([found(head, ends[:, :128]), found(head, ends[:, 128:])], axis=1)
+        rest = jnp.transpose(jnp.concatenate([rest, jnp.zeros((112, 256), F32)], axis=0))
+        bias[head, :, 128:] = rest[:WT, :16]
+
+    high_row = lax.broadcasted_iota(jnp.int32, (16, 256), 0)
+    low_row = lax.broadcasted_iota(jnp.int32, (48, 256), 0)
+    for n in range(88):
+        if n < 72:
+            places = jnp.concatenate([own[2 * n : 2 * n + 1, :128], own[2 * n + 1 : 2 * n + 2, :128]], axis=1)
+        else:
+            places = ends[n - 72 : n - 71]
+        upper = jnp.floor(places.astype(F32) * (1.0 / 48.0) + 0.01).astype(jnp.int32)
+        highs[n] = (high_row == upper).astype(F32).astype(BF16)
+        lows[n] = (low_row == places - upper * 48).astype(F32).astype(BF16)
 
 
 def eastern(width):
@@ -139,13 +152,15 @@
             rows[pl.ds(pl.multiple_of(at + 72, 8), 8), :] = jnp.zeros((8, rows.shape[1]), F32)
 
 
-def head_mask(head, rows):
-    lane = lax.broadcasted_iota(jnp.int32, (rows, WIDTH), 1)
-    return lax.shift_right_logical(lane, 6) == head
-
-
-def only(head, x):
-    return jnp.where(head_mask(head, x.shape[0]), x, 0.0).astype(BF16)
+def by_head(x):
+    lane = lax.shift_right_logical(lax.broadcasted_iota(jnp.int32, (1, WIDTH), 1), 6)
+    return jnp.concatenate([x * (lane == head).astype(F32).astype(BF16) for head in range(HEADS)], axis=0)
+
+
+def own_columns(x):
+    first = lax.broadcasted_iota(jnp.int32, (WT, 128), 1) < HD
+    part = [x[head * WT : (head + 1) * WT, head // 2 * 128 : head // 2 * 128 + 128] for head in range(HEADS)]
+    return jnp.concatenate([jnp.where(first, part[0], part[1]), jnp.where(first, part[2], part[3])], axis=1)
 
 
 def stacked(pieces, tall, gall):
@@ -168,61 +183,38 @@
         proj[m] = projected(m, tall, gall, weight, wo)
 
 
-def segment_sums(sums, ends, places, places_end):
-    low_row = lax.broadcasted_iota(jnp.int32, (128, 256), 0)
-
-    def terms(idx, values):
-        high = jnp.right_shift(idx, 7)
-        low = lax.bitwise_and(idx, 127)
-        a = jnp.concatenate([jnp.where(high == c, values, 0.0) for c in range(6)], axis=0)
-        return a.astype(BF16), (low_row == low).astype(F32).astype(BF16)
-
-    def added(acc, pairs):
-        a = jnp.concatenate([p[0] for p in pairs], axis=1)
-        b = jnp.concatenate([p[1] for p in pairs], axis=1)
-        return acc + lax.dot_general(a, b, NT, preferred_element_type=F32)
-
-    def split(block):
-        top = block.astype(BF16).astype(F32)
-        return top, block - top
-
-    def rows_of(blocks, i):
-        return jnp.concatenate([b[0][i : i + 1] for b in blocks] + [b[1][i : i + 1] for b in blocks], axis=0)
-
-    def step(i, acc):
-        at = pl.ds(pl.multiple_of(i * 8, 8), 8)
-        idx = places[at, :]
-        blocks = [split(sums[head, at, :128]) for head in range(HEADS)]
-        pairs = []
-        for j in range(0, 8, 2):
-            both = jnp.concatenate([idx[j : j + 1], idx[j + 1 : j + 2]], axis=1)
-            pairs.append(terms(both, jnp.concatenate([rows_of(blocks, j), rows_of(blocks, j + 1)], axis=1)))
-        return added(acc, pairs)
-
-    acc = lax.fori_loop(0, 18, step, jnp.zeros((48, 128), F32))
-
-    def last(i, acc):
-        at = pl.ds(pl.multiple_of(i * 8, 8), 8)
-        idx = places_end[at, :]
-        blocks = [split(ends[head, at, :]) for head in range(HEADS)]
-        for j in range(0, 8, 4):
-            acc = added(acc, [terms(idx[n : n + 1], rows_of(blocks, n)) for n in range(j, j + 4)])
-        return acc
-
-    acc = lax.fori_loop(0, 2, last, acc)
-    return jnp.concatenate([acc[c * 8 : (c + 1) * 8] for c in range(6)], axis=1)
+def segment_sums(sums, highs, lows):
+    total = jnp.zeros((64, 48), F32)
+    ends = [turned(sums[head], 0.0) for head in range(HEADS)]
+    for n in range(88):
+        rows = []
+        for head in range(HEADS):
+            if n < 72:
+                row = jnp.concatenate([sums[head, 2 * n : 2 * n + 1, :128], sums[head, 2 * n + 1 : 2 * n + 2, :128]], axis=1)
+            else:
+                row = ends[head][n - 72 : n - 71]
+            rows.append(jnp.broadcast_to(row, (16, 256)).astype(BF16) * highs[n])
+        total += lax.dot_general(jnp.concatenate(rows, axis=0), lows[n], NT, preferred_element_type=F32)
+    return total
 
 
 def bias_rows(x):
     top = x.astype(BF16).astype(F32)
-    return jnp.concatenate([top, x - top], axis=0).astype(BF16)
+    x = top + pltpu.roll(x - top, 64, 1)
+    return jnp.concatenate([x[head * 16 : (head + 1) * 16] for head in range(HEADS)], axis=1).astype(BF16)
+
+
+def bias_sum(s):
+    x = jnp.concatenate([s[:, head * 128 : (head + 1) * 128] for head in range(HEADS)], axis=0)
+    lane = lax.broadcasted_iota(jnp.int32, x.shape, 1)
+    return jnp.where(lane < 64, x + pltpu.roll(x, 64, 1), 0.0)
 
 
 def band_kernel(*refs):
     highs, lows = refs[:4], refs[4:8]
-    weight, wo, bias, early, places, places_end, grads = refs[8:15]
+    weight, wo, bias, early, high_rows, low_rows, grads = refs[8:15]
     ways, pairs = refs[15:19], refs[19:23]
-    tall, gall, qkv, rows, wins, outs, sums, ends, att, labels, full = refs[23:]
+    tall, gall, qkv, rows, wins, outs, sums, att, labels, full = refs[23:]
     own = lax.axis_index("head")
     labels[...] = jnp.zeros_like(labels)
     row = lax.broadcasted_iota(jnp.int32, (8, WIDTH), 0)
@@ -240,57 +232,35 @@
         to_windows(rows, wins, own)
         if m < 3:
             qkv[m] = wins[...].astype(BF16)
-    sums[...] = jnp.zeros_like(sums)
-
-    def window(w, _):
+    for w in range(4):
         marks = labels[w].astype(BF16)
         same = lax.dot_general(marks, marks, TN, preferred_element_type=F32)[:WT, :WT] > 0.5
-        q = qkv[0, w].astype(F32)
+        same = jnp.where(same, 0.0, -jnp.inf)
+        q = by_head(qkv[0, w] * jnp.asarray(0.125, BF16))
         k = qkv[1, w]
         v = qkv[2, w]
-        d = wins[w]
-        k_f = k.astype(F32)
-        v_f = v.astype(F32)
-        total = jnp.zeros((WT, WIDTH), F32)
-        dq = jnp.zeros((WT, WIDTH), F32)
-        dk = jnp.zeros((WT, WIDTH), F32)
-        dv = jnp.zeros((WT, WIDTH), F32)
-        for head in range(HEADS):
-            qh = only(head, q)
-            dh = only(head, d)
-            s = lax.dot_general(qh, k, NT, preferred_element_type=F32)
-            dp = lax.dot_general(dh, v, NT, preferred_element_type=F32)
-            s = s * 0.125 + bias[head]
-            s = jnp.where(same, s, -jnp.inf)
-            e = jnp.exp(s - jnp.max(s, axis=1, keepdims=True))
-            pr = e / jnp.sum(e, axis=1, keepdims=True)
-            prb = pr.astype(BF16)
-            total += jnp.dot(prb, only(head, v_f), preferred_element_type=F32)
-            dv += lax.dot_general(prb, dh, TN, preferred_element_type=F32)
-            ds = pr * (dp - jnp.sum(pr * dp, axis=1, keepdims=True))
-            sums[head] += ds
-            dsb = ds.astype(BF16)
-            dq += jnp.dot(dsb, only(head, k_f), preferred_element_type=F32)
-            dk += lax.dot_general(dsb, qh, TN, preferred_element_type=F32)
-        outs[0, w] = dq * 0.125
-        outs[1, w] = dk * 0.125
-        outs[2, w] = dv
-        outs[3, w] = total
-        return 0
-
-    lax.fori_loop(0, 4, window, 0)
+        d = by_head(wins[w].astype(BF16))
+        s = lax.dot_general(q, k, NT, preferred_element_type=F32).reshape(HEADS, WT, WT)
+        dp = lax.dot_general(d, v, NT, preferred_element_type=F32).reshape(HEADS, WT, WT)
+        s = s + bias[...] + same[None]
+        e = jnp.exp(s - jnp.max(s, axis=2, keepdims=True))
+        pr = e * (1.0 / jnp.sum(e, axis=2, keepdims=True))
+        ds = pr * (dp - jnp.sum(pr * dp, axis=2, keepdims=True))
+        sums[...] = ds if w == 0 else sums[...] + ds
+        prb = pr.astype(BF16).reshape(HEADS * WT, WT)
+        dsb = ds.astype(BF16).reshape(HEADS * WT, WT)
+        outs[0, w] = own_columns(jnp.dot(dsb, k, preferred_element_type=F32)) * 0.125
+        outs[1, w] = lax.dot_general(dsb, q, TN, preferred_element_type=F32)
+        outs[2, w] = lax.dot_general(prb, d, TN, preferred_element_type=F32)
+        outs[3, w] = own_columns(jnp.dot(prb, v, preferred_element_type=F32))
     for m in range(4):
         from_windows(outs.at[m], rows, own)
         if m < 3:
             grads[:, m * WIDTH : (m + 1) * WIDTH] = rows[...].astype(BF16)
     att[...] = rows[...].astype(BF16)
 
-    for head in range(HEADS):
-        ends[head] = turned(sums[head], 0.0)
-    found = segment_sums(sums, ends, places, places_end)
-    found = found + pltpu.roll(found, 4, 0)
-    rest = jnp.concatenate([found[:, 512:], jnp.zeros((8, 256), F32)], axis=1)
-    found = bias_rows(jnp.where(lax.broadcasted_iota(jnp.int32, (8, 512), 0) < 4, found[:, :512], rest))
+    found = segment_sums(sums, high_rows, low_rows)
+    found = bias_rows(jnp.concatenate([found, jnp.zeros((64, 80), F32)], axis=1))
 
     full[:, : 3 * WIDTH] = lax.dot_general(tall[...], grads[...], TN, preferred_element_type=F32).astype(BF16)
     full[:, 3 * WIDTH :] = lax.dot_general(gall[...], att[...], TN, preferred_element_type=F32).astype(BF16)
@@ -332,7 +302,7 @@
     lat = lax.axis_index("lat")
     x, y, z = lat // (NY * NZ), lax.rem(lat // NZ, NY), lax.rem(lat, 2)
     found = stage_rows(ways, pl.ds(256, 16))
-    found = bias_rows(found[:8] + found[8:])
+    found = bias_rows(bias_sum(found))
     for i, out in enumerate(to_pairs):
         start = lax.bitwise_xor(x, i // 2) * 128 + lax.bitwise_xor(z, i % 2) * 16
         for k in range(4):
@@ -348,7 +318,7 @@
     pairs, ways, outs = refs[:4], refs[4:8], refs[8:]
     z = lax.rem(lax.axis_index("lat"), NZ) // 2
     found = stage_rows(pairs, pl.ds(64, 16))
-    found = bias_rows(found[:8] + found[8:])
+    found = bias_rows(bias_sum(found))
     for e, out in enumerate(outs):
         rows = pl.ds(pl.multiple_of(lax.rem(z + e, 4) * 16, 16), 16)
         out[:16, :512] = stage_rows(pairs, rows).astype(BF16)
@@ -363,9 +333,11 @@
     for m in range(3):
         qkv[m] = total[:, m * WIDTH : (m + 1) * WIDTH]
     out[...] = total[:, 3 * WIDTH :]
-    found = stage_rows(parts, pl.ds(16, 16))
-    found = found[:8, :512] + found[8:, :512]
-    bias[...] = jnp.concatenate([found[:4], found[4:]], axis=1)[:, :NB]
+    found = bias_sum(stage_rows(parts, pl.ds(16, 16))[:, :512])
+    for head in range(HEADS):
+        for c in range(16):
+            stop = min(c * 48 + 48, NB)
+            bias[head : head + 1, c * 48 : stop] = found[head * 16 + c : head * 16 + c + 1, : stop - c * 48]
 
 
 def label_rows(labels, first):
@@ -391,19 +363,20 @@
     high = message(0)
     low = back(message(1))
     far_high = across(high)
-    highs = (high, core(high), far_high, core(far_high))
-
     table = jnp.pad(bias_table.T, ((0, 0), (0, 9)))
-    bias, places, places_end = call(
+    bias, high_rows, low_rows = call(
         bias_kernel,
-        (shape((HEADS, WT, WT), F32), shape((WT, 128), jnp.int32), shape((16, 256), jnp.int32)),
+        (shape((HEADS, WT, WT), F32), shape((88, 16, 256), BF16), shape((88, 48, 256), BF16)),
         (),
-        2 * 10**7,
-        10**6,
+        10**8,
+        4 * 10**6,
     )(table, bias_index, jnp.asarray(window_order(), BF16))
-
-    low, bias, places, places_end = lax.optimization_barrier((low, bias, places, places_end))
+    high, bias, high_rows, low_rows = lax.optimization_barrier((high, bias, high_rows, low_rows))
+    near_high = core(high)
     far_low = across(low)
+    far_high, low = lax.optimization_barrier((far_high, low))
+    highs = (high, near_high, far_high, core(far_high))
+
     early = call(
         early_kernel,
         shape((4, HALF, WIDTH), BF16),
@@ -426,7 +399,6 @@
             pltpu.VMEM((4, WT, WIDTH), F32),
             pltpu.VMEM((4, 4, WT, WIDTH), F32),
             pltpu.VMEM((HEADS, WT, WT), F32),
-            pltpu.VMEM((HEADS, 16, 256), F32),
             pltpu.VMEM((ALL, WIDTH), BF16),
             pltpu.VMEM((4, 8, WIDTH), F32),
             pltpu.VMEM((D, D), BF16),
@@ -434,7 +406,7 @@
         3 * 10**9,
         10**7,
         24,
-    )(*highs, *lows, qkv_weight, out_weight, bias, early, places, places_end)
+    )(*highs, *lows, qkv_weight, out_weight, bias, early, high_rows, low_rows)
 
     def by_y(parts):
         return [parts[0]] + [sent(parts[d], "lat", moved(0, d, 0)) for d in range(1, 4)]
@@ -444,6 +416,8 @@
 
     ways, pairs = by_y(blocks[:4]), by_pair(blocks[4:])
 
+    grads, near_pair = lax.optimization_barrier((grads, pairs[1]))
+    pairs[1] = near_pair
     near, far, given = call(
         input_kernel, (shape((WT, D), BF16), shape((WT, D), BF16), shape((2 * WT, D), BF16)), (), 10**9, 5 * 10**6
     )(grads, qkv_weight)

time: 106 us -> 104 us (0.981); the launches traced: 106 us -> 103 us
  waiting for transfers between devices: 33.3 us -> 43.5 us
  Pallas kernels: 21.7 us -> 13 us
  starting transfers between devices: 44.4 us -> 39.6 us
    ppermute x25, waiting for transfers between devices: 33.3 us -> 43.5 us  [sent(): return lax.ppermute(x, axis, [(i, to(i)) for i in range(size)])]
    pallas_call x1, Pallas kernels: 16 us -> 7.48 us  [shards(): call(band_kernel, (shape((ALL, 3 * WIDTH), BF16),) + (shape((272, 512), B...]
    ppermute x25, starting transfers between devices: 44.4 us -> 39.6 us  [sent(): return lax.ppermute(x, axis, [(i, to(i)) for i in range(size)])]
  transfers between devices with their start and end apart: 25 -> 25, of which waited for: 9 -> 12; matrix products, arithmetic and copies ran while one was open for 1% -> 1% of each run, Pallas kernels for 4% -> 3%
where the time goes in v2:
time: 104 us; the launch traced here: 103 us
  waiting for transfers between devices  43.5 us (42%)
  starting transfers between devices  39.6 us (38%)
  Pallas kernels  13 us (12%)
  local copies, waits for them, and re-layouts  5.2 us (5%)
    ppermute x25, waiting for transfers between devices, sent(): return lax.ppermute(x, axis, [(i, to(i)) for i in range(size)])  43.5 us
    ppermute x25, starting transfers between devices, sent(): return lax.ppermute(x, axis, [(i, to(i)) for i in range(size)])  39.6 us
    pallas_call x1, Pallas kernels, shards(): call(band_kernel, (shape((ALL, 3 * WIDTH), BF16),) + (shape((272, 512), B...  7.48 us
    transpose x2, local copies, waits for them, and re-layouts, message(): x[rows].transpose(0, 2, 1, 3).reshape(72, D)  2.38 us
    pallas_call x1, Pallas kernels, shards(): call(bias_kernel, (shape((HEADS, WT, WT), F32), shape((88, 16, 256), BF16...  2.14 us
  transfers between devices with their start and end apart: 25, of which 12 were waited for; matrix products, arithmetic and copies ran while one was open for 1% of the time, Pallas kernels for 3%

profile of v2, /device:TPU:2, one launch (start us, length us, event | category | flops | bytes accessed | tf_op | source)
XLA Modules:
  0.0 102.9 jit_solution(4355205575477092323)
XLA Ops:
  5.1 8.4 %collective-permute-start.2 = (bf16[160,1024]{1,0:T(8,128)(2,1)S(1)}, bf16[160,1024]{1,0:T(8,128)(2,1)S(1)}, u32[]{:S(2)}, u32[]{:S(2)}) collective-permute-start(bf16[160,1024]{1,0:T(8,128)(2,1)S(1)} %get-tuple-element.138), channel_id=1, source_target_pairs={{0,252},{4,0},{8,4},{12,8},{16,12},{20,16},{24,20},{28,24},{32,28}... | collective-permute-start | bytes 983048 | tf_op jit(solution)/shard_map/ppermute | solution.py:31
  13.5 2.4 %collective-permute-start.1 = (bf16[160,1024]{1,0:T(8,128)(2,1)S(1)}, bf16[160,1024]{1,0:T(8,128)(2,1)S(1)}, u32[]{:S(2)}, u32[]{:S(2)}) collective-permute-start(bf16[160,1024]{1,0:T(8,128)(2,1)S(1)} %get-tuple-element.70.m0.refs_0_), channel_id=1, source_target_pairs={{0,2},{1,3},{2,0},{3,1},{4,6},{5,7},{6,4},{7,5},{8,10},{9,11},{10,... | collective-permute-start | bytes 983048 | tf_op jit(solution)/shard_map/ppermute | solution.py:31
  15.9 2.1 %shard_map.111 = (f32[4,144,144]{2,1,0:T(8,128)S(1)}, bf16[88,16,256]{2,1,0:T(8,128)(2,1)S(1)}, bf16[88,48,256]{2,1,0:T(8,128)(2,1)S(1)}) custom-call(f32[4,768]{1,0:T(4,128)S(1)} %pad.20.table, s32[144,144]{1,0:T(8,128)S(1)} %copy-done.2, bf16[144,144]{1,0:T(8,128)(2,1)S(1)} %copy-done.3), custom_call_target="tpu_custom_call" | custom-call | flops 100000000 | bytes 4000000 | tf_op jit(solution)/shard_map/pallas_call | solution.py:367
  18.2 2.3 %collective-permute-done.2.refs_4_ = bf16[160,1024]{1,0:T(8,128)(2,1)S(1)} collective-permute-done((bf16[160,1024]{1,0:T(8,128)(2,1)S(1)}, bf16[160,1024]{1,0:T(8,128)(2,1)S(1)}, u32[]{:S(2)}, u32[]{:S(2)}) %collective-permute-start.2) | collective-permute-done | bytes 327712 | tf_op jit(solution)/shard_map/ppermute | solution.py:31
  20.5 3.7 %collective-permute-done.1.m2.refs_2_ = bf16[160,1024]{1,0:T(8,128)(2,1)S(1)} collective-permute-done((bf16[160,1024]{1,0:T(8,128)(2,1)S(1)}, bf16[160,1024]{1,0:T(8,128)(2,1)S(1)}, u32[]{:S(2)}, u32[]{:S(2)}) %collective-permute-start.1) | collective-permute-done | bytes 327712 | tf_op jit(solution)/shard_map/ppermute | solution.py:31
  24.2 2.4 %collective-permute-start.5 = (bf16[160,1024]{1,0:T(8,128)(2,1)S(1)}, bf16[160,1024]{1,0:T(8,128)(2,1)S(1)}, u32[]{:S(2)}, u32[]{:S(2)}) collective-permute-start(bf16[160,1024]{1,0:T(8,128)(2,1)S(1)} %collective-permute-done.2.refs_4_), channel_id=1, source_target_pairs={{0,2},{1,3},{2,0},{3,1},{4,6},{5,7},{6,4},{7,5},{8,10},{9,11},{10,... | collective-permute-start | bytes 983048 | tf_op jit(solution)/shard_map/ppermute | solution.py:31
  27.7 8.1 %collective-permute-done.5.refs_6_ = bf16[160,1024]{1,0:T(8,128)(2,1)S(1)} collective-permute-done((bf16[160,1024]{1,0:T(8,128)(2,1)S(1)}, bf16[160,1024]{1,0:T(8,128)(2,1)S(1)}, u32[]{:S(2)}, u32[]{:S(2)}) %collective-permute-start.5) | collective-permute-done | bytes 327712 | tf_op jit(solution)/shard_map/ppermute | solution.py:31
  35.8 1.6 %collective-permute-done.6.refs_7_ = bf16[160,1024]{1,0:T(8,128)(2,1)S(1)} collective-permute-done((bf16[160,1024]{1,0:T(8,128)(2,1)S(1)}, bf16[160,1024]{1,0:T(8,128)(2,1)S(1)}, u32[]{:S(2)}, u32[]{:S(2)}) %collective-permute-start.6) | collective-permute-done | bytes 327712 | tf_op jit(solution)/shard_map/ppermute | solution.py:31
  37.4 7.5 %shard_map.113 = (bf16[640,768]{1,0:T(8,128)(2,1)S(1)}, bf16[272,512]{1,0:T(8,128)(2,1)S(1)}, bf16[272,512]{1,0:T(8,128)(2,1)S(1)}, bf16[272,512]{1,0:T(8,128)(2...) custom-call(bf16[160,1024]{1,0:T(8,128)(2,1)S(1)} %get-tuple-element, ...), custom_call_target="tpu_custom_call" | custom-call | flops 3000000000 | bytes 10000000 | tf_op jit(solution)/shard_map/pallas_call | solution.py:391
  45.0 8.3 %collective-permute-done.7.refs_5_ = bf16[256,512]{1,0:T(8,128)(2,1)S(1)} collective-permute-done((bf16[256,512]{1,0:T(8,128)(2,1)S(1)}, bf16[256,512]{1,0:T(8,128)(2,1)S(1)}, u32[]{:S(2)}, u32[]{:S(2)}) %collective-permute-start.7) | collective-permute-done | bytes 262176 | tf_op jit(solution)/shard_map/ppermute | solution.py:31
  54.7 1.6 %collective-permute-start.12 = (bf16[256,512]{1,0:T(8,128)(2,1)S(1)}, bf16[256,512]{1,0:T(8,128)(2,1)S(1)}, u32[]{:S(2)}, u32[]{:S(2)}) collective-permute-start(bf16[256,512]{1,0:T(8,128)(2,1)S(1)} %get-tuple-element.89), channel_id=1, source_target_pairs={{0,128},{4,132},{8,136},{12,140},{16,144},{20,148},{24,152},{28,15... | collective-permute-start | bytes 786440 | tf_op jit(solution)/shard_map/ppermute | solution.py:31
  56.2 1.3 %collective-permute-start.10 = (bf16[272,512]{1,0:T(8,128)(2,1)S(1)}, bf16[272,512]{1,0:T(8,128)(2,1)S(1)}, u32[]{:S(2)}, u32[]{:S(2)}) collective-permute-start(bf16[272,512]{1,0:T(8,128)(2,1)S(1)} %get-tuple-element.85), channel_id=1, source_target_pairs={{0,64},{4,68},{8,72},{12,76},{16,80},{20,84},{24,88},{28,92},{32,9... | collective-permute-start | bytes 835592 | tf_op jit(solution)/shard_map/ppermute | solution.py:31
  57.5 1.9 %collective-permute-start.11 = (bf16[272,512]{1,0:T(8,128)(2,1)S(1)}, bf16[272,512]{1,0:T(8,128)(2,1)S(1)}, u32[]{:S(2)}, u32[]{:S(2)}) collective-permute-start(bf16[272,512]{1,0:T(8,128)(2,1)S(1)} %get-tuple-element.86), channel_id=1, source_target_pairs={{0,96},{4,100},{8,104},{12,108},{16,112},{20,116},{24,120},{28,124... | collective-permute-start | bytes 835592 | tf_op jit(solution)/shard_map/ppermute | solution.py:31
  59.5 3.9 %collective-permute-done.12.refs_6_ = bf16[256,512]{1,0:T(8,128)(2,1)S(1)} collective-permute-done((bf16[256,512]{1,0:T(8,128)(2,1)S(1)}, bf16[256,512]{1,0:T(8,128)(2,1)S(1)}, u32[]{:S(2)}, u32[]{:S(2)}) %collective-permute-start.12) | collective-permute-done | bytes 262176 | tf_op jit(solution)/shard_map/ppermute | solution.py:31
  64.6 7.5 %collective-permute-done.13.refs_7_ = bf16[256,512]{1,0:T(8,128)(2,1)S(1)} collective-permute-done((bf16[256,512]{1,0:T(8,128)(2,1)S(1)}, bf16[256,512]{1,0:T(8,128)(2,1)S(1)}, u32[]{:S(2)}, u32[]{:S(2)}) %collective-permute-start.13) | collective-permute-done | bytes 262176 | tf_op jit(solution)/shard_map/ppermute | solution.py:31
  73.2 2.2 %collective-permute-start.20 = (bf16[144,1024]{1,0:T(8,128)(2,1)S(1)}, bf16[144,1024]{1,0:T(8,128)(2,1)S(1)}, u32[]{:S(2)}, u32[]{:S(2)}) collective-permute-start(bf16[144,1024]{1,0:T(8,128)(2,1)S(1)} %add_convert_fusion), channel_id=1, source_target_pairs={{0,2},{1,3},{2,0},{3,1},{4,6},{5,7},{6,4},{7,5},{8,10},{9,11},{10,... | collective-permute-start | bytes 884744 | tf_op jit(solution)/shard_map/ppermute | solution.py:31
  75.7 3.6 %collective-permute-start.18 = (bf16[64,512]{1,0:T(8,128)(2,1)S(1)}, bf16[64,512]{1,0:T(8,128)(2,1)S(1)}, u32[]{:S(2)}, u32[]{:S(2)}) collective-permute-start(bf16[64,512]{1,0:T(8,128)(2,1)S(1)} %get-tuple-element.105), channel_id=1, source_target_pairs={{0,64},{4,68},{8,72},{12,76},{16,80},{20,84},{24,88},{28,92},{32,9... | collective-permute-start | bytes 196616 | tf_op jit(solution)/shard_map/ppermute | solution.py:31
  79.5 1.4 %collective-permute-start.15 = (bf16[80,512]{1,0:T(8,128)(2,1)S(1)}, bf16[80,512]{1,0:T(8,128)(2,1)S(1)}, u32[]{:S(2)}, u32[]{:S(2)}) collective-permute-start(bf16[80,512]{1,0:T(8,128)(2,1)S(1)} %get-tuple-element.101), channel_id=1, source_target_pairs={{0,128},{4,132},{8,136},{12,140},{16,144},{20,148},{24,152},{28,15... | collective-permute-start | bytes 245768 | tf_op jit(solution)/shard_map/ppermute | solution.py:31
  81.3 1.4 %collective-permute-start.16 = (bf16[80,512]{1,0:T(8,128)(2,1)S(1)}, bf16[80,512]{1,0:T(8,128)(2,1)S(1)}, u32[]{:S(2)}, u32[]{:S(2)}) collective-permute-start(bf16[80,512]{1,0:T(8,128)(2,1)S(1)} %get-tuple-element.102), channel_id=1, source_target_pairs={{0,132},{4,128},{8,140},{12,136},{16,148},{20,144},{24,156},{28,15... | collective-permute-start | bytes 245768 | tf_op jit(solution)/shard_map/ppermute | solution.py:31
  82.7 1.7 %collective-permute-start.19 = (bf16[64,512]{1,0:T(8,128)(2,1)S(1)}, bf16[64,512]{1,0:T(8,128)(2,1)S(1)}, u32[]{:S(2)}, u32[]{:S(2)}) collective-permute-start(bf16[64,512]{1,0:T(8,128)(2,1)S(1)} %get-tuple-element.106), channel_id=1, source_target_pairs={{0,96},{4,100},{8,104},{12,108},{16,112},{20,116},{24,120},{28,124... | collective-permute-start | bytes 196616 | tf_op jit(solution)/shard_map/ppermute | solution.py:31
  84.4 2.6 %collective-permute-done.19.refs_7_ = bf16[64,512]{1,0:T(8,128)(2,1)S(1)} collective-permute-done((bf16[64,512]{1,0:T(8,128)(2,1)S(1)}, bf16[64,512]{1,0:T(8,128)(2,1)S(1)}, u32[]{:S(2)}, u32[]{:S(2)}) %collective-permute-start.19) | collective-permute-done | bytes 65568 | tf_op jit(solution)/shard_map/ppermute | solution.py:31
  87.2 1.6 %collective-permute-start.24 = (bf16[72,1024]{1,0:T(8,128)(2,1)S(1)}, bf16[72,1024]{1,0:T(8,128)(2,1)S(1)}, u32[]{:S(2)}, u32[]{:S(2)}) collective-permute-start(bf16[72,1024]{1,0:T(8,128)(2,1)S(1)} %slice.54), channel_id=1, source_target_pairs={{0,4},{4,8},{8,12},{12,16},{16,20},{20,24},{24,28},{28,32},{32,36}... | collective-permute-start | bytes 442376 | tf_op jit(solution)/shard_map/ppermute | solution.py:31
  89.0 7.4 %collective-permute-start.22 = (bf16[32,1024]{1,0:T(8,128)(2,1)S(1)}, bf16[32,1024]{1,0:T(8,128)(2,1)S(1)}, u32[]{:S(2)}, u32[]{:S(2)}) collective-permute-start(bf16[32,1024]{1,0:T(8,128)(2,1)S(1)} %get-tuple-element.118), channel_id=1, source_target_pairs={{0,16},{4,20},{8,24},{12,28},{16,0},{20,4},{24,8},{28,12},{32,48},... | collective-permute-start | bytes 196616 | tf_op jit(solution)/shard_map/ppermute | solution.py:31
  96.4 4.2 %collective-permute-done.24 = bf16[72,1024]{1,0:T(8,128)(2,1)S(1)} collective-permute-done((bf16[72,1024]{1,0:T(8,128)(2,1)S(1)}, bf16[72,1024]{1,0:T(8,128)(2,1)S(1)}, u32[]{:S(2)}, u32[]{:S(2)}) %collective-permute-start.24) | collective-permute-done | bytes 147488 | tf_op jit(solution)/shard_map/ppermute | solution.py:31
  (74 shorter events, 12.8 us)
Async XLA Ops:
  5.1 15.4 %collective-permute-start.2 = (bf16[160,1024]{1,0:T(8,128)(2,1)S(1)}, bf16[160,1024]{1,0:T(8,128)(2,1)S(1)}, u32[]{:S(2)}, u32[]{:S(2)}) collective-permute-start(bf16[160,1024]{1,0:T(8,128)(2,1)S(1)} %get-tuple-element.138), channel_id=1, source_target_pairs={{0,252},{4,0},{8,4},{12,8},{16,12},{20,16},{24,20},{28,24},{32,28}... | collective-permute-start | bytes 983048 | tf_op jit(solution)/shard_map/ppermute | solution.py:31
  13.5 10.7 %collective-permute-start.1 = (bf16[160,1024]{1,0:T(8,128)(2,1)S(1)}, bf16[160,1024]{1,0:T(8,128)(2,1)S(1)}, u32[]{:S(2)}, u32[]{:S(2)}) collective-permute-start(bf16[160,1024]{1,0:T(8,128)(2,1)S(1)} %get-tuple-element.70.m0.refs_0_), channel_id=1, source_target_pairs={{0,2},{1,3},{2,0},{3,1},{4,6},{5,7},{6,4},{7,5},{8,10},{9,11},{10,... | collective-permute-start | bytes 983048 | tf_op jit(solution)/shard_map/ppermute | solution.py:31
  18.1 8.7 %collective-permute-start = (bf16[160,1024]{1,0:T(8,128)(2,1)S(1)}, bf16[160,1024]{1,0:T(8,128)(2,1)S(1)}, u32[]{:S(2)}, u32[]{:S(2)}) collective-permute-start(bf16[160,1024]{1,0:T(8,128)(2,1)S(1)} %get-tuple-element.70.m0.refs_0_), channel_id=1, source_target_pairs={{0,1},{1,0},{2,3},{3,2},{4,5},{5,4},{6,7},{7,6},{8,9},{9,8},{10,11... | collective-permute-start | bytes 983048 | tf_op jit(solution)/shard_map/ppermute | solution.py:31
  24.2 2.7 %collective-permute-start.3 = (bf16[160,1024]{1,0:T(8,128)(2,1)S(1)}, bf16[160,1024]{1,0:T(8,128)(2,1)S(1)}, u32[]{:S(2)}, u32[]{:S(2)}) collective-permute-start(bf16[160,1024]{1,0:T(8,128)(2,1)S(1)} %collective-permute-done.1.m2.refs_2_), channel_id=1, source_target_pairs={{0,1},{1,0},{2,3},{3,2},{4,5},{5,4},{6,7},{7,6},{8,9},{9,8},{10,11... | collective-permute-start | bytes 983048 | tf_op jit(solution)/shard_map/ppermute | solution.py:31
  24.2 11.6 %collective-permute-start.5 = (bf16[160,1024]{1,0:T(8,128)(2,1)S(1)}, bf16[160,1024]{1,0:T(8,128)(2,1)S(1)}, u32[]{:S(2)}, u32[]{:S(2)}) collective-permute-start(bf16[160,1024]{1,0:T(8,128)(2,1)S(1)} %collective-permute-done.2.refs_4_), channel_id=1, source_target_pairs={{0,2},{1,3},{2,0},{3,1},{4,6},{5,7},{6,4},{7,5},{8,10},{9,11},{10,... | collective-permute-start | bytes 983048 | tf_op jit(solution)/shard_map/ppermute | solution.py:31
  26.6 9.2 %collective-permute-start.4 = (bf16[160,1024]{1,0:T(8,128)(2,1)S(1)}, bf16[160,1024]{1,0:T(8,128)(2,1)S(1)}, u32[]{:S(2)}, u32[]{:S(2)}) collective-permute-start(bf16[160,1024]{1,0:T(8,128)(2,1)S(1)} %collective-permute-done.2.refs_4_), channel_id=1, source_target_pairs={{0,1},{1,0},{2,3},{3,2},{4,5},{5,4},{6,7},{7,6},{8,9},{9,8},{10,11... | collective-permute-start | bytes 983048 | tf_op jit(solution)/shard_map/ppermute | solution.py:31
  44.9 8.4 %collective-permute-start.7 = (bf16[256,512]{1,0:T(8,128)(2,1)S(1)}, bf16[256,512]{1,0:T(8,128)(2,1)S(1)}, u32[]{:S(2)}, u32[]{:S(2)}) collective-permute-start(bf16[256,512]{1,0:T(8,128)(2,1)S(1)} %get-tuple-element.79), channel_id=1, source_target_pairs={{0,4},{4,0},{8,12},{12,8},{16,20},{20,16},{24,28},{28,24},{32,36},... | collective-permute-start | bytes 786440 | tf_op jit(solution)/shard_map/ppermute | solution.py:31
  54.6 18.6 %collective-permute-start.8 = (bf16[288,1024]{1,0:T(8,128)(2,1)S(1)}, bf16[288,1024]{1,0:T(8,128)(2,1)S(1)}, u32[]{:S(2)}, u32[]{:S(2)}) collective-permute-start(bf16[288,1024]{1,0:T(8,128)(2,1)S(1)} %get-tuple-element.82), channel_id=1, source_target_pairs={{0,1},{1,0},{2,3},{3,2},{4,5},{5,4},{6,7},{7,6},{8,9},{9,8},{10,11... | collective-permute-start | bytes 1769480 | tf_op jit(solution)/shard_map/ppermute | solution.py:31
  54.7 8.7 %collective-permute-start.12 = (bf16[256,512]{1,0:T(8,128)(2,1)S(1)}, bf16[256,512]{1,0:T(8,128)(2,1)S(1)}, u32[]{:S(2)}, u32[]{:S(2)}) collective-permute-start(bf16[256,512]{1,0:T(8,128)(2,1)S(1)} %get-tuple-element.89), channel_id=1, source_target_pairs={{0,128},{4,132},{8,136},{12,140},{16,144},{20,148},{24,152},{28,15... | collective-permute-start | bytes 786440 | tf_op jit(solution)/shard_map/ppermute | solution.py:31
  56.2 15.9 %collective-permute-start.9 = (bf16[272,512]{1,0:T(8,128)(2,1)S(1)}, bf16[272,512]{1,0:T(8,128)(2,1)S(1)}, u32[]{:S(2)}, u32[]{:S(2)}) collective-permute-start(bf16[272,512]{1,0:T(8,128)(2,1)S(1)} %get-tuple-element.84), channel_id=1, source_target_pairs={{0,32},{4,36},{8,40},{12,44},{16,48},{20,52},{24,56},{28,60},{32,6... | collective-permute-start | bytes 835592 | tf_op jit(solution)/shard_map/ppermute | solution.py:31
  56.2 15.9 %collective-permute-start.10 = (bf16[272,512]{1,0:T(8,128)(2,1)S(1)}, bf16[272,512]{1,0:T(8,128)(2,1)S(1)}, u32[]{:S(2)}, u32[]{:S(2)}) collective-permute-start(bf16[272,512]{1,0:T(8,128)(2,1)S(1)} %get-tuple-element.85), channel_id=1, source_target_pairs={{0,64},{4,68},{8,72},{12,76},{16,80},{20,84},{24,88},{28,92},{32,9... | collective-permute-start | bytes 835592 | tf_op jit(solution)/shard_map/ppermute | solution.py:31
  57.5 15.2 %collective-permute-start.11 = (bf16[272,512]{1,0:T(8,128)(2,1)S(1)}, bf16[272,512]{1,0:T(8,128)(2,1)S(1)}, u32[]{:S(2)}, u32[]{:S(2)}) collective-permute-start(bf16[272,512]{1,0:T(8,128)(2,1)S(1)} %get-tuple-element.86), channel_id=1, source_target_pairs={{0,96},{4,100},{8,104},{12,108},{16,112},{20,116},{24,120},{28,124... | collective-permute-start | bytes 835592 | tf_op jit(solution)/shard_map/ppermute | solution.py:31
  63.4 8.7 %collective-permute-start.13 = (bf16[256,512]{1,0:T(8,128)(2,1)S(1)}, bf16[256,512]{1,0:T(8,128)(2,1)S(1)}, u32[]{:S(2)}, u32[]{:S(2)}) collective-permute-start(bf16[256,512]{1,0:T(8,128)(2,1)S(1)} %get-tuple-element.90), channel_id=1, source_target_pairs={{0,132},{4,128},{8,140},{12,136},{16,148},{20,144},{24,156},{28,15... | collective-permute-start | bytes 786440 | tf_op jit(solution)/shard_map/ppermute | solution.py:31
  73.2 13.8 %collective-permute-start.20 = (bf16[144,1024]{1,0:T(8,128)(2,1)S(1)}, bf16[144,1024]{1,0:T(8,128)(2,1)S(1)}, u32[]{:S(2)}, u32[]{:S(2)}) collective-permute-start(bf16[144,1024]{1,0:T(8,128)(2,1)S(1)} %add_convert_fusion), channel_id=1, source_target_pairs={{0,2},{1,3},{2,0},{3,1},{4,6},{5,7},{6,4},{7,5},{8,10},{9,11},{10,... | collective-permute-start | bytes 884744 | tf_op jit(solution)/shard_map/ppermute | solution.py:31
  75.4 5.9 %collective-permute-start.17 = (bf16[64,512]{1,0:T(8,128)(2,1)S(1)}, bf16[64,512]{1,0:T(8,128)(2,1)S(1)}, u32[]{:S(2)}, u32[]{:S(2)}) collective-permute-start(bf16[64,512]{1,0:T(8,128)(2,1)S(1)} %get-tuple-element.104), channel_id=1, source_target_pairs={{0,32},{4,36},{8,40},{12,44},{16,48},{20,52},{24,56},{28,60},{32,6... | collective-permute-start | bytes 196616 | tf_op jit(solution)/shard_map/ppermute | solution.py:31
  75.7 7.1 %collective-permute-start.18 = (bf16[64,512]{1,0:T(8,128)(2,1)S(1)}, bf16[64,512]{1,0:T(8,128)(2,1)S(1)}, u32[]{:S(2)}, u32[]{:S(2)}) collective-permute-start(bf16[64,512]{1,0:T(8,128)(2,1)S(1)} %get-tuple-element.105), channel_id=1, source_target_pairs={{0,64},{4,68},{8,72},{12,76},{16,80},{20,84},{24,88},{28,92},{32,9... | collective-permute-start | bytes 196616 | tf_op jit(solution)/shard_map/ppermute | solution.py:31
  79.2 7.8 %collective-permute-start.14 = (bf16[80,512]{1,0:T(8,128)(2,1)S(1)}, bf16[80,512]{1,0:T(8,128)(2,1)S(1)}, u32[]{:S(2)}, u32[]{:S(2)}) collective-permute-start(bf16[80,512]{1,0:T(8,128)(2,1)S(1)} %get-tuple-element.100), channel_id=1, source_target_pairs={{0,4},{4,0},{8,12},{12,8},{16,20},{20,16},{24,28},{28,24},{32,36},... | collective-permute-start | bytes 245768 | tf_op jit(solution)/shard_map/ppermute | solution.py:31
  79.5 7.5 %collective-permute-start.15 = (bf16[80,512]{1,0:T(8,128)(2,1)S(1)}, bf16[80,512]{1,0:T(8,128)(2,1)S(1)}, u32[]{:S(2)}, u32[]{:S(2)}) collective-permute-start(bf16[80,512]{1,0:T(8,128)(2,1)S(1)} %get-tuple-element.101), channel_id=1, source_target_pairs={{0,128},{4,132},{8,136},{12,140},{16,144},{20,148},{24,152},{28,15... | collective-permute-start | bytes 245768 | tf_op jit(solution)/shard_map/ppermute | solution.py:31
  81.3 5.7 %collective-permute-start.16 = (bf16[80,512]{1,0:T(8,128)(2,1)S(1)}, bf16[80,512]{1,0:T(8,128)(2,1)S(1)}, u32[]{:S(2)}, u32[]{:S(2)}) collective-permute-start(bf16[80,512]{1,0:T(8,128)(2,1)S(1)} %get-tuple-element.102), channel_id=1, source_target_pairs={{0,132},{4,128},{8,140},{12,136},{16,148},{20,144},{24,156},{28,15... | collective-permute-start | bytes 245768 | tf_op jit(solution)/shard_map/ppermute | solution.py:31
  82.7 4.3 %collective-permute-start.19 = (bf16[64,512]{1,0:T(8,128)(2,1)S(1)}, bf16[64,512]{1,0:T(8,128)(2,1)S(1)}, u32[]{:S(2)}, u32[]{:S(2)}) collective-permute-start(bf16[64,512]{1,0:T(8,128)(2,1)S(1)} %get-tuple-element.106), channel_id=1, source_target_pairs={{0,96},{4,100},{8,104},{12,108},{16,112},{20,116},{24,120},{28,124... | collective-permute-start | bytes 196616 | tf_op jit(solution)/shard_map/ppermute | solution.py:31
  87.2 13.4 %collective-permute-start.24 = (bf16[72,1024]{1,0:T(8,128)(2,1)S(1)}, bf16[72,1024]{1,0:T(8,128)(2,1)S(1)}, u32[]{:S(2)}, u32[]{:S(2)}) collective-permute-start(bf16[72,1024]{1,0:T(8,128)(2,1)S(1)} %slice.54), channel_id=1, source_target_pairs={{0,4},{4,8},{8,12},{12,16},{16,20},{20,24},{24,28},{28,32},{32,36}... | collective-permute-start | bytes 442376 | tf_op jit(solution)/shard_map/ppermute | solution.py:31
  88.9 12.9 %collective-permute-start.21 = (bf16[32,1024]{1,0:T(8,128)(2,1)S(1)}, bf16[32,1024]{1,0:T(8,128)(2,1)S(1)}, u32[]{:S(2)}, u32[]{:S(2)}) collective-permute-start(bf16[32,1024]{1,0:T(8,128)(2,1)S(1)} %get-tuple-element.117), channel_id=1, source_target_pairs={{0,8},{4,12},{8,16},{12,20},{16,24},{20,28},{24,0},{28,4},{32,40},... | collective-permute-start | bytes 196616 | tf_op jit(solution)/shard_map/ppermute | solution.py:31
  89.0 12.8 %collective-permute-start.22 = (bf16[32,1024]{1,0:T(8,128)(2,1)S(1)}, bf16[32,1024]{1,0:T(8,128)(2,1)S(1)}, u32[]{:S(2)}, u32[]{:S(2)}) collective-permute-start(bf16[32,1024]{1,0:T(8,128)(2,1)S(1)} %get-tuple-element.118), channel_id=1, source_target_pairs={{0,16},{4,20},{8,24},{12,28},{16,0},{20,4},{24,8},{28,12},{32,48},... | collective-permute-start | bytes 196616 | tf_op jit(solution)/shard_map/ppermute | solution.py:31
  96.4 5.7 %collective-permute-start.23 = (bf16[32,1024]{1,0:T(8,128)(2,1)S(1)}, bf16[32,1024]{1,0:T(8,128)(2,1)S(1)}, u32[]{:S(2)}, u32[]{:S(2)}) collective-permute-start(bf16[32,1024]{1,0:T(8,128)(2,1)S(1)} %get-tuple-element.119), channel_id=1, source_target_pairs={{0,24},{4,28},{8,0},{12,4},{16,8},{20,12},{24,16},{28,20},{32,56},... | collective-permute-start | bytes 196616 | tf_op jit(solution)/shard_map/ppermute | solution.py:31
  (6 other events, 99.8 us)

commit v3 on v2

--- a/solution.py
+++ b/solution.py
@@ -132,22 +132,22 @@
 def to_windows(rows, wins, own):
     first = eastern(rows.shape[1])
     for w in range(4):
-        near = lax.bitwise_xor(own, w) * ROWS
-        east = lax.bitwise_xor(own, (w + 1) % 4) * ROWS
+        near = lax.bitwise_xor(own, w) * 2 * ROWS
+        east = lax.bitwise_xor(own, (w + 1) % 4) * 2 * ROWS
         for r in range(2):
-            a = rows[pl.ds(pl.multiple_of(near + r * HALF, 8), 72), :]
-            b = rows[pl.ds(pl.multiple_of(east + r * HALF, 8), 72), :]
+            a = rows[pl.ds(pl.multiple_of(near + r * ROWS, 8), 72), :]
+            b = rows[pl.ds(pl.multiple_of(east + r * ROWS, 8), 72), :]
             wins[w, r * 72 : (r + 1) * 72, :] = jnp.where(first, b, a)
 
 
 def from_windows(wins, rows, own):
     first = eastern(rows.shape[1])
     for s in range(4):
-        start = lax.bitwise_xor(own, s) * ROWS
+        start = lax.bitwise_xor(own, s) * 2 * ROWS
         for r in range(2):
             a = wins[s, r * 72 : (r + 1) * 72, :]
             b = wins[(s + 3) % 4, r * 72 : (r + 1) * 72, :]
-            at = pl.multiple_of(start + r * HALF, 8)
+            at = pl.multiple_of(start + r * ROWS, 8)
             rows[pl.ds(at, 72), :] = jnp.where(first, b, a)
             rows[pl.ds(pl.multiple_of(at + 72, 8), 8), :] = jnp.zeros((8, rows.shape[1]), F32)
 
@@ -166,7 +166,8 @@
 def stacked(pieces, tall, gall):
     for p, piece in enumerate(pieces):
         tall[p * ROWS : (p + 1) * ROWS, :] = piece[:ROWS, :]
-        gall[p * ROWS : (p + 1) * ROWS, :] = piece[ROWS:, :]
+        rows = jnp.concatenate([piece[ROWS:, :].astype(F32), jnp.zeros((8, D), F32)], axis=0)
+        gall[p * ROWS : (p + 1) * ROWS, :] = rows.astype(BF16)
 
 
 def projected(m, tall, gall, weight, wo):
@@ -210,10 +211,19 @@
     return jnp.where(lane < 64, x + pltpu.roll(x, 64, 1), 0.0)
 
 
+def folded(rows):
+    rest = jnp.concatenate([rows[:, 384:], jnp.zeros((16, 256), BF16)], axis=1)
+    return jnp.concatenate([rows[:, :384], rest], axis=0)
+
+
+def unfolded(rows):
+    return jnp.concatenate([rows[:16], rows[16:, :128]], axis=1)
+
+
 def band_kernel(*refs):
-    highs, lows = refs[:4], refs[4:8]
+    pieces = refs[:8]
     weight, wo, bias, early, high_rows, low_rows, grads = refs[8:15]
-    ways, pairs = refs[15:19], refs[19:23]
+    ways, sides, pairs = refs[15:19], refs[19:21], refs[21:23]
     tall, gall, qkv, rows, wins, outs, sums, att, labels, full = refs[23:]
     own = lax.axis_index("head")
     labels[...] = jnp.zeros_like(labels)
@@ -221,11 +231,11 @@
     for p in range(4):
         shard = lax.bitwise_xor(own, p)
         before = lax.rem(shard + 3, 4)
-        marks = highs[p][64:80, :WIDTH].astype(F32)[8:16] + lows[p][64:80, :WIDTH].astype(F32)[8:16]
+        marks = sum(pieces[2 * p + r][64:80, :WIDTH].astype(F32)[8:16] for r in range(2))
         labels[shard] += jnp.where(row < 4, marks, 0.0)
         labels[before] += jnp.where(row < 4, pltpu.roll(marks, 4, 0), 0.0)
-    stacked(highs, tall.at[:HALF, :], gall.at[:HALF, :])
-    stacked(lows, tall.at[HALF:, :], gall.at[HALF:, :])
+    stacked(pieces[:4], tall.at[:HALF, :], gall.at[:HALF, :])
+    stacked(pieces[4:], tall.at[HALF:, :], gall.at[HALF:, :])
     for m in range(4):
         rows[:HALF, :] = early[m].astype(F32)
         rows[HALF:, :] = projected(m, tall.at[HALF:, :], gall.at[HALF:, :], weight, wo).astype(F32)
@@ -267,15 +277,16 @@
     lat = lax.axis_index("lat")
     x, y, z = lat // (NY * NZ), lax.rem(lat // NZ, NY), lax.rem(lat, 2)
     for d, out in enumerate(ways):
-        out[256:272, :] = found
         for half in range(2):
             at = pl.ds(pl.multiple_of(half * 512 + lax.rem(y + d, NY) * 128, 128), 128)
-            out[half * 128 : (half + 1) * 128, :] = full[at, :512]
+            out[half * 128 : (half + 1) * 128, :] = full[at, :384]
+    for i, out in enumerate(sides):
+        out[:512, :] = full[pl.ds(pl.multiple_of(lax.bitwise_xor(x, i) * 512, 512), 512), 384:768]
+        out[512:, :] = folded(found)
     for i, out in enumerate(pairs):
-        start = lax.bitwise_xor(x, i // 2) * 512 + lax.bitwise_xor(z, i % 2) * 16
-        for b in range(16):
-            at = pl.ds(pl.multiple_of(start + (b // 4) * 128 + (b % 4) * 32, 16), 16)
-            out[b * 16 : (b + 1) * 16, :] = full[at, 512:]
+        for b in range(32):
+            at = pl.ds(pl.multiple_of(lax.bitwise_xor(z, i) * 16 + (b // 4) * 128 + (b % 4) * 32, 16), 16)
+            out[b * 16 : (b + 1) * 16, :] = full[at, 768:]
 
 
 def input_kernel(grads, weight, near, far, given):
@@ -285,44 +296,67 @@
             grads[:, m * WIDTH : (m + 1) * WIDTH], weight[m], NT, preferred_element_type=F32
         )
     for p, out in enumerate((near.at[...], given.at[:WT, :], far.at[...], given.at[WT:, :])):
-        start = p * ROWS
-        both = jnp.concatenate([total[start : start + 72], total[start + HALF : start + HALF + 72]], axis=0)
+        start = p * 2 * ROWS
+        both = jnp.concatenate([total[start : start + 72], total[start + ROWS : start + ROWS + 72]], axis=0)
         out[...] = both.astype(BF16)
 
 
-def stage_rows(parts, rows):
-    total = parts[0][rows, :].astype(F32)
+def stage_rows(parts, rows, columns=slice(None)):
+    total = parts[0][rows, columns].astype(F32)
     for part in parts[1:]:
-        total += part[rows, :].astype(F32)
+        total += part[rows, columns].astype(F32)
     return total
 
 
+def place():
+    lat = lax.axis_index("lat")
+    return lat // (NY * NZ), lax.rem(lat // NZ, NY), lax.rem(lat, NZ)
+
+
 def second_kernel(*refs):
-    ways, pairs, to_pairs, to_ways = refs[:4], refs[4:8], refs[8:12], refs[12:]
-    lat = lax.axis_index("lat")
-    x, y, z = lat // (NY * NZ), lax.rem(lat // NZ, NY), lax.rem(lat, 2)
-    found = stage_rows(ways, pl.ds(256, 16))
-    found = bias_rows(bias_sum(found))
+    ways, sides, pairs, mixed, to_ways = refs[:4], refs[4:6], refs[6:8], refs[8:10], refs[10:]
+    x, y, _ = place()
+    for i, out in enumerate(mixed):
+        to = lax.bitwise_xor(x, i)
+        first = stage_rows(ways, pl.ds(pl.multiple_of(to * 128, 128), 128)).astype(BF16)
+        out[:, :256] = stage_rows(pairs, pl.ds(pl.multiple_of(to * 256, 256), 256)).astype(BF16)
+        out[:128, 256:] = first[:, :256]
+        out[128:, 256:384] = first[:, 256:]
+        out[128:, 384:] = jnp.zeros((128, 128), BF16)
+    found = folded(bias_rows(bias_sum(unfolded(stage_rows(sides, pl.ds(512, 32))))))
+    for d, out in enumerate(to_ways):
+        out[:128, :] = stage_rows(sides, pl.ds(pl.multiple_of(lax.rem(y + d, NY) * 128, 128), 128)).astype(BF16)
+        out[128:, :] = found
+
+
+def third_kernel(*refs):
+    mixed, ways, to_pairs, to_ways = refs[:2], refs[2:6], refs[6:8], refs[8:]
+    _, y, z = place()
+    found = bias_rows(bias_sum(unfolded(stage_rows(ways, pl.ds(128, 32)))))
     for i, out in enumerate(to_pairs):
-        start = lax.bitwise_xor(x, i // 2) * 128 + lax.bitwise_xor(z, i % 2) * 16
+        start = lax.bitwise_xor(lax.rem(z, 2), i) * 16
         for k in range(4):
             rows = pl.ds(pl.multiple_of(start + k * 32, 16), 16)
-            out[k * 16 : (k + 1) * 16, :] = stage_rows(ways, rows).astype(BF16)
-        out[64:80, :] = found
+            late = pl.ds(pl.multiple_of(start + k * 32 + 128, 16), 16)
+            here = slice(k * 16, (k + 1) * 16)
+            out[here, :256] = stage_rows(mixed, rows, slice(256, 512)).astype(BF16)
+            out[here, 256:384] = stage_rows(mixed, late, slice(256, 384)).astype(BF16)
+            out[here, 384:] = stage_rows(ways, rows).astype(BF16)
+        out[64:, :512] = found
+        out[64:, 512:] = jnp.zeros((16, 256), BF16)
     for d, out in enumerate(to_ways):
         rows = pl.ds(pl.multiple_of(lax.rem(y + d, NY) * 64, 64), 64)
-        out[...] = stage_rows(pairs, rows).astype(BF16)
-
-
-def third_kernel(*refs):
-    pairs, ways, outs = refs[:4], refs[4:8], refs[8:]
-    z = lax.rem(lax.axis_index("lat"), NZ) // 2
-    found = stage_rows(pairs, pl.ds(64, 16))
-    found = bias_rows(bias_sum(found))
+        out[...] = stage_rows(mixed, rows, slice(0, 256)).astype(BF16)
+
+
+def fourth_kernel(*refs):
+    pairs, ways, outs = refs[:2], refs[2:6], refs[6:]
+    z = place()[2] // 2
+    found = bias_rows(bias_sum(stage_rows(pairs, pl.ds(64, 16), slice(0, 512))))
     for e, out in enumerate(outs):
         rows = pl.ds(pl.multiple_of(lax.rem(z + e, 4) * 16, 16), 16)
-        out[:16, :512] = stage_rows(pairs, rows).astype(BF16)
-        out[:16, 512:] = stage_rows(ways, rows).astype(BF16)
+        out[:16, :768] = stage_rows(pairs, rows).astype(BF16)
+        out[:16, 768:] = stage_rows(ways, rows).astype(BF16)
         out[16:, :512] = found
         out[16:, 512:] = jnp.zeros_like(found)
 
@@ -340,6 +374,15 @@
             bias[head : head + 1, c * 48 : stop] = found[head * 16 + c : head * 16 + c + 1, : stop - c * 48]
 
 
+def load_kernel(*refs):
+    sources, targets, arrived = refs[:3], refs[3:6], refs[6]
+    copies = [pltpu.make_async_copy(a, b, arrived.at[i]) for i, (a, b) in enumerate(zip(sources, targets))]
+    for copy in copies:
+        copy.start()
+    for copy in copies:
+        copy.wait()
+
+
 def label_rows(labels, first):
     row = lax.broadcasted_iota(jnp.int32, (8, 72), 0)
     col = lax.broadcasted_iota(jnp.int32, (8, 72), 1)
@@ -354,15 +397,25 @@
     back = functools.partial(sent, axis="lat", to=lambda i: (i - 1) % 64)
     onward = functools.partial(sent, axis="lat", to=lambda i: (i + 1) % 64)
 
+    inputs = tokens.transpose(0, 2, 1, 3), output_grad.transpose(0, 2, 1, 3), region_labels
+    loaded = pl.pallas_call(
+        load_kernel,
+        out_shape=[shape(x.shape, x.dtype) for x in inputs],
+        in_specs=[pl.BlockSpec(memory_space=pl.ANY)] * 3,
+        out_specs=[pl.BlockSpec(memory_space=pltpu.VMEM)] * 3,
+        scratch_shapes=[pltpu.SemaphoreType.DMA((3,))],
+        compiler_params=pltpu.CompilerParams(vmem_limit_bytes=8 * 2**20),
+    )(*inputs)
+
     def message(r):
         rows = slice(3 - 3 * r, 6 - 3 * r)
-        t, g = (x[rows].transpose(0, 2, 1, 3).reshape(72, D) for x in (tokens, output_grad))
-        marks = label_rows(region_labels[rows], 72 * r)
-        return jnp.concatenate([t, marks, g, jnp.zeros((8, D), BF16)])
+        t, g = (x[rows].reshape(72, D) for x in loaded[:2])
+        return jnp.concatenate([t, label_rows(loaded[2][rows], 72 * r), g])
 
     high = message(0)
     low = back(message(1))
     far_high = across(high)
+
     table = jnp.pad(bias_table.T, ((0, 0), (0, 9)))
     bias, high_rows, low_rows = call(
         bias_kernel,
@@ -371,11 +424,9 @@
         10**8,
         4 * 10**6,
     )(table, bias_index, jnp.asarray(window_order(), BF16))
-    high, bias, high_rows, low_rows = lax.optimization_barrier((high, bias, high_rows, low_rows))
-    near_high = core(high)
+    low, far_high, bias, high_rows, low_rows = lax.optimization_barrier((low, far_high, bias, high_rows, low_rows))
     far_low = across(low)
-    far_high, low = lax.optimization_barrier((far_high, low))
-    highs = (high, near_high, far_high, core(far_high))
+    near = (high, low, core(high), core(low))
 
     early = call(
         early_kernel,
@@ -384,13 +435,16 @@
         10**9,
         5 * 10**6,
         8,
-    )(*highs, qkv_weight, out_weight)
-    far_low, early = lax.optimization_barrier((far_low, early))
-    lows = (low, core(low), far_low, core(far_low))
+    )(*near, qkv_weight, out_weight)
+    far_high, far_low, early = lax.optimization_barrier((far_high, far_low, early))
+    far = (far_high, far_low, core(far_high), core(far_low))
 
     grads, *blocks = call(
         band_kernel,
-        (shape((ALL, 3 * WIDTH), BF16),) + (shape((272, 512), BF16),) * 4 + (shape((256, 512), BF16),) * 4,
+        (shape((ALL, 3 * WIDTH), BF16),)
+        + (shape((256, 384), BF16),) * 4
+        + (shape((544, 384), BF16),) * 2
+        + (shape((512, 256), BF16),) * 2,
         [
             pltpu.VMEM((ALL, D), BF16),
             pltpu.VMEM((ALL, D), BF16),
@@ -406,33 +460,35 @@
         3 * 10**9,
         10**7,
         24,
-    )(*highs, *lows, qkv_weight, out_weight, bias, early, high_rows, low_rows)
+    )(*near, *far, qkv_weight, out_weight, bias, early, high_rows, low_rows)
 
     def by_y(parts):
         return [parts[0]] + [sent(parts[d], "lat", moved(0, d, 0)) for d in range(1, 4)]
 
-    def by_pair(parts):
-        return [parts[0]] + [sent(parts[d], "lat", paired(d // 2, d % 2)) for d in range(1, 4)]
-
-    ways, pairs = by_y(blocks[:4]), by_pair(blocks[4:])
-
-    grads, near_pair = lax.optimization_barrier((grads, pairs[1]))
-    pairs[1] = near_pair
+    def swapped(parts, dx, dz):
+        return [parts[0], sent(parts[1], "lat", paired(dx, dz))]
+
+    ways, sides, pairs = by_y(blocks[:4]), swapped(blocks[4:6], 1, 0), swapped(blocks[6:], 0, 1)
+
     near, far, given = call(
         input_kernel, (shape((WT, D), BF16), shape((WT, D), BF16), shape((2 * WT, D), BF16)), (), 10**9, 5 * 10**6
     )(grads, qkv_weight)
     given = core(given)
     far = (far.astype(F32) + given[WT:].astype(F32)).astype(BF16)
+    ways, sides, pairs, far = lax.optimization_barrier((ways, sides, pairs, far))
     parts = call(
-        second_kernel, (shape((80, 512), BF16),) * 4 + (shape((64, 512), BF16),) * 4, (), 10**6, 3 * 10**6, 8
-    )(*ways, *pairs)
-    far, parts = lax.optimization_barrier((far, parts))
+        second_kernel, (shape((256, 512), BF16),) * 2 + (shape((160, 384), BF16),) * 4, (), 10**6, 3 * 10**6, 8
+    )(*ways, *sides, *pairs)
     more = across(far)
-    pairs, ways = by_pair(parts[:4]), by_y(parts[4:])
-    pairs, ways, more = lax.optimization_barrier((pairs, ways, more))
-    parts = call(third_kernel, (shape((32, D), BF16),) * 4, (), 10**6, 10**6, 8)(*pairs, *ways)
+    mixed, ways = swapped(parts[:2], 1, 0), by_y(parts[2:])
+    parts = call(
+        third_kernel, (shape((80, 768), BF16),) * 2 + (shape((64, 256), BF16),) * 4, (), 10**6, 10**6, 8
+    )(*mixed, *ways)
+    pairs, ways = swapped(parts[:2], 0, 1), by_y(parts[2:])
+    near = near.astype(F32) + given[:WT].astype(F32) + more.astype(F32)
+    pairs, ways, near = lax.optimization_barrier((pairs, ways, near))
+    parts = call(fourth_kernel, (shape((32, D), BF16),) * 4, (), 10**6, 10**6, 8)(*pairs, *ways)
     got = [parts[0]] + [sent(parts[e], "lat", moved(0, 0, 2 * e)) for e in range(1, 4)]
-    near = near.astype(F32) + given[:WT].astype(F32) + more.astype(F32)
     low = onward(near[72:].astype(BF16)).astype(F32)
     input_grad = jnp.concatenate([low, near[:72]]).reshape(6, 12, 2, D).transpose(0, 2, 1, 3)
     got, input_grad = lax.optimization_barrier((got, input_grad))

time: 104 us -> 101 us (0.971)
  waiting for transfers between devices: 43.5 us -> 39.6 us
  starting transfers between devices: 39.6 us -> 41.3 us
    ppermute x25 -> x26, waiting for transfers between devices: 43.5 us -> 39.6 us  [sent(): return lax.ppermute(x, axis, [(i, to(i)) for i in range(size)])]
    unnamed x10 -> x16, local copies, waits for them, and re-layouts: 0.02 us -> 2.63 us
    transpose x2 -> x0, local copies, waits for them, and re-layouts: 2.38 us -> none  [message(): x[rows].transpose(0, 2, 1, 3).reshape(72, D)]
    ppermute x25 -> x26, starting transfers between devices: 39.6 us -> 41.3 us  [sent(): return lax.ppermute(x, axis, [(i, to(i)) for i in range(size)])]
    pallas_call x3 -> x5, Pallas kernels: 8 us -> 8.42 us  [the longest x1 7.49 us: shards(): call(band_kernel, (shape((ALL, 3 * WIDTH), BF16),) + (shape((256, 384), B...]
  transfers between devices with their start and end apart: 25 -> 26, of which waited for: 12 -> 17; matrix products, arithmetic and copies ran while one was open for 1% -> 2% of each run, Pallas kernels for 3% -> 4%
where the time goes in v3:
time: 101 us
  starting transfers between devices  41.3 us (41%)
  waiting for transfers between devices  39.6 us (39%)
  Pallas kernels  13.4 us (13%)
  local copies, waits for them, and re-layouts  5 us (5%)
    ppermute x26, starting transfers between devices, sent(): return lax.ppermute(x, axis, [(i, to(i)) for i in range(size)])  41.3 us
    ppermute x26, waiting for transfers between devices, sent(): return lax.ppermute(x, axis, [(i, to(i)) for i in range(size)])  39.6 us
    pallas_call x1, Pallas kernels, shards(): call(band_kernel, (shape((ALL, 3 * WIDTH), BF16),) + (shape((256, 384), B...  7.49 us
    unnamed x16, local copies, waits for them, and re-layouts  2.63 us
    pallas_call x1, Pallas kernels, shards(): call(bias_kernel, (shape((HEADS, WT, WT), F32), shape((88, 16, 256), BF16...  2.14 us
  transfers between devices with their start and end apart: 26, of which 17 were waited for; matrix products, arithmetic and copies ran while one was open for 2% of the time, Pallas kernels for 4%

profile of v3, /device:TPU:2, one launch (start us, length us, event | category | flops | bytes accessed | tf_op | source)
XLA Modules:
  0.0 100.7 jit_solution(5320956646412573509)
XLA Ops:
  4.8 8.4 %collective-permute-start = (bf16[152,1024]{1,0:T(8,128)(2,1)S(1)}, bf16[152,1024]{1,0:T(8,128)(2,1)S(1)}, u32[]{:S(2)}, u32[]{:S(2)}) collective-permute-start(bf16[152,1024]{1,0:T(8,128)(2,1)S(1)} %pad_maximum_fusion.2), channel_id=1, source_target_pairs={{0,252},{4,0},{8,4},{12,8},{16,12},{20,16},{24,20},{28,24},{32,28}... | collective-permute-start | bytes 933896 | tf_op jit(solution)/shard_map/ppermute | solution.py:31
  13.3 2.5 %collective-permute-start.1 = (bf16[152,1024]{1,0:T(8,128)(2,1)S(1)}, bf16[152,1024]{1,0:T(8,128)(2,1)S(1)}, u32[]{:S(2)}, u32[]{:S(2)}) collective-permute-start(bf16[152,1024]{1,0:T(8,128)(2,1)S(1)} %pad_maximum_fusion.1.m0.refs_0_), channel_id=1, source_target_pairs={{0,2},{1,3},{2,0},{3,1},{4,6},{5,7},{6,4},{7,5},{8,10},{9,11},{10,... | collective-permute-start | bytes 933896 | tf_op jit(solution)/shard_map/ppermute | solution.py:31
  15.8 2.1 %shard_map.112 = (f32[4,144,144]{2,1,0:T(8,128)S(1)}, bf16[88,16,256]{2,1,0:T(8,128)(2,1)S(1)}, bf16[88,48,256]{2,1,0:T(8,128)(2,1)S(1)}) custom-call(f32[4,768]{1,0:T(4,128)S(1)} %pad.22.table, s32[144,144]{1,0:T(8,128)S(1)} %copy-done.5, bf16[144,144]{1,0:T(8,128)(2,1)S(1)} %copy-done.6), custom_call_target="tpu_custom_call" | custom-call | flops 100000000 | bytes 4000000 | tf_op jit(solution)/shard_map/pallas_call | solution.py:420
  18.0 1.8 %collective-permute-done.m1.refs_1_ = bf16[152,1024]{1,0:T(8,128)(2,1)S(1)} collective-permute-done((bf16[152,1024]{1,0:T(8,128)(2,1)S(1)}, bf16[152,1024]{1,0:T(8,128)(2,1)S(1)}, u32[]{:S(2)}, u32[]{:S(2)}) %collective-permute-start) | collective-permute-done | bytes 311328 | tf_op jit(solution)/shard_map/ppermute | solution.py:31
  19.8 3.9 %collective-permute-done.1.refs_4_ = bf16[152,1024]{1,0:T(8,128)(2,1)S(1)} collective-permute-done((bf16[152,1024]{1,0:T(8,128)(2,1)S(1)}, bf16[152,1024]{1,0:T(8,128)(2,1)S(1)}, u32[]{:S(2)}, u32[]{:S(2)}) %collective-permute-start.1) | collective-permute-done | bytes 311328 | tf_op jit(solution)/shard_map/ppermute | solution.py:31
  23.7 2.4 %collective-permute-start.4 = (bf16[152,1024]{1,0:T(8,128)(2,1)S(1)}, bf16[152,1024]{1,0:T(8,128)(2,1)S(1)}, u32[]{:S(2)}, u32[]{:S(2)}) collective-permute-start(bf16[152,1024]{1,0:T(8,128)(2,1)S(1)} %collective-permute-done.m1.refs_1_), channel_id=1, source_target_pairs={{0,2},{1,3},{2,0},{3,1},{4,6},{5,7},{6,4},{7,5},{8,10},{9,11},{10,... | collective-permute-start | bytes 933896 | tf_op jit(solution)/shard_map/ppermute | solution.py:31
  27.0 8.0 %collective-permute-done.4.refs_5_ = bf16[152,1024]{1,0:T(8,128)(2,1)S(1)} collective-permute-done((bf16[152,1024]{1,0:T(8,128)(2,1)S(1)}, bf16[152,1024]{1,0:T(8,128)(2,1)S(1)}, u32[]{:S(2)}, u32[]{:S(2)}) %collective-permute-start.4) | collective-permute-done | bytes 311328 | tf_op jit(solution)/shard_map/ppermute | solution.py:31
  37.0 7.5 %shard_map.114 = (bf16[640,768]{1,0:T(8,128)(2,1)S(1)}, bf16[256,384]{1,0:T(8,128)(2,1)S(1)}, bf16[256,384]{1,0:T(8,128)(2,1)S(1)}, bf16[256,384]{1,0:T(8,128)(2...) custom-call(bf16[152,1024]{1,0:T(8,128)(2,1)S(1)} %pad_maximum_fusio, ...), custom_call_target="tpu_custom_call" | custom-call | flops 3000000000 | bytes 10000000 | tf_op jit(solution)/shard_map/pallas_call | solution.py:442
  46.0 1.5 %collective-permute-start.10 = (bf16[544,384]{1,0:T(8,128)(2,1)S(1)}, bf16[544,384]{1,0:T(8,128)(2,1)S(1)}, u32[]{:S(2)}, u32[]{:S(2)}) collective-permute-start(bf16[544,384]{1,0:T(8,128)(2,1)S(1)} %get-tuple-element.89), channel_id=1, source_target_pairs={{0,128},{4,132},{8,136},{12,140},{16,144},{20,148},{24,152},{28,15... | collective-permute-start | bytes 1253384 | tf_op jit(solution)/shard_map/ppermute | solution.py:31
  47.5 1.3 %collective-permute-start.8 = (bf16[256,384]{1,0:T(8,128)(2,1)S(1)}, bf16[256,384]{1,0:T(8,128)(2,1)S(1)}, u32[]{:S(2)}, u32[]{:S(2)}) collective-permute-start(bf16[256,384]{1,0:T(8,128)(2,1)S(1)} %get-tuple-element.86), channel_id=1, source_target_pairs={{0,64},{4,68},{8,72},{12,76},{16,80},{20,84},{24,88},{28,92},{32,9... | collective-permute-start | bytes 589832 | tf_op jit(solution)/shard_map/ppermute | solution.py:31
  48.8 2.0 %collective-permute-start.9 = (bf16[256,384]{1,0:T(8,128)(2,1)S(1)}, bf16[256,384]{1,0:T(8,128)(2,1)S(1)}, u32[]{:S(2)}, u32[]{:S(2)}) collective-permute-start(bf16[256,384]{1,0:T(8,128)(2,1)S(1)} %get-tuple-element.87), channel_id=1, source_target_pairs={{0,96},{4,100},{8,104},{12,108},{16,112},{20,116},{24,120},{28,124... | collective-permute-start | bytes 589832 | tf_op jit(solution)/shard_map/ppermute | solution.py:31
  50.8 9.0 %collective-permute-done.7.refs_1_ = bf16[256,384]{1,0:T(8,128)(2,1)S(1)} collective-permute-done((bf16[256,384]{1,0:T(8,128)(2,1)S(1)}, bf16[256,384]{1,0:T(8,128)(2,1)S(1)}, u32[]{:S(2)}, u32[]{:S(2)}) %collective-permute-start.7) | collective-permute-done | bytes 196640 | tf_op jit(solution)/shard_map/ppermute | solution.py:31
  60.4 2.1 %collective-permute-start.21 = (bf16[144,1024]{1,0:T(8,128)(2,1)S(1)}, bf16[144,1024]{1,0:T(8,128)(2,1)S(1)}, u32[]{:S(2)}, u32[]{:S(2)}) collective-permute-start(bf16[144,1024]{1,0:T(8,128)(2,1)S(1)} %add_convert_fusion), channel_id=1, source_target_pairs={{0,2},{1,3},{2,0},{3,1},{4,6},{5,7},{6,4},{7,5},{8,10},{9,11},{10,... | collective-permute-start | bytes 884744 | tf_op jit(solution)/shard_map/ppermute | solution.py:31
  63.0 1.5 %collective-permute-start.13 = (bf16[256,512]{1,0:T(8,128)(2,1)S(1)}, bf16[256,512]{1,0:T(8,128)(2,1)S(1)}, u32[]{:S(2)}, u32[]{:S(2)}) collective-permute-start(bf16[256,512]{1,0:T(8,128)(2,1)S(1)} %get-tuple-element.104), channel_id=1, source_target_pairs={{0,128},{4,132},{8,136},{12,140},{16,144},{20,148},{24,152},{28,15... | collective-permute-start | bytes 786440 | tf_op jit(solution)/shard_map/ppermute | solution.py:31
  64.7 3.6 %collective-permute-start.15 = (bf16[160,384]{1,0:T(8,128)(2,1)S(1)}, bf16[160,384]{1,0:T(8,128)(2,1)S(1)}, u32[]{:S(2)}, u32[]{:S(2)}) collective-permute-start(bf16[160,384]{1,0:T(8,128)(2,1)S(1)} %get-tuple-element.107), channel_id=1, source_target_pairs={{0,64},{4,68},{8,72},{12,76},{16,80},{20,84},{24,88},{28,92},{32,9... | collective-permute-start | bytes 368648 | tf_op jit(solution)/shard_map/ppermute | solution.py:31
  68.3 3.6 %collective-permute-done.14.refs_3_ = bf16[160,384]{1,0:T(8,128)(2,1)S(1)} collective-permute-done((bf16[160,384]{1,0:T(8,128)(2,1)S(1)}, bf16[160,384]{1,0:T(8,128)(2,1)S(1)}, u32[]{:S(2)}, u32[]{:S(2)}) %collective-permute-start.14) | collective-permute-done | bytes 122912 | tf_op jit(solution)/shard_map/ppermute | solution.py:31
  71.9 1.4 %collective-permute-done.15.refs_4_ = bf16[160,384]{1,0:T(8,128)(2,1)S(1)} collective-permute-done((bf16[160,384]{1,0:T(8,128)(2,1)S(1)}, bf16[160,384]{1,0:T(8,128)(2,1)S(1)}, u32[]{:S(2)}, u32[]{:S(2)}) %collective-permute-start.15) | collective-permute-done | bytes 122912 | tf_op jit(solution)/shard_map/ppermute | solution.py:31
  73.4 2.1 %collective-permute-done.13.refs_1_ = bf16[256,512]{1,0:T(8,128)(2,1)S(1)} collective-permute-done((bf16[256,512]{1,0:T(8,128)(2,1)S(1)}, bf16[256,512]{1,0:T(8,128)(2,1)S(1)}, u32[]{:S(2)}, u32[]{:S(2)}) %collective-permute-start.13) | collective-permute-done | bytes 262176 | tf_op jit(solution)/shard_map/ppermute | solution.py:31
  76.9 3.3 %collective-permute-start.19 = (bf16[64,256]{1,0:T(8,128)(2,1)S(1)}, bf16[64,256]{1,0:T(8,128)(2,1)S(1)}, u32[]{:S(2)}, u32[]{:S(2)}) collective-permute-start(bf16[64,256]{1,0:T(8,128)(2,1)S(1)} %get-tuple-element.113), channel_id=1, source_target_pairs={{0,64},{4,68},{8,72},{12,76},{16,80},{20,84},{24,88},{28,92},{32,9... | collective-permute-start | bytes 98312 | tf_op jit(solution)/shard_map/ppermute | solution.py:31
  80.2 1.7 %collective-permute-start.17 = (bf16[80,768]{1,0:T(8,128)(2,1)S(1)}, bf16[80,768]{1,0:T(8,128)(2,1)S(1)}, u32[]{:S(2)}, u32[]{:S(2)}) collective-permute-start(bf16[80,768]{1,0:T(8,128)(2,1)S(1)} %get-tuple-element.110), channel_id=1, source_target_pairs={{0,4},{4,0},{8,12},{12,8},{16,20},{20,16},{24,28},{28,24},{32,36},... | collective-permute-start | bytes 368648 | tf_op jit(solution)/shard_map/ppermute | solution.py:31
  82.4 1.7 %collective-permute-done.20.refs_5_ = bf16[64,256]{1,0:T(8,128)(2,1)S(1)} collective-permute-done((bf16[64,256]{1,0:T(8,128)(2,1)S(1)}, bf16[64,256]{1,0:T(8,128)(2,1)S(1)}, u32[]{:S(2)}, u32[]{:S(2)}) %collective-permute-start.20) | collective-permute-done | bytes 32800 | tf_op jit(solution)/shard_map/ppermute | solution.py:31
  85.1 1.8 %collective-permute-start.25 = (bf16[72,1024]{1,0:T(8,128)(2,1)S(1)}, bf16[72,1024]{1,0:T(8,128)(2,1)S(1)}, u32[]{:S(2)}, u32[]{:S(2)}) collective-permute-start(bf16[72,1024]{1,0:T(8,128)(2,1)S(1)} %slice.49), channel_id=1, source_target_pairs={{0,4},{4,8},{8,12},{12,16},{16,20},{20,24},{24,28},{28,32},{32,36}... | collective-permute-start | bytes 442376 | tf_op jit(solution)/shard_map/ppermute | solution.py:31
  87.1 7.1 %collective-permute-start.23 = (bf16[32,1024]{1,0:T(8,128)(2,1)S(1)}, bf16[32,1024]{1,0:T(8,128)(2,1)S(1)}, u32[]{:S(2)}, u32[]{:S(2)}) collective-permute-start(bf16[32,1024]{1,0:T(8,128)(2,1)S(1)} %get-tuple-element.125), channel_id=1, source_target_pairs={{0,16},{4,20},{8,24},{12,28},{16,0},{20,4},{24,8},{28,12},{32,48},... | collective-permute-start | bytes 196616 | tf_op jit(solution)/shard_map/ppermute | solution.py:31
  97.3 2.5 %collective-permute-done.24.d = bf16[32,1024]{1,0:T(8,128)(2,1)S(1)} collective-permute-done((bf16[32,1024]{1,0:T(8,128)(2,1)S(1)}, bf16[32,1024]{1,0:T(8,128)(2,1)S(1)}, u32[]{:S(2)}, u32[]{:S(2)}) %collective-permute-start.24) | collective-permute-done | bytes 65568 | tf_op jit(solution)/shard_map/ppermute | solution.py:31
  (80 shorter events, 17.1 us)
Async XLA Ops:
  4.8 15.0 %collective-permute-start = (bf16[152,1024]{1,0:T(8,128)(2,1)S(1)}, bf16[152,1024]{1,0:T(8,128)(2,1)S(1)}, u32[]{:S(2)}, u32[]{:S(2)}) collective-permute-start(bf16[152,1024]{1,0:T(8,128)(2,1)S(1)} %pad_maximum_fusion.2), channel_id=1, source_target_pairs={{0,252},{4,0},{8,4},{12,8},{16,12},{20,16},{24,20},{28,24},{32,28}... | collective-permute-start | bytes 933896 | tf_op jit(solution)/shard_map/ppermute | solution.py:31
  13.3 10.4 %collective-permute-start.1 = (bf16[152,1024]{1,0:T(8,128)(2,1)S(1)}, bf16[152,1024]{1,0:T(8,128)(2,1)S(1)}, u32[]{:S(2)}, u32[]{:S(2)}) collective-permute-start(bf16[152,1024]{1,0:T(8,128)(2,1)S(1)} %pad_maximum_fusion.1.m0.refs_0_), channel_id=1, source_target_pairs={{0,2},{1,3},{2,0},{3,1},{4,6},{5,7},{6,4},{7,5},{8,10},{9,11},{10,... | collective-permute-start | bytes 933896 | tf_op jit(solution)/shard_map/ppermute | solution.py:31
  15.8 10.3 %collective-permute-start.2 = (bf16[152,1024]{1,0:T(8,128)(2,1)S(1)}, bf16[152,1024]{1,0:T(8,128)(2,1)S(1)}, u32[]{:S(2)}, u32[]{:S(2)}) collective-permute-start(bf16[152,1024]{1,0:T(8,128)(2,1)S(1)} %pad_maximum_fusion.1.m0.refs_0_), channel_id=1, source_target_pairs={{0,1},{1,0},{2,3},{3,2},{4,5},{5,4},{6,7},{7,6},{8,9},{9,8},{10,11... | collective-permute-start | bytes 933896 | tf_op jit(solution)/shard_map/ppermute | solution.py:31
  23.7 2.4 %collective-permute-start.3 = (bf16[152,1024]{1,0:T(8,128)(2,1)S(1)}, bf16[152,1024]{1,0:T(8,128)(2,1)S(1)}, u32[]{:S(2)}, u32[]{:S(2)}) collective-permute-start(bf16[152,1024]{1,0:T(8,128)(2,1)S(1)} %collective-permute-done.m1.refs_1_), channel_id=1, source_target_pairs={{0,1},{1,0},{2,3},{3,2},{4,5},{5,4},{6,7},{7,6},{8,9},{9,8},{10,11... | collective-permute-start | bytes 933896 | tf_op jit(solution)/shard_map/ppermute | solution.py:31
  23.7 11.3 %collective-permute-start.4 = (bf16[152,1024]{1,0:T(8,128)(2,1)S(1)}, bf16[152,1024]{1,0:T(8,128)(2,1)S(1)}, u32[]{:S(2)}, u32[]{:S(2)}) collective-permute-start(bf16[152,1024]{1,0:T(8,128)(2,1)S(1)} %collective-permute-done.m1.refs_1_), channel_id=1, source_target_pairs={{0,2},{1,3},{2,0},{3,1},{4,6},{5,7},{6,4},{7,5},{8,10},{9,11},{10,... | collective-permute-start | bytes 933896 | tf_op jit(solution)/shard_map/ppermute | solution.py:31
  45.7 3.0 %collective-permute-start.12 = (bf16[288,1024]{1,0:T(8,128)(2,1)S(1)}, bf16[288,1024]{1,0:T(8,128)(2,1)S(1)}, u32[]{:S(2)}, u32[]{:S(2)}) collective-permute-start(bf16[288,1024]{1,0:T(8,128)(2,1)S(1)} %get-tuple-element.94), channel_id=1, source_target_pairs={{0,1},{1,0},{2,3},{3,2},{4,5},{5,4},{6,7},{7,6},{8,9},{9,8},{10,11... | collective-permute-start | bytes 1769480 | tf_op jit(solution)/shard_map/ppermute | solution.py:31
  46.0 14.4 %collective-permute-start.10 = (bf16[544,384]{1,0:T(8,128)(2,1)S(1)}, bf16[544,384]{1,0:T(8,128)(2,1)S(1)}, u32[]{:S(2)}, u32[]{:S(2)}) collective-permute-start(bf16[544,384]{1,0:T(8,128)(2,1)S(1)} %get-tuple-element.89), channel_id=1, source_target_pairs={{0,128},{4,132},{8,136},{12,140},{16,144},{20,148},{24,152},{28,15... | collective-permute-start | bytes 1253384 | tf_op jit(solution)/shard_map/ppermute | solution.py:31
  47.5 12.9 %collective-permute-start.11 = (bf16[512,256]{1,0:T(8,128)(2,1)S(1)}, bf16[512,256]{1,0:T(8,128)(2,1)S(1)}, u32[]{:S(2)}, u32[]{:S(2)}) collective-permute-start(bf16[512,256]{1,0:T(8,128)(2,1)S(1)} %get-tuple-element.91), channel_id=1, source_target_pairs={{0,4},{4,0},{8,12},{12,8},{16,20},{20,16},{24,28},{28,24},{32,36},... | collective-permute-start | bytes 786440 | tf_op jit(solution)/shard_map/ppermute | solution.py:31
  47.5 12.3 %collective-permute-start.7 = (bf16[256,384]{1,0:T(8,128)(2,1)S(1)}, bf16[256,384]{1,0:T(8,128)(2,1)S(1)}, u32[]{:S(2)}, u32[]{:S(2)}) collective-permute-start(bf16[256,384]{1,0:T(8,128)(2,1)S(1)} %get-tuple-element.85), channel_id=1, source_target_pairs={{0,32},{4,36},{8,40},{12,44},{16,48},{20,52},{24,56},{28,60},{32,6... | collective-permute-start | bytes 589832 | tf_op jit(solution)/shard_map/ppermute | solution.py:31
  47.5 12.3 %collective-permute-start.8 = (bf16[256,384]{1,0:T(8,128)(2,1)S(1)}, bf16[256,384]{1,0:T(8,128)(2,1)S(1)}, u32[]{:S(2)}, u32[]{:S(2)}) collective-permute-start(bf16[256,384]{1,0:T(8,128)(2,1)S(1)} %get-tuple-element.86), channel_id=1, source_target_pairs={{0,64},{4,68},{8,72},{12,76},{16,80},{20,84},{24,88},{28,92},{32,9... | collective-permute-start | bytes 589832 | tf_op jit(solution)/shard_map/ppermute | solution.py:31
  48.8 11.6 %collective-permute-start.9 = (bf16[256,384]{1,0:T(8,128)(2,1)S(1)}, bf16[256,384]{1,0:T(8,128)(2,1)S(1)}, u32[]{:S(2)}, u32[]{:S(2)}) collective-permute-start(bf16[256,384]{1,0:T(8,128)(2,1)S(1)} %get-tuple-element.87), channel_id=1, source_target_pairs={{0,96},{4,100},{8,104},{12,108},{16,112},{20,116},{24,120},{28,124... | collective-permute-start | bytes 589832 | tf_op jit(solution)/shard_map/ppermute | solution.py:31
  60.4 21.5 %collective-permute-start.21 = (bf16[144,1024]{1,0:T(8,128)(2,1)S(1)}, bf16[144,1024]{1,0:T(8,128)(2,1)S(1)}, u32[]{:S(2)}, u32[]{:S(2)}) collective-permute-start(bf16[144,1024]{1,0:T(8,128)(2,1)S(1)} %add_convert_fusion), channel_id=1, source_target_pairs={{0,2},{1,3},{2,0},{3,1},{4,6},{5,7},{6,4},{7,5},{8,10},{9,11},{10,... | collective-permute-start | bytes 884744 | tf_op jit(solution)/shard_map/ppermute | solution.py:31
  63.0 12.6 %collective-permute-start.13 = (bf16[256,512]{1,0:T(8,128)(2,1)S(1)}, bf16[256,512]{1,0:T(8,128)(2,1)S(1)}, u32[]{:S(2)}, u32[]{:S(2)}) collective-permute-start(bf16[256,512]{1,0:T(8,128)(2,1)S(1)} %get-tuple-element.104), channel_id=1, source_target_pairs={{0,128},{4,132},{8,136},{12,140},{16,144},{20,148},{24,152},{28,15... | collective-permute-start | bytes 786440 | tf_op jit(solution)/shard_map/ppermute | solution.py:31
  64.5 7.4 %collective-permute-start.14 = (bf16[160,384]{1,0:T(8,128)(2,1)S(1)}, bf16[160,384]{1,0:T(8,128)(2,1)S(1)}, u32[]{:S(2)}, u32[]{:S(2)}) collective-permute-start(bf16[160,384]{1,0:T(8,128)(2,1)S(1)} %get-tuple-element.106), channel_id=1, source_target_pairs={{0,32},{4,36},{8,40},{12,44},{16,48},{20,52},{24,56},{28,60},{32,6... | collective-permute-start | bytes 368648 | tf_op jit(solution)/shard_map/ppermute | solution.py:31
  64.7 8.5 %collective-permute-start.15 = (bf16[160,384]{1,0:T(8,128)(2,1)S(1)}, bf16[160,384]{1,0:T(8,128)(2,1)S(1)}, u32[]{:S(2)}, u32[]{:S(2)}) collective-permute-start(bf16[160,384]{1,0:T(8,128)(2,1)S(1)} %get-tuple-element.107), channel_id=1, source_target_pairs={{0,64},{4,68},{8,72},{12,76},{16,80},{20,84},{24,88},{28,92},{32,9... | collective-permute-start | bytes 368648 | tf_op jit(solution)/shard_map/ppermute | solution.py:31
  68.3 5.1 %collective-permute-start.16 = (bf16[160,384]{1,0:T(8,128)(2,1)S(1)}, bf16[160,384]{1,0:T(8,128)(2,1)S(1)}, u32[]{:S(2)}, u32[]{:S(2)}) collective-permute-start(bf16[160,384]{1,0:T(8,128)(2,1)S(1)} %get-tuple-element.108), channel_id=1, source_target_pairs={{0,96},{4,100},{8,104},{12,108},{16,112},{20,116},{24,120},{28,124... | collective-permute-start | bytes 368648 | tf_op jit(solution)/shard_map/ppermute | solution.py:31
  75.8 6.3 %collective-permute-start.18 = (bf16[64,256]{1,0:T(8,128)(2,1)S(1)}, bf16[64,256]{1,0:T(8,128)(2,1)S(1)}, u32[]{:S(2)}, u32[]{:S(2)}) collective-permute-start(bf16[64,256]{1,0:T(8,128)(2,1)S(1)} %get-tuple-element.112), channel_id=1, source_target_pairs={{0,32},{4,36},{8,40},{12,44},{16,48},{20,52},{24,56},{28,60},{32,6... | collective-permute-start | bytes 98312 | tf_op jit(solution)/shard_map/ppermute | solution.py:31
  76.9 5.5 %collective-permute-start.19 = (bf16[64,256]{1,0:T(8,128)(2,1)S(1)}, bf16[64,256]{1,0:T(8,128)(2,1)S(1)}, u32[]{:S(2)}, u32[]{:S(2)}) collective-permute-start(bf16[64,256]{1,0:T(8,128)(2,1)S(1)} %get-tuple-element.113), channel_id=1, source_target_pairs={{0,64},{4,68},{8,72},{12,76},{16,80},{20,84},{24,88},{28,92},{32,9... | collective-permute-start | bytes 98312 | tf_op jit(solution)/shard_map/ppermute | solution.py:31
  80.2 3.9 %collective-permute-start.20 = (bf16[64,256]{1,0:T(8,128)(2,1)S(1)}, bf16[64,256]{1,0:T(8,128)(2,1)S(1)}, u32[]{:S(2)}, u32[]{:S(2)}) collective-permute-start(bf16[64,256]{1,0:T(8,128)(2,1)S(1)} %get-tuple-element.114), channel_id=1, source_target_pairs={{0,96},{4,100},{8,104},{12,108},{16,112},{20,116},{24,120},{28,124... | collective-permute-start | bytes 98312 | tf_op jit(solution)/shard_map/ppermute | solution.py:31
  80.2 4.9 %collective-permute-start.17 = (bf16[80,768]{1,0:T(8,128)(2,1)S(1)}, bf16[80,768]{1,0:T(8,128)(2,1)S(1)}, u32[]{:S(2)}, u32[]{:S(2)}) collective-permute-start(bf16[80,768]{1,0:T(8,128)(2,1)S(1)} %get-tuple-element.110), channel_id=1, source_target_pairs={{0,4},{4,0},{8,12},{12,8},{16,20},{20,16},{24,28},{28,24},{32,36},... | collective-permute-start | bytes 368648 | tf_op jit(solution)/shard_map/ppermute | solution.py:31
  85.1 10.3 %collective-permute-start.25 = (bf16[72,1024]{1,0:T(8,128)(2,1)S(1)}, bf16[72,1024]{1,0:T(8,128)(2,1)S(1)}, u32[]{:S(2)}, u32[]{:S(2)}) collective-permute-start(bf16[72,1024]{1,0:T(8,128)(2,1)S(1)} %slice.49), channel_id=1, source_target_pairs={{0,4},{4,8},{8,12},{12,16},{16,20},{20,24},{24,28},{28,32},{32,36}... | collective-permute-start | bytes 442376 | tf_op jit(solution)/shard_map/ppermute | solution.py:31
  87.1 9.5 %collective-permute-start.22 = (bf16[32,1024]{1,0:T(8,128)(2,1)S(1)}, bf16[32,1024]{1,0:T(8,128)(2,1)S(1)}, u32[]{:S(2)}, u32[]{:S(2)}) collective-permute-start(bf16[32,1024]{1,0:T(8,128)(2,1)S(1)} %get-tuple-element.124), channel_id=1, source_target_pairs={{0,8},{4,12},{8,16},{12,20},{16,24},{20,28},{24,0},{28,4},{32,40},... | collective-permute-start | bytes 196616 | tf_op jit(solution)/shard_map/ppermute | solution.py:31
  87.1 10.2 %collective-permute-start.23 = (bf16[32,1024]{1,0:T(8,128)(2,1)S(1)}, bf16[32,1024]{1,0:T(8,128)(2,1)S(1)}, u32[]{:S(2)}, u32[]{:S(2)}) collective-permute-start(bf16[32,1024]{1,0:T(8,128)(2,1)S(1)} %get-tuple-element.125), channel_id=1, source_target_pairs={{0,16},{4,20},{8,24},{12,28},{16,0},{20,4},{24,8},{28,12},{32,48},... | collective-permute-start | bytes 196616 | tf_op jit(solution)/shard_map/ppermute | solution.py:31
  94.2 5.6 %collective-permute-start.24 = (bf16[32,1024]{1,0:T(8,128)(2,1)S(1)}, bf16[32,1024]{1,0:T(8,128)(2,1)S(1)}, u32[]{:S(2)}, u32[]{:S(2)}) collective-permute-start(bf16[32,1024]{1,0:T(8,128)(2,1)S(1)} %get-tuple-element.126), channel_id=1, source_target_pairs={{0,24},{4,28},{8,0},{12,4},{16,8},{20,12},{24,16},{28,20},{32,56},... | collective-permute-start | bytes 196616 | tf_op jit(solution)/shard_map/ppermute | solution.py:31
  (10 other events, 89.1 us)

commit v4 on v3

--- a/solution.py
+++ b/solution.py
@@ -211,19 +211,10 @@
     return jnp.where(lane < 64, x + pltpu.roll(x, 64, 1), 0.0)
 
 
-def folded(rows):
-    rest = jnp.concatenate([rows[:, 384:], jnp.zeros((16, 256), BF16)], axis=1)
-    return jnp.concatenate([rows[:, :384], rest], axis=0)
-
-
-def unfolded(rows):
-    return jnp.concatenate([rows[:16], rows[16:, :128]], axis=1)
-
-
 def band_kernel(*refs):
     pieces = refs[:8]
     weight, wo, bias, early, high_rows, low_rows, grads = refs[8:15]
-    ways, sides, pairs = refs[15:19], refs[19:21], refs[21:23]
+    ways, pairs = refs[15:19], refs[19:23]
     tall, gall, qkv, rows, wins, outs, sums, att, labels, full = refs[23:]
     own = lax.axis_index("head")
     labels[...] = jnp.zeros_like(labels)
@@ -277,16 +268,16 @@
     lat = lax.axis_index("lat")
     x, y, z = lat // (NY * NZ), lax.rem(lat // NZ, NY), lax.rem(lat, 2)
     for d, out in enumerate(ways):
+        out[256:272, :512] = found
+        out[256:272, 512:] = jnp.zeros((16, 128), BF16)
         for half in range(2):
             at = pl.ds(pl.multiple_of(half * 512 + lax.rem(y + d, NY) * 128, 128), 128)
-            out[half * 128 : (half + 1) * 128, :] = full[at, :384]
-    for i, out in enumerate(sides):
-        out[:512, :] = full[pl.ds(pl.multiple_of(lax.bitwise_xor(x, i) * 512, 512), 512), 384:768]
-        out[512:, :] = folded(found)
+            out[half * 128 : (half + 1) * 128, :] = full[at, :640]
     for i, out in enumerate(pairs):
-        for b in range(32):
-            at = pl.ds(pl.multiple_of(lax.bitwise_xor(z, i) * 16 + (b // 4) * 128 + (b % 4) * 32, 16), 16)
-            out[b * 16 : (b + 1) * 16, :] = full[at, 768:]
+        start = lax.bitwise_xor(x, i // 2) * 512 + lax.bitwise_xor(z, i % 2) * 16
+        for b in range(16):
+            at = pl.ds(pl.multiple_of(start + (b // 4) * 128 + (b % 4) * 32, 16), 16)
+            out[b * 16 : (b + 1) * 16, :] = full[at, 640:]
 
 
 def input_kernel(grads, weight, near, far, given):
@@ -313,50 +304,35 @@
     return lat // (NY * NZ), lax.rem(lat // NZ, NY), lax.rem(lat, NZ)
 
 
-def second_kernel(*refs):
-    ways, sides, pairs, mixed, to_ways = refs[:4], refs[4:6], refs[6:8], refs[8:10], refs[10:]
-    x, y, _ = place()
-    for i, out in enumerate(mixed):
-        to = lax.bitwise_xor(x, i)
-        first = stage_rows(ways, pl.ds(pl.multiple_of(to * 128, 128), 128)).astype(BF16)
-        out[:, :256] = stage_rows(pairs, pl.ds(pl.multiple_of(to * 256, 256), 256)).astype(BF16)
-        out[:128, 256:] = first[:, :256]
-        out[128:, 256:384] = first[:, 256:]
-        out[128:, 384:] = jnp.zeros((128, 128), BF16)
-    found = folded(bias_rows(bias_sum(unfolded(stage_rows(sides, pl.ds(512, 32))))))
-    for d, out in enumerate(to_ways):
-        out[:128, :] = stage_rows(sides, pl.ds(pl.multiple_of(lax.rem(y + d, NY) * 128, 128), 128)).astype(BF16)
-        out[128:, :] = found
-
-
-def third_kernel(*refs):
-    mixed, ways, to_pairs, to_ways = refs[:2], refs[2:6], refs[6:8], refs[8:]
-    _, y, z = place()
-    found = bias_rows(bias_sum(unfolded(stage_rows(ways, pl.ds(128, 32)))))
-    for i, out in enumerate(to_pairs):
-        start = lax.bitwise_xor(lax.rem(z, 2), i) * 16
+def after_ways_kernel(*refs):
+    ways, outs = refs[:4], refs[4:]
+    x, _, z = place()
+    found = bias_rows(bias_sum(stage_rows(ways, pl.ds(256, 16), slice(0, 512))))
+    for i, out in enumerate(outs):
+        start = lax.bitwise_xor(x, i // 2) * 128 + lax.bitwise_xor(lax.rem(z, 2), i % 2) * 16
         for k in range(4):
             rows = pl.ds(pl.multiple_of(start + k * 32, 16), 16)
-            late = pl.ds(pl.multiple_of(start + k * 32 + 128, 16), 16)
-            here = slice(k * 16, (k + 1) * 16)
-            out[here, :256] = stage_rows(mixed, rows, slice(256, 512)).astype(BF16)
-            out[here, 256:384] = stage_rows(mixed, late, slice(256, 384)).astype(BF16)
-            out[here, 384:] = stage_rows(ways, rows).astype(BF16)
-        out[64:, :512] = found
-        out[64:, 512:] = jnp.zeros((16, 256), BF16)
-    for d, out in enumerate(to_ways):
+            out[k * 16 : (k + 1) * 16, :] = stage_rows(ways, rows).astype(BF16)
+        out[64:80, :512] = found
+        out[64:80, 512:] = jnp.zeros((16, 128), BF16)
+
+
+def after_pairs_kernel(*refs):
+    pairs, outs = refs[:4], refs[4:]
+    y = place()[1]
+    for d, out in enumerate(outs):
         rows = pl.ds(pl.multiple_of(lax.rem(y + d, NY) * 64, 64), 64)
-        out[...] = stage_rows(mixed, rows, slice(0, 256)).astype(BF16)
-
-
-def fourth_kernel(*refs):
-    pairs, ways, outs = refs[:2], refs[2:6], refs[6:]
+        out[...] = stage_rows(pairs, rows).astype(BF16)
+
+
+def third_kernel(*refs):
+    pairs, ways, outs = refs[:4], refs[4:8], refs[8:]
     z = place()[2] // 2
     found = bias_rows(bias_sum(stage_rows(pairs, pl.ds(64, 16), slice(0, 512))))
     for e, out in enumerate(outs):
         rows = pl.ds(pl.multiple_of(lax.rem(z + e, 4) * 16, 16), 16)
-        out[:16, :768] = stage_rows(pairs, rows).astype(BF16)
-        out[:16, 768:] = stage_rows(ways, rows).astype(BF16)
+        out[:16, :640] = stage_rows(pairs, rows).astype(BF16)
+        out[:16, 640:] = stage_rows(ways, rows).astype(BF16)
         out[16:, :512] = found
         out[16:, 512:] = jnp.zeros_like(found)
 
@@ -442,9 +418,8 @@
     grads, *blocks = call(
         band_kernel,
         (shape((ALL, 3 * WIDTH), BF16),)
-        + (shape((256, 384), BF16),) * 4
-        + (shape((544, 384), BF16),) * 2
-        + (shape((512, 256), BF16),) * 2,
+        + (shape((272, 640), BF16),) * 4
+        + (shape((256, 384), BF16),) * 4,
         [
             pltpu.VMEM((ALL, D), BF16),
             pltpu.VMEM((ALL, D), BF16),
@@ -463,34 +438,32 @@
     )(*near, *far, qkv_weight, out_weight, bias, early, high_rows, low_rows)
 
     def by_y(parts):
-        return [parts[0]] + [sent(parts[d], "lat", moved(0, d, 0)) for d in range(1, 4)]
-
-    def swapped(parts, dx, dz):
-        return [parts[0], sent(parts[1], "lat", paired(dx, dz))]
-
-    ways, sides, pairs = by_y(blocks[:4]), swapped(blocks[4:6], 1, 0), swapped(blocks[6:], 0, 1)
+        far = sent(parts[2], "lat", moved(0, 2, 0))
+        return [parts[0], sent(parts[1], "lat", moved(0, 1, 0)), far, sent(parts[3], "lat", moved(0, 3, 0))]
+
+    def by_pair(parts):
+        return [parts[0]] + [sent(parts[d], "lat", paired(d // 2, d % 2)) for d in range(1, 4)]
+
+    ways, pairs = by_y(blocks[:4]), by_pair(blocks[4:])
 
     near, far, given = call(
         input_kernel, (shape((WT, D), BF16), shape((WT, D), BF16), shape((2 * WT, D), BF16)), (), 10**9, 5 * 10**6
     )(grads, qkv_weight)
     given = core(given)
     far = (far.astype(F32) + given[WT:].astype(F32)).astype(BF16)
-    ways, sides, pairs, far = lax.optimization_barrier((ways, sides, pairs, far))
-    parts = call(
-        second_kernel, (shape((256, 512), BF16),) * 2 + (shape((160, 384), BF16),) * 4, (), 10**6, 3 * 10**6, 8
-    )(*ways, *sides, *pairs)
     more = across(far)
-    mixed, ways = swapped(parts[:2], 1, 0), by_y(parts[2:])
-    parts = call(
-        third_kernel, (shape((80, 768), BF16),) * 2 + (shape((64, 256), BF16),) * 4, (), 10**6, 10**6, 8
-    )(*mixed, *ways)
-    pairs, ways = swapped(parts[:2], 0, 1), by_y(parts[2:])
+    parts = call(after_pairs_kernel, (shape((64, 384), BF16),) * 4, (), 10**6, 10**6, 8)(*pairs)
+    late = by_y(parts)
+    ways, more = lax.optimization_barrier((ways, more))
     near = near.astype(F32) + given[:WT].astype(F32) + more.astype(F32)
-    pairs, ways, near = lax.optimization_barrier((pairs, ways, near))
-    parts = call(fourth_kernel, (shape((32, D), BF16),) * 4, (), 10**6, 10**6, 8)(*pairs, *ways)
-    got = [parts[0]] + [sent(parts[e], "lat", moved(0, 0, 2 * e)) for e in range(1, 4)]
-    low = onward(near[72:].astype(BF16)).astype(F32)
-    input_grad = jnp.concatenate([low, near[:72]]).reshape(6, 12, 2, D).transpose(0, 2, 1, 3)
+    low = onward(near[72:].astype(BF16))
+    parts = call(after_ways_kernel, (shape((80, 640), BF16),) * 4, (), 10**6, 2 * 10**6, 8)(*ways)
+    pairs = by_pair(parts)
+    pairs, late, low = lax.optimization_barrier((pairs, late, low))
+    input_grad = jnp.concatenate([low.astype(F32), near[:72]]).reshape(6, 12, 2, D).transpose(0, 2, 1, 3)
+    parts = call(third_kernel, (shape((32, D), BF16),) * 4, (), 10**6, 10**6, 8)(*pairs, *late)
+    far = sent(parts[2], "lat", moved(0, 0, 4))
+    got = [parts[0], sent(parts[1], "lat", moved(0, 0, 2)), far, sent(parts[3], "lat", moved(0, 0, 6))]
     got, input_grad = lax.optimization_barrier((got, input_grad))
     qkv_grad, out_grad, bias_grad = call(
         last_kernel,

time: 101 us -> 97.4 us (0.964)
  starting transfers between devices: 41.3 us -> 39 us
  waiting for transfers between devices: 39.6 us -> 38.1 us
    ppermute x26 -> x25, starting transfers between devices: 41.3 us -> 39 us  [sent(): return lax.ppermute(x, axis, [(i, to(i)) for i in range(size)])]
    ppermute x26 -> x25, waiting for transfers between devices: 39.6 us -> 38.1 us  [sent(): return lax.ppermute(x, axis, [(i, to(i)) for i in range(size)])]
  transfers between devices with their start and end apart: 26 -> 25, of which waited for: 17 -> 14; matrix products, arithmetic and copies ran while one was open for 2% -> 2% of each run, Pallas kernels for 4% -> 3%
where the time goes in v4:
time: 97.4 us; the launch traced here: 96.7 us
  starting transfers between devices  39 us (40%)
  waiting for transfers between devices  38.1 us (39%)
  Pallas kernels  13.2 us (14%)
  local copies, waits for them, and re-layouts  5 us (5%)
    ppermute x25, starting transfers between devices, sent(): return lax.ppermute(x, axis, [(i, to(i)) for i in range(size)])  39 us
    ppermute x25, waiting for transfers between devices, sent(): return lax.ppermute(x, axis, [(i, to(i)) for i in range(size)])  38.1 us
    pallas_call x1, Pallas kernels, shards(): call(band_kernel, (shape((ALL, 3 * WIDTH), BF16),) + (shape((272, 640), B...  7.53 us
    unnamed x16, local copies, waits for them, and re-layouts  2.63 us
    pallas_call x1, Pallas kernels, shards(): call(bias_kernel, (shape((HEADS, WT, WT), F32), shape((88, 16, 256), BF16...  2.14 us
  transfers between devices with their start and end apart: 25, of which 14 were waited for; matrix products, arithmetic and copies ran while one was open for 2% of the time, Pallas kernels for 3%

profile of v4, /device:TPU:2, one launch (start us, length us, event | category | flops | bytes accessed | tf_op | source)
XLA Modules:
  0.0 96.7 jit_solution(6368153407179227775)
XLA Ops:
  4.8 8.4 %collective-permute-start = (bf16[152,1024]{1,0:T(8,128)(2,1)S(1)}, bf16[152,1024]{1,0:T(8,128)(2,1)S(1)}, u32[]{:S(2)}, u32[]{:S(2)}) collective-permute-start(bf16[152,1024]{1,0:T(8,128)(2,1)S(1)} %pad_maximum_fusion.2), channel_id=1, source_target_pairs={{0,252},{4,0},{8,4},{12,8},{16,12},{20,16},{24,20},{28,24},{32,28}... | collective-permute-start | bytes 933896 | tf_op jit(solution)/shard_map/ppermute | solution.py:31
  13.3 2.5 %collective-permute-start.1 = (bf16[152,1024]{1,0:T(8,128)(2,1)S(1)}, bf16[152,1024]{1,0:T(8,128)(2,1)S(1)}, u32[]{:S(2)}, u32[]{:S(2)}) collective-permute-start(bf16[152,1024]{1,0:T(8,128)(2,1)S(1)} %pad_maximum_fusion.1.m0.refs_0_), channel_id=1, source_target_pairs={{0,2},{1,3},{2,0},{3,1},{4,6},{5,7},{6,4},{7,5},{8,10},{9,11},{10,... | collective-permute-start | bytes 933896 | tf_op jit(solution)/shard_map/ppermute | solution.py:31
  15.8 2.1 %shard_map.112 = (f32[4,144,144]{2,1,0:T(8,128)S(1)}, bf16[88,16,256]{2,1,0:T(8,128)(2,1)S(1)}, bf16[88,48,256]{2,1,0:T(8,128)(2,1)S(1)}) custom-call(f32[4,768]{1,0:T(4,128)S(1)} %pad.22.table, s32[144,144]{1,0:T(8,128)S(1)} %copy-done.5, bf16[144,144]{1,0:T(8,128)(2,1)S(1)} %copy-done.6), custom_call_target="tpu_custom_call" | custom-call | flops 100000000 | bytes 4000000 | tf_op jit(solution)/shard_map/pallas_call | solution.py:396
  18.0 1.8 %collective-permute-done.m1.refs_1_ = bf16[152,1024]{1,0:T(8,128)(2,1)S(1)} collective-permute-done((bf16[152,1024]{1,0:T(8,128)(2,1)S(1)}, bf16[152,1024]{1,0:T(8,128)(2,1)S(1)}, u32[]{:S(2)}, u32[]{:S(2)}) %collective-permute-start) | collective-permute-done | bytes 311328 | tf_op jit(solution)/shard_map/ppermute | solution.py:31
  19.8 3.9 %collective-permute-done.1.refs_4_ = bf16[152,1024]{1,0:T(8,128)(2,1)S(1)} collective-permute-done((bf16[152,1024]{1,0:T(8,128)(2,1)S(1)}, bf16[152,1024]{1,0:T(8,128)(2,1)S(1)}, u32[]{:S(2)}, u32[]{:S(2)}) %collective-permute-start.1) | collective-permute-done | bytes 311328 | tf_op jit(solution)/shard_map/ppermute | solution.py:31
  23.7 2.4 %collective-permute-start.4 = (bf16[152,1024]{1,0:T(8,128)(2,1)S(1)}, bf16[152,1024]{1,0:T(8,128)(2,1)S(1)}, u32[]{:S(2)}, u32[]{:S(2)}) collective-permute-start(bf16[152,1024]{1,0:T(8,128)(2,1)S(1)} %collective-permute-done.m1.refs_1_), channel_id=1, source_target_pairs={{0,2},{1,3},{2,0},{3,1},{4,6},{5,7},{6,4},{7,5},{8,10},{9,11},{10,... | collective-permute-start | bytes 933896 | tf_op jit(solution)/shard_map/ppermute | solution.py:31
  27.0 8.0 %collective-permute-done.4.refs_5_ = bf16[152,1024]{1,0:T(8,128)(2,1)S(1)} collective-permute-done((bf16[152,1024]{1,0:T(8,128)(2,1)S(1)}, bf16[152,1024]{1,0:T(8,128)(2,1)S(1)}, u32[]{:S(2)}, u32[]{:S(2)}) %collective-permute-start.4) | collective-permute-done | bytes 311328 | tf_op jit(solution)/shard_map/ppermute | solution.py:31
  37.0 7.5 %shard_map.114 = (bf16[640,768]{1,0:T(8,128)(2,1)S(1)}, bf16[272,640]{1,0:T(8,128)(2,1)S(1)}, bf16[272,640]{1,0:T(8,128)(2,1)S(1)}, bf16[272,640]{1,0:T(8,128)(2...) custom-call(bf16[152,1024]{1,0:T(8,128)(2,1)S(1)} %pad_maximum_fusio, ...), custom_call_target="tpu_custom_call" | custom-call | flops 3000000000 | bytes 10000000 | tf_op jit(solution)/shard_map/pallas_call | solution.py:418
  46.0 1.5 %collective-permute-start.16 = (bf16[256,384]{1,0:T(8,128)(2,1)S(1)}, bf16[256,384]{1,0:T(8,128)(2,1)S(1)}, u32[]{:S(2)}, u32[]{:S(2)}) collective-permute-start(bf16[256,384]{1,0:T(8,128)(2,1)S(1)} %get-tuple-element.95), channel_id=1, source_target_pairs={{0,128},{4,132},{8,136},{12,140},{16,144},{20,148},{24,152},{28,15... | collective-permute-start | bytes 589832 | tf_op jit(solution)/shard_map/ppermute | solution.py:31
  47.6 1.3 %collective-permute-start.8 = (bf16[272,640]{1,0:T(8,128)(2,1)S(1)}, bf16[272,640]{1,0:T(8,128)(2,1)S(1)}, u32[]{:S(2)}, u32[]{:S(2)}) collective-permute-start(bf16[272,640]{1,0:T(8,128)(2,1)S(1)} %get-tuple-element.80), channel_id=1, source_target_pairs={{0,64},{4,68},{8,72},{12,76},{16,80},{20,84},{24,88},{28,92},{32,9... | collective-permute-start | bytes 1044488 | tf_op jit(solution)/shard_map/ppermute | solution.py:31
  48.9 1.9 %collective-permute-start.9 = (bf16[272,640]{1,0:T(8,128)(2,1)S(1)}, bf16[272,640]{1,0:T(8,128)(2,1)S(1)}, u32[]{:S(2)}, u32[]{:S(2)}) collective-permute-start(bf16[272,640]{1,0:T(8,128)(2,1)S(1)} %get-tuple-element.81), channel_id=1, source_target_pairs={{0,96},{4,100},{8,104},{12,108},{16,112},{20,116},{24,120},{28,124... | collective-permute-start | bytes 1044488 | tf_op jit(solution)/shard_map/ppermute | solution.py:31
  50.9 2.3 %collective-permute-done.15.refs_1_ = bf16[256,384]{1,0:T(8,128)(2,1)S(1)} collective-permute-done((bf16[256,384]{1,0:T(8,128)(2,1)S(1)}, bf16[256,384]{1,0:T(8,128)(2,1)S(1)}, u32[]{:S(2)}, u32[]{:S(2)}) %collective-permute-start.15) | collective-permute-done | bytes 196640 | tf_op jit(solution)/shard_map/ppermute | solution.py:31
  53.2 2.4 %collective-permute-start.11 = (bf16[144,1024]{1,0:T(8,128)(2,1)S(1)}, bf16[144,1024]{1,0:T(8,128)(2,1)S(1)}, u32[]{:S(2)}, u32[]{:S(2)}) collective-permute-start(bf16[144,1024]{1,0:T(8,128)(2,1)S(1)} %add_convert_fusion), channel_id=1, source_target_pairs={{0,2},{1,3},{2,0},{3,1},{4,6},{5,7},{6,4},{7,5},{8,10},{9,11},{10,... | collective-permute-start | bytes 884744 | tf_op jit(solution)/shard_map/ppermute | solution.py:31
  55.6 1.5 %collective-permute-start.17 = (bf16[256,384]{1,0:T(8,128)(2,1)S(1)}, bf16[256,384]{1,0:T(8,128)(2,1)S(1)}, u32[]{:S(2)}, u32[]{:S(2)}) collective-permute-start(bf16[256,384]{1,0:T(8,128)(2,1)S(1)} %get-tuple-element.96), channel_id=1, source_target_pairs={{0,132},{4,128},{8,140},{12,136},{16,148},{20,144},{24,156},{28,15... | collective-permute-start | bytes 589832 | tf_op jit(solution)/shard_map/ppermute | solution.py:31
  57.1 5.5 %collective-permute-done.17.refs_3_ = bf16[256,384]{1,0:T(8,128)(2,1)S(1)} collective-permute-done((bf16[256,384]{1,0:T(8,128)(2,1)S(1)}, bf16[256,384]{1,0:T(8,128)(2,1)S(1)}, u32[]{:S(2)}, u32[]{:S(2)}) %collective-permute-start.17) | collective-permute-done | bytes 196640 | tf_op jit(solution)/shard_map/ppermute | solution.py:31
  62.9 4.0 %collective-permute-done.7.refs_1_ = bf16[272,640]{1,0:T(8,128)(2,1)S(1)} collective-permute-done((bf16[272,640]{1,0:T(8,128)(2,1)S(1)}, bf16[272,640]{1,0:T(8,128)(2,1)S(1)}, u32[]{:S(2)}, u32[]{:S(2)}) %collective-permute-start.7) | collective-permute-done | bytes 348192 | tf_op jit(solution)/shard_map/ppermute | solution.py:31
  67.5 1.4 %collective-permute-start.21 = (bf16[72,1024]{1,0:T(8,128)(2,1)S(1)}, bf16[72,1024]{1,0:T(8,128)(2,1)S(1)}, u32[]{:S(2)}, u32[]{:S(2)}) collective-permute-start(bf16[72,1024]{1,0:T(8,128)(2,1)S(1)} %slice.50), channel_id=1, source_target_pairs={{0,4},{4,8},{8,12},{12,16},{16,20},{20,24},{24,28},{28,32},{32,36}... | collective-permute-start | bytes 442376 | tf_op jit(solution)/shard_map/ppermute | solution.py:31
  70.0 2.7 %collective-permute-start.14 = (bf16[80,640]{1,0:T(8,128)(2,1)S(1)}, bf16[80,640]{1,0:T(8,128)(2,1)S(1)}, u32[]{:S(2)}, u32[]{:S(2)}) collective-permute-start(bf16[80,640]{1,0:T(8,128)(2,1)S(1)} %get-tuple-element.92), channel_id=1, source_target_pairs={{0,132},{4,128},{8,140},{12,136},{16,148},{20,144},{24,156},{28,15... | collective-permute-start | bytes 307208 | tf_op jit(solution)/shard_map/ppermute | solution.py:31
  73.7 5.2 %collective-permute-done.19.refs_6_ = bf16[64,384]{1,0:T(8,128)(2,1)S(1)} collective-permute-done((bf16[64,384]{1,0:T(8,128)(2,1)S(1)}, bf16[64,384]{1,0:T(8,128)(2,1)S(1)}, u32[]{:S(2)}, u32[]{:S(2)}) %collective-permute-start.19) | collective-permute-done | bytes 49184 | tf_op jit(solution)/shard_map/ppermute | solution.py:31
  78.9 1.8 %collective-permute-start.20 = (bf16[64,384]{1,0:T(8,128)(2,1)S(1)}, bf16[64,384]{1,0:T(8,128)(2,1)S(1)}, u32[]{:S(2)}, u32[]{:S(2)}) collective-permute-start(bf16[64,384]{1,0:T(8,128)(2,1)S(1)} %get-tuple-element.100), channel_id=1, source_target_pairs={{0,96},{4,100},{8,104},{12,108},{16,112},{20,116},{24,120},{28,124... | collective-permute-start | bytes 147464 | tf_op jit(solution)/shard_map/ppermute | solution.py:31
  80.7 2.3 %collective-permute-done.20.refs_7_ = bf16[64,384]{1,0:T(8,128)(2,1)S(1)} collective-permute-done((bf16[64,384]{1,0:T(8,128)(2,1)S(1)}, bf16[64,384]{1,0:T(8,128)(2,1)S(1)}, u32[]{:S(2)}, u32[]{:S(2)}) %collective-permute-start.20) | collective-permute-done | bytes 49184 | tf_op jit(solution)/shard_map/ppermute | solution.py:31
  83.3 7.2 %collective-permute-start.23 = (bf16[32,1024]{1,0:T(8,128)(2,1)S(1)}, bf16[32,1024]{1,0:T(8,128)(2,1)S(1)}, u32[]{:S(2)}, u32[]{:S(2)}) collective-permute-start(bf16[32,1024]{1,0:T(8,128)(2,1)S(1)} %get-tuple-element.113), channel_id=1, source_target_pairs={{0,16},{4,20},{8,24},{12,28},{16,0},{20,4},{24,8},{28,12},{32,48},... | collective-permute-start | bytes 196616 | tf_op jit(solution)/shard_map/ppermute | solution.py:31
  90.4 1.3 %collective-permute-start.24 = (bf16[32,1024]{1,0:T(8,128)(2,1)S(1)}, bf16[32,1024]{1,0:T(8,128)(2,1)S(1)}, u32[]{:S(2)}, u32[]{:S(2)}) collective-permute-start(bf16[32,1024]{1,0:T(8,128)(2,1)S(1)} %get-tuple-element.114), channel_id=1, source_target_pairs={{0,24},{4,28},{8,0},{12,4},{16,8},{20,12},{24,16},{28,20},{32,56},... | collective-permute-start | bytes 196616 | tf_op jit(solution)/shard_map/ppermute | solution.py:31
  93.4 2.5 %collective-permute-done.24.d = bf16[32,1024]{1,0:T(8,128)(2,1)S(1)} collective-permute-done((bf16[32,1024]{1,0:T(8,128)(2,1)S(1)}, bf16[32,1024]{1,0:T(8,128)(2,1)S(1)}, u32[]{:S(2)}, u32[]{:S(2)}) %collective-permute-start.24) | collective-permute-done | bytes 65568 | tf_op jit(solution)/shard_map/ppermute | solution.py:31
  (78 shorter events, 14.3 us)
Async XLA Ops:
  4.8 15.0 %collective-permute-start = (bf16[152,1024]{1,0:T(8,128)(2,1)S(1)}, bf16[152,1024]{1,0:T(8,128)(2,1)S(1)}, u32[]{:S(2)}, u32[]{:S(2)}) collective-permute-start(bf16[152,1024]{1,0:T(8,128)(2,1)S(1)} %pad_maximum_fusion.2), channel_id=1, source_target_pairs={{0,252},{4,0},{8,4},{12,8},{16,12},{20,16},{24,20},{28,24},{32,28}... | collective-permute-start | bytes 933896 | tf_op jit(solution)/shard_map/ppermute | solution.py:31
  13.3 10.4 %collective-permute-start.1 = (bf16[152,1024]{1,0:T(8,128)(2,1)S(1)}, bf16[152,1024]{1,0:T(8,128)(2,1)S(1)}, u32[]{:S(2)}, u32[]{:S(2)}) collective-permute-start(bf16[152,1024]{1,0:T(8,128)(2,1)S(1)} %pad_maximum_fusion.1.m0.refs_0_), channel_id=1, source_target_pairs={{0,2},{1,3},{2,0},{3,1},{4,6},{5,7},{6,4},{7,5},{8,10},{9,11},{10,... | collective-permute-start | bytes 933896 | tf_op jit(solution)/shard_map/ppermute | solution.py:31
  15.8 10.3 %collective-permute-start.2 = (bf16[152,1024]{1,0:T(8,128)(2,1)S(1)}, bf16[152,1024]{1,0:T(8,128)(2,1)S(1)}, u32[]{:S(2)}, u32[]{:S(2)}) collective-permute-start(bf16[152,1024]{1,0:T(8,128)(2,1)S(1)} %pad_maximum_fusion.1.m0.refs_0_), channel_id=1, source_target_pairs={{0,1},{1,0},{2,3},{3,2},{4,5},{5,4},{6,7},{7,6},{8,9},{9,8},{10,11... | collective-permute-start | bytes 933896 | tf_op jit(solution)/shard_map/ppermute | solution.py:31
  23.7 2.4 %collective-permute-start.3 = (bf16[152,1024]{1,0:T(8,128)(2,1)S(1)}, bf16[152,1024]{1,0:T(8,128)(2,1)S(1)}, u32[]{:S(2)}, u32[]{:S(2)}) collective-permute-start(bf16[152,1024]{1,0:T(8,128)(2,1)S(1)} %collective-permute-done.m1.refs_1_), channel_id=1, source_target_pairs={{0,1},{1,0},{2,3},{3,2},{4,5},{5,4},{6,7},{7,6},{8,9},{9,8},{10,11... | collective-permute-start | bytes 933896 | tf_op jit(solution)/shard_map/ppermute | solution.py:31
  23.7 11.3 %collective-permute-start.4 = (bf16[152,1024]{1,0:T(8,128)(2,1)S(1)}, bf16[152,1024]{1,0:T(8,128)(2,1)S(1)}, u32[]{:S(2)}, u32[]{:S(2)}) collective-permute-start(bf16[152,1024]{1,0:T(8,128)(2,1)S(1)} %collective-permute-done.m1.refs_1_), channel_id=1, source_target_pairs={{0,2},{1,3},{2,0},{3,1},{4,6},{5,7},{6,4},{7,5},{8,10},{9,11},{10,... | collective-permute-start | bytes 933896 | tf_op jit(solution)/shard_map/ppermute | solution.py:31
  35.0 2.0 %collective-permute-start.6 = (bf16[152,1024]{1,0:T(8,128)(2,1)S(1)}, bf16[152,1024]{1,0:T(8,128)(2,1)S(1)}, u32[]{:S(2)}, u32[]{:S(2)}) collective-permute-start(bf16[152,1024]{1,0:T(8,128)(2,1)S(1)} %collective-permute-done.4.refs_5_), channel_id=1, source_target_pairs={{0,1},{1,0},{2,3},{3,2},{4,5},{5,4},{6,7},{7,6},{8,9},{9,8},{10,11... | collective-permute-start | bytes 933896 | tf_op jit(solution)/shard_map/ppermute | solution.py:31
  45.8 3.1 %collective-permute-start.10 = (bf16[288,1024]{1,0:T(8,128)(2,1)S(1)}, bf16[288,1024]{1,0:T(8,128)(2,1)S(1)}, u32[]{:S(2)}, u32[]{:S(2)}) collective-permute-start(bf16[288,1024]{1,0:T(8,128)(2,1)S(1)} %get-tuple-element.84), channel_id=1, source_target_pairs={{0,1},{1,0},{2,3},{3,2},{4,5},{5,4},{6,7},{7,6},{8,9},{9,8},{10,11... | collective-permute-start | bytes 1769480 | tf_op jit(solution)/shard_map/ppermute | solution.py:31
  46.0 7.2 %collective-permute-start.15 = (bf16[256,384]{1,0:T(8,128)(2,1)S(1)}, bf16[256,384]{1,0:T(8,128)(2,1)S(1)}, u32[]{:S(2)}, u32[]{:S(2)}) collective-permute-start(bf16[256,384]{1,0:T(8,128)(2,1)S(1)} %get-tuple-element.94), channel_id=1, source_target_pairs={{0,4},{4,0},{8,12},{12,8},{16,20},{20,16},{24,28},{28,24},{32,36},... | collective-permute-start | bytes 589832 | tf_op jit(solution)/shard_map/ppermute | solution.py:31
  46.0 9.6 %collective-permute-start.16 = (bf16[256,384]{1,0:T(8,128)(2,1)S(1)}, bf16[256,384]{1,0:T(8,128)(2,1)S(1)}, u32[]{:S(2)}, u32[]{:S(2)}) collective-permute-start(bf16[256,384]{1,0:T(8,128)(2,1)S(1)} %get-tuple-element.95), channel_id=1, source_target_pairs={{0,128},{4,132},{8,136},{12,140},{16,144},{20,148},{24,152},{28,15... | collective-permute-start | bytes 589832 | tf_op jit(solution)/shard_map/ppermute | solution.py:31
  47.6 19.3 %collective-permute-start.7 = (bf16[272,640]{1,0:T(8,128)(2,1)S(1)}, bf16[272,640]{1,0:T(8,128)(2,1)S(1)}, u32[]{:S(2)}, u32[]{:S(2)}) collective-permute-start(bf16[272,640]{1,0:T(8,128)(2,1)S(1)} %get-tuple-element.79), channel_id=1, source_target_pairs={{0,32},{4,36},{8,40},{12,44},{16,48},{20,52},{24,56},{28,60},{32,6... | collective-permute-start | bytes 1044488 | tf_op jit(solution)/shard_map/ppermute | solution.py:31
  47.6 19.3 %collective-permute-start.8 = (bf16[272,640]{1,0:T(8,128)(2,1)S(1)}, bf16[272,640]{1,0:T(8,128)(2,1)S(1)}, u32[]{:S(2)}, u32[]{:S(2)}) collective-permute-start(bf16[272,640]{1,0:T(8,128)(2,1)S(1)} %get-tuple-element.80), channel_id=1, source_target_pairs={{0,64},{4,68},{8,72},{12,76},{16,80},{20,84},{24,88},{28,92},{32,9... | collective-permute-start | bytes 1044488 | tf_op jit(solution)/shard_map/ppermute | solution.py:31
  48.9 18.1 %collective-permute-start.9 = (bf16[272,640]{1,0:T(8,128)(2,1)S(1)}, bf16[272,640]{1,0:T(8,128)(2,1)S(1)}, u32[]{:S(2)}, u32[]{:S(2)}) collective-permute-start(bf16[272,640]{1,0:T(8,128)(2,1)S(1)} %get-tuple-element.81), channel_id=1, source_target_pairs={{0,96},{4,100},{8,104},{12,108},{16,112},{20,116},{24,120},{28,124... | collective-permute-start | bytes 1044488 | tf_op jit(solution)/shard_map/ppermute | solution.py:31
  53.2 14.2 %collective-permute-start.11 = (bf16[144,1024]{1,0:T(8,128)(2,1)S(1)}, bf16[144,1024]{1,0:T(8,128)(2,1)S(1)}, u32[]{:S(2)}, u32[]{:S(2)}) collective-permute-start(bf16[144,1024]{1,0:T(8,128)(2,1)S(1)} %add_convert_fusion), channel_id=1, source_target_pairs={{0,2},{1,3},{2,0},{3,1},{4,6},{5,7},{6,4},{7,5},{8,10},{9,11},{10,... | collective-permute-start | bytes 884744 | tf_op jit(solution)/shard_map/ppermute | solution.py:31
  55.6 7.1 %collective-permute-start.17 = (bf16[256,384]{1,0:T(8,128)(2,1)S(1)}, bf16[256,384]{1,0:T(8,128)(2,1)S(1)}, u32[]{:S(2)}, u32[]{:S(2)}) collective-permute-start(bf16[256,384]{1,0:T(8,128)(2,1)S(1)} %get-tuple-element.96), channel_id=1, source_target_pairs={{0,132},{4,128},{8,140},{12,136},{16,148},{20,144},{24,156},{28,15... | collective-permute-start | bytes 589832 | tf_op jit(solution)/shard_map/ppermute | solution.py:31
  62.8 9.9 %collective-permute-start.18 = (bf16[64,384]{1,0:T(8,128)(2,1)S(1)}, bf16[64,384]{1,0:T(8,128)(2,1)S(1)}, u32[]{:S(2)}, u32[]{:S(2)}) collective-permute-start(bf16[64,384]{1,0:T(8,128)(2,1)S(1)} %get-tuple-element.98), channel_id=1, source_target_pairs={{0,32},{4,36},{8,40},{12,44},{16,48},{20,52},{24,56},{28,60},{32,6... | collective-permute-start | bytes 147464 | tf_op jit(solution)/shard_map/ppermute | solution.py:31
  67.5 15.5 %collective-permute-start.21 = (bf16[72,1024]{1,0:T(8,128)(2,1)S(1)}, bf16[72,1024]{1,0:T(8,128)(2,1)S(1)}, u32[]{:S(2)}, u32[]{:S(2)}) collective-permute-start(bf16[72,1024]{1,0:T(8,128)(2,1)S(1)} %slice.50), channel_id=1, source_target_pairs={{0,4},{4,8},{8,12},{12,16},{16,20},{20,24},{24,28},{28,32},{32,36}... | collective-permute-start | bytes 442376 | tf_op jit(solution)/shard_map/ppermute | solution.py:31
  69.2 13.8 %collective-permute-start.12 = (bf16[80,640]{1,0:T(8,128)(2,1)S(1)}, bf16[80,640]{1,0:T(8,128)(2,1)S(1)}, u32[]{:S(2)}, u32[]{:S(2)}) collective-permute-start(bf16[80,640]{1,0:T(8,128)(2,1)S(1)} %get-tuple-element.90), channel_id=1, source_target_pairs={{0,4},{4,0},{8,12},{12,8},{16,20},{20,16},{24,28},{28,24},{32,36},... | collective-permute-start | bytes 307208 | tf_op jit(solution)/shard_map/ppermute | solution.py:31
  69.3 13.8 %collective-permute-start.13 = (bf16[80,640]{1,0:T(8,128)(2,1)S(1)}, bf16[80,640]{1,0:T(8,128)(2,1)S(1)}, u32[]{:S(2)}, u32[]{:S(2)}) collective-permute-start(bf16[80,640]{1,0:T(8,128)(2,1)S(1)} %get-tuple-element.91), channel_id=1, source_target_pairs={{0,128},{4,132},{8,136},{12,140},{16,144},{20,148},{24,152},{28,15... | collective-permute-start | bytes 307208 | tf_op jit(solution)/shard_map/ppermute | solution.py:31
  70.0 13.0 %collective-permute-start.14 = (bf16[80,640]{1,0:T(8,128)(2,1)S(1)}, bf16[80,640]{1,0:T(8,128)(2,1)S(1)}, u32[]{:S(2)}, u32[]{:S(2)}) collective-permute-start(bf16[80,640]{1,0:T(8,128)(2,1)S(1)} %get-tuple-element.92), channel_id=1, source_target_pairs={{0,132},{4,128},{8,140},{12,136},{16,148},{20,144},{24,156},{28,15... | collective-permute-start | bytes 307208 | tf_op jit(solution)/shard_map/ppermute | solution.py:31
  72.7 6.2 %collective-permute-start.19 = (bf16[64,384]{1,0:T(8,128)(2,1)S(1)}, bf16[64,384]{1,0:T(8,128)(2,1)S(1)}, u32[]{:S(2)}, u32[]{:S(2)}) collective-permute-start(bf16[64,384]{1,0:T(8,128)(2,1)S(1)} %get-tuple-element.99), channel_id=1, source_target_pairs={{0,64},{4,68},{8,72},{12,76},{16,80},{20,84},{24,88},{28,92},{32,9... | collective-permute-start | bytes 147464 | tf_op jit(solution)/shard_map/ppermute | solution.py:31
  78.9 4.1 %collective-permute-start.20 = (bf16[64,384]{1,0:T(8,128)(2,1)S(1)}, bf16[64,384]{1,0:T(8,128)(2,1)S(1)}, u32[]{:S(2)}, u32[]{:S(2)}) collective-permute-start(bf16[64,384]{1,0:T(8,128)(2,1)S(1)} %get-tuple-element.100), channel_id=1, source_target_pairs={{0,96},{4,100},{8,104},{12,108},{16,112},{20,116},{24,120},{28,124... | collective-permute-start | bytes 147464 | tf_op jit(solution)/shard_map/ppermute | solution.py:31
  83.2 9.7 %collective-permute-start.22 = (bf16[32,1024]{1,0:T(8,128)(2,1)S(1)}, bf16[32,1024]{1,0:T(8,128)(2,1)S(1)}, u32[]{:S(2)}, u32[]{:S(2)}) collective-permute-start(bf16[32,1024]{1,0:T(8,128)(2,1)S(1)} %get-tuple-element.112), channel_id=1, source_target_pairs={{0,8},{4,12},{8,16},{12,20},{16,24},{20,28},{24,0},{28,4},{32,40},... | collective-permute-start | bytes 196616 | tf_op jit(solution)/shard_map/ppermute | solution.py:31
  83.3 10.1 %collective-permute-start.23 = (bf16[32,1024]{1,0:T(8,128)(2,1)S(1)}, bf16[32,1024]{1,0:T(8,128)(2,1)S(1)}, u32[]{:S(2)}, u32[]{:S(2)}) collective-permute-start(bf16[32,1024]{1,0:T(8,128)(2,1)S(1)} %get-tuple-element.113), channel_id=1, source_target_pairs={{0,16},{4,20},{8,24},{12,28},{16,0},{20,4},{24,8},{28,12},{32,48},... | collective-permute-start | bytes 196616 | tf_op jit(solution)/shard_map/ppermute | solution.py:31
  90.4 5.5 %collective-permute-start.24 = (bf16[32,1024]{1,0:T(8,128)(2,1)S(1)}, bf16[32,1024]{1,0:T(8,128)(2,1)S(1)}, u32[]{:S(2)}, u32[]{:S(2)}) collective-permute-start(bf16[32,1024]{1,0:T(8,128)(2,1)S(1)} %get-tuple-element.114), channel_id=1, source_target_pairs={{0,24},{4,28},{8,0},{12,4},{16,8},{20,12},{24,16},{28,20},{32,56},... | collective-permute-start | bytes 196616 | tf_op jit(solution)/shard_map/ppermute | solution.py:31
  (9 other events, 87.0 us)

commit v5 on v4

--- a/solution.py
+++ b/solution.py
@@ -214,8 +214,8 @@
 def band_kernel(*refs):
     pieces = refs[:8]
     weight, wo, bias, early, high_rows, low_rows, grads = refs[8:15]
-    ways, pairs = refs[15:19], refs[19:23]
-    tall, gall, qkv, rows, wins, outs, sums, att, labels, full = refs[23:]
+    ways, pairs = refs[15:19], refs[19:21]
+    tall, gall, qkv, rows, wins, outs, sums, att, labels, full = refs[21:]
     own = lax.axis_index("head")
     labels[...] = jnp.zeros_like(labels)
     row = lax.broadcasted_iota(jnp.int32, (8, WIDTH), 0)
@@ -266,7 +266,7 @@
     full[:, : 3 * WIDTH] = lax.dot_general(tall[...], grads[...], TN, preferred_element_type=F32).astype(BF16)
     full[:, 3 * WIDTH :] = lax.dot_general(gall[...], att[...], TN, preferred_element_type=F32).astype(BF16)
     lat = lax.axis_index("lat")
-    x, y, z = lat // (NY * NZ), lax.rem(lat // NZ, NY), lax.rem(lat, 2)
+    y, z = lax.rem(lat // NZ, NY), lax.rem(lat, 2)
     for d, out in enumerate(ways):
         out[256:272, :512] = found
         out[256:272, 512:] = jnp.zeros((16, 128), BF16)
@@ -274,8 +274,8 @@
             at = pl.ds(pl.multiple_of(half * 512 + lax.rem(y + d, NY) * 128, 128), 128)
             out[half * 128 : (half + 1) * 128, :] = full[at, :640]
     for i, out in enumerate(pairs):
-        start = lax.bitwise_xor(x, i // 2) * 512 + lax.bitwise_xor(z, i % 2) * 16
-        for b in range(16):
+        start = lax.bitwise_xor(z, i) * 16
+        for b in range(32):
             at = pl.ds(pl.multiple_of(start + (b // 4) * 128 + (b % 4) * 32, 16), 16)
             out[b * 16 : (b + 1) * 16, :] = full[at, 640:]
 
@@ -304,35 +304,43 @@
     return lat // (NY * NZ), lax.rem(lat // NZ, NY), lax.rem(lat, NZ)
 
 
-def after_ways_kernel(*refs):
-    ways, outs = refs[:4], refs[4:]
+def after_pairs_kernel(*refs):
+    pairs, outs = refs[:2], refs[2:]
+    y = place()[1]
+    for d, out in enumerate(outs):
+        to = lax.rem(y + d, NY) * 64
+        for half in range(2):
+            rows = pl.ds(pl.multiple_of(half * 256 + to, 64), 64)
+            out[half * 64 : (half + 1) * 64, :] = stage_rows(pairs, rows).astype(BF16)
+
+
+def second_kernel(*refs):
+    ways, late, (near, given, more), outs, (high, low) = refs[:4], refs[4:8], refs[8:11], refs[11:15], refs[15:]
+    total = near[...].astype(F32) + given[...].astype(F32) + more[...].astype(F32)
+    high[...] = total[:72]
+    low[...] = total[72:].astype(BF16)
     x, _, z = place()
     found = bias_rows(bias_sum(stage_rows(ways, pl.ds(256, 16), slice(0, 512))))
     for i, out in enumerate(outs):
-        start = lax.bitwise_xor(x, i // 2) * 128 + lax.bitwise_xor(lax.rem(z, 2), i % 2) * 16
+        to = lax.bitwise_xor(x, i // 2)
+        start = to * 128 + lax.bitwise_xor(lax.rem(z, 2), i % 2) * 16
         for k in range(4):
             rows = pl.ds(pl.multiple_of(start + k * 32, 16), 16)
-            out[k * 16 : (k + 1) * 16, :] = stage_rows(ways, rows).astype(BF16)
-        out[64:80, :512] = found
-        out[64:80, 512:] = jnp.zeros((16, 128), BF16)
-
-
-def after_pairs_kernel(*refs):
-    pairs, outs = refs[:4], refs[4:]
-    y = place()[1]
-    for d, out in enumerate(outs):
-        rows = pl.ds(pl.multiple_of(lax.rem(y + d, NY) * 64, 64), 64)
-        out[...] = stage_rows(pairs, rows).astype(BF16)
-
-
-def third_kernel(*refs):
-    pairs, ways, outs = refs[:4], refs[4:8], refs[8:]
+            out[k * 16 : (k + 1) * 16, :640] = stage_rows(ways, rows).astype(BF16)
+        out[64:, :512] = found
+        out[64:, 512:640] = jnp.zeros((16, 128), BF16)
+        if i % 2 == 0:
+            out[:64, 640:] = stage_rows(late, pl.ds(pl.multiple_of(to * 64, 64), 64)).astype(BF16)
+            out[64:, 640:] = jnp.zeros((16, 384), BF16)
+
+
+def third_kernel(a, b, c, d, *outs):
     z = place()[2] // 2
-    found = bias_rows(bias_sum(stage_rows(pairs, pl.ds(64, 16), slice(0, 512))))
+    found = bias_rows(bias_sum(stage_rows((a, b, c, d), pl.ds(64, 16), slice(0, 512))))
     for e, out in enumerate(outs):
         rows = pl.ds(pl.multiple_of(lax.rem(z + e, 4) * 16, 16), 16)
-        out[:16, :640] = stage_rows(pairs, rows).astype(BF16)
-        out[:16, 640:] = stage_rows(ways, rows).astype(BF16)
+        out[:16, :640] = stage_rows((a, b, c, d), rows, slice(0, 640)).astype(BF16)
+        out[:16, 640:] = stage_rows((a, c), rows, slice(640, 1024)).astype(BF16)
         out[16:, :512] = found
         out[16:, 512:] = jnp.zeros_like(found)
 
@@ -389,6 +397,7 @@
         return jnp.concatenate([t, label_rows(loaded[2][rows], 72 * r), g])
 
     high = message(0)
+    high, qkv_weight, out_weight, bias_index = lax.optimization_barrier((high, qkv_weight, out_weight, bias_index))
     low = back(message(1))
     far_high = across(high)
 
@@ -400,7 +409,7 @@
         10**8,
         4 * 10**6,
     )(table, bias_index, jnp.asarray(window_order(), BF16))
-    low, far_high, bias, high_rows, low_rows = lax.optimization_barrier((low, far_high, bias, high_rows, low_rows))
+    low, bias, high_rows, low_rows = lax.optimization_barrier((low, bias, high_rows, low_rows))
     far_low = across(low)
     near = (high, low, core(high), core(low))
 
@@ -412,14 +421,14 @@
         5 * 10**6,
         8,
     )(*near, qkv_weight, out_weight)
-    far_high, far_low, early = lax.optimization_barrier((far_high, far_low, early))
+    far_low, early = lax.optimization_barrier((far_low, early))
     far = (far_high, far_low, core(far_high), core(far_low))
 
     grads, *blocks = call(
         band_kernel,
         (shape((ALL, 3 * WIDTH), BF16),)
         + (shape((272, 640), BF16),) * 4
-        + (shape((256, 384), BF16),) * 4,
+        + (shape((512, 384), BF16),) * 2,
         [
             pltpu.VMEM((ALL, D), BF16),
             pltpu.VMEM((ALL, D), BF16),
@@ -441,10 +450,11 @@
         far = sent(parts[2], "lat", moved(0, 2, 0))
         return [parts[0], sent(parts[1], "lat", moved(0, 1, 0)), far, sent(parts[3], "lat", moved(0, 3, 0))]
 
-    def by_pair(parts):
-        return [parts[0]] + [sent(parts[d], "lat", paired(d // 2, d % 2)) for d in range(1, 4)]
-
-    ways, pairs = by_y(blocks[:4]), by_pair(blocks[4:])
+    def swapped(parts, dx, dz):
+        return [parts[0], sent(parts[1], "lat", paired(dx, dz))]
+
+    pairs = swapped(blocks[4:], 0, 1)
+    ways = by_y(blocks[:4])
 
     near, far, given = call(
         input_kernel, (shape((WT, D), BF16), shape((WT, D), BF16), shape((2 * WT, D), BF16)), (), 10**9, 5 * 10**6
@@ -452,16 +462,17 @@
     given = core(given)
     far = (far.astype(F32) + given[WT:].astype(F32)).astype(BF16)
     more = across(far)
-    parts = call(after_pairs_kernel, (shape((64, 384), BF16),) * 4, (), 10**6, 10**6, 8)(*pairs)
+    parts = call(after_pairs_kernel, (shape((128, 384), BF16),) * 4, (), 10**6, 10**6, 8)(*pairs)
     late = by_y(parts)
-    ways, more = lax.optimization_barrier((ways, more))
-    near = near.astype(F32) + given[:WT].astype(F32) + more.astype(F32)
-    low = onward(near[72:].astype(BF16))
-    parts = call(after_ways_kernel, (shape((80, 640), BF16),) * 4, (), 10**6, 2 * 10**6, 8)(*ways)
-    pairs = by_pair(parts)
-    pairs, late, low = lax.optimization_barrier((pairs, late, low))
-    input_grad = jnp.concatenate([low.astype(F32), near[:72]]).reshape(6, 12, 2, D).transpose(0, 2, 1, 3)
-    parts = call(third_kernel, (shape((32, D), BF16),) * 4, (), 10**6, 10**6, 8)(*pairs, *late)
+    ways, late, more = lax.optimization_barrier((ways, late, more))
+    full, part = shape((80, D), BF16), shape((80, 640), BF16)
+    *parts, near, low = call(
+        second_kernel, (full, part, full, part, shape((72, D), F32), shape((72, D), BF16)), (), 10**6, 4 * 10**6, 8
+    )(*ways, *late, near, given[:WT], more)
+    parts = [parts[0]] + [sent(parts[i], "lat", paired(i // 2, i % 2)) for i in range(1, 4)]
+    parts, low = lax.optimization_barrier((parts, onward(low)))
+    input_grad = jnp.concatenate([low.astype(F32), near]).reshape(6, 12, 2, D).transpose(0, 2, 1, 3)
+    parts = call(third_kernel, (shape((32, D), BF16),) * 4, (), 10**6, 10**6, 8)(*parts)
     far = sent(parts[2], "lat", moved(0, 0, 4))
     got = [parts[0], sent(parts[1], "lat", moved(0, 0, 2)), far, sent(parts[3], "lat", moved(0, 0, 6))]
     got, input_grad = lax.optimization_barrier((got, input_grad))

time: 97.4 us -> 90.9 us (0.933)
  starting transfers between devices: 39 us -> 28.5 us
  waiting for transfers between devices: 38.1 us -> 41.9 us
    ppermute x25 -> x23, starting transfers between devices: 39 us -> 28.5 us  [sent(): return lax.ppermute(x, axis, [(i, to(i)) for i in range(size)])]
    ppermute x25 -> x23, waiting for transfers between devices: 38.1 us -> 41.9 us  [sent(): return lax.ppermute(x, axis, [(i, to(i)) for i in range(size)])]
  transfers between devices with their start and end apart: 25 -> 23, of which waited for: 14 -> 15; matrix products, arithmetic and copies ran while one was open for 2% -> 2% of each run, Pallas kernels for 3% -> 3%
where the time goes in v5:
time: 90.9 us; the launch traced here: 90.1 us
  waiting for transfers between devices  41.9 us (46%)
  starting transfers between devices  28.5 us (31%)
  Pallas kernels  13.5 us (15%)
  local copies, waits for them, and re-layouts  4.98 us (5%)
    ppermute x23, waiting for transfers between devices, sent(): return lax.ppermute(x, axis, [(i, to(i)) for i in range(size)])  41.9 us
    ppermute x23, starting transfers between devices, sent(): return lax.ppermute(x, axis, [(i, to(i)) for i in range(size)])  28.5 us
    pallas_call x1, Pallas kernels, shards(): call(band_kernel, (shape((ALL, 3 * WIDTH), BF16),) + (shape((272, 640), B...  7.57 us
    unnamed x16, local copies, waits for them, and re-layouts  2.63 us
    pallas_call x1, Pallas kernels, shards(): call(bias_kernel, (shape((HEADS, WT, WT), F32), shape((88, 16, 256), BF16...  2.14 us
  transfers between devices with their start and end apart: 23, of which 15 were waited for; matrix products, arithmetic and copies ran while one was open for 2% of the time, Pallas kernels for 3%

profile of v5, /device:TPU:2, one launch (start us, length us, event | category | flops | bytes accessed | tf_op | source)
XLA Modules:
  0.0 90.1 jit_solution(14881628814071336243)
XLA Ops:
  4.8 8.4 %collective-permute-start = (bf16[152,1024]{1,0:T(8,128)(2,1)S(1)}, bf16[152,1024]{1,0:T(8,128)(2,1)S(1)}, u32[]{:S(2)}, u32[]{:S(2)}) collective-permute-start(bf16[152,1024]{1,0:T(8,128)(2,1)S(1)} %pad_maximum_fusion.2), channel_id=1, source_target_pairs={{0,252},{4,0},{8,4},{12,8},{16,12},{20,16},{24,20},{28,24},{32,28}... | collective-permute-start | bytes 933896 | tf_op jit(solution)/shard_map/ppermute | solution.py:31
  13.3 2.5 %collective-permute-start.3 = (bf16[152,1024]{1,0:T(8,128)(2,1)S(1)}, bf16[152,1024]{1,0:T(8,128)(2,1)S(1)}, u32[]{:S(2)}, u32[]{:S(2)}) collective-permute-start(bf16[152,1024]{1,0:T(8,128)(2,1)S(1)} %pad_maximum_fusion.1.m0.refs_0_), channel_id=1, source_target_pairs={{0,2},{1,3},{2,0},{3,1},{4,6},{5,7},{6,4},{7,5},{8,10},{9,11},{10,... | collective-permute-start | bytes 933896 | tf_op jit(solution)/shard_map/ppermute | solution.py:31
  15.8 2.1 %shard_map.112 = (f32[4,144,144]{2,1,0:T(8,128)S(1)}, bf16[88,16,256]{2,1,0:T(8,128)(2,1)S(1)}, bf16[88,48,256]{2,1,0:T(8,128)(2,1)S(1)}) custom-call(f32[4,768]{1,0:T(4,128)S(1)} %pad.22.table, s32[144,144]{1,0:T(8,128)S(1)} %copy-done.5, bf16[144,144]{1,0:T(8,128)(2,1)S(1)} %copy-done.6), custom_call_target="tpu_custom_call" | custom-call | flops 100000000 | bytes 4000000 | tf_op jit(solution)/shard_map/pallas_call | solution.py:405
  18.0 1.8 %collective-permute-done.m1.refs_1_ = bf16[152,1024]{1,0:T(8,128)(2,1)S(1)} collective-permute-done((bf16[152,1024]{1,0:T(8,128)(2,1)S(1)}, bf16[152,1024]{1,0:T(8,128)(2,1)S(1)}, u32[]{:S(2)}, u32[]{:S(2)}) %collective-permute-start) | collective-permute-done | bytes 311328 | tf_op jit(solution)/shard_map/ppermute | solution.py:31
  19.8 2.4 %collective-permute-start.4 = (bf16[152,1024]{1,0:T(8,128)(2,1)S(1)}, bf16[152,1024]{1,0:T(8,128)(2,1)S(1)}, u32[]{:S(2)}, u32[]{:S(2)}) collective-permute-start(bf16[152,1024]{1,0:T(8,128)(2,1)S(1)} %collective-permute-done.m1.refs_1_), channel_id=1, source_target_pairs={{0,2},{1,3},{2,0},{3,1},{4,6},{5,7},{6,4},{7,5},{8,10},{9,11},{10,... | collective-permute-start | bytes 933896 | tf_op jit(solution)/shard_map/ppermute | solution.py:31
  22.2 1.5 %collective-permute-done.3.refs_4_ = bf16[152,1024]{1,0:T(8,128)(2,1)S(1)} collective-permute-done((bf16[152,1024]{1,0:T(8,128)(2,1)S(1)}, bf16[152,1024]{1,0:T(8,128)(2,1)S(1)}, u32[]{:S(2)}, u32[]{:S(2)}) %collective-permute-start.3) | collective-permute-done | bytes 311328 | tf_op jit(solution)/shard_map/ppermute | solution.py:31
  24.6 6.5 %collective-permute-done.4.refs_5_ = bf16[152,1024]{1,0:T(8,128)(2,1)S(1)} collective-permute-done((bf16[152,1024]{1,0:T(8,128)(2,1)S(1)}, bf16[152,1024]{1,0:T(8,128)(2,1)S(1)}, u32[]{:S(2)}, u32[]{:S(2)}) %collective-permute-start.4) | collective-permute-done | bytes 311328 | tf_op jit(solution)/shard_map/ppermute | solution.py:31
  31.1 1.6 %collective-permute-done.6.refs_7_ = bf16[152,1024]{1,0:T(8,128)(2,1)S(1)} collective-permute-done((bf16[152,1024]{1,0:T(8,128)(2,1)S(1)}, bf16[152,1024]{1,0:T(8,128)(2,1)S(1)}, u32[]{:S(2)}, u32[]{:S(2)}) %collective-permute-start.6) | collective-permute-done | bytes 311328 | tf_op jit(solution)/shard_map/ppermute | solution.py:31
  32.7 7.6 %shard_map.114 = (bf16[640,768]{1,0:T(8,128)(2,1)S(1)}, bf16[272,640]{1,0:T(8,128)(2,1)S(1)}, bf16[272,640]{1,0:T(8,128)(2,1)S(1)}, bf16[272,640]{1,0:T(8,128)(2...) custom-call(bf16[152,1024]{1,0:T(8,128)(2,1)S(1)} %pad_maximum_fusion.1.m0.refs_0_, ...), custom_call_target="tpu_custom_call" | custom-call | flops 3000000000 | bytes 10000000 | tf_op jit(solution)/shard_map/pallas_call | solution.py:427
  40.2 1.2 %shard_map.116 = (bf16[144,1024]{1,0:T(8,128)(2,1)S(1)}, bf16[144,1024]{1,0:T(8,128)(2,1)S(1)}, bf16[288,1024]{1,0:T(8,128)(2,1)S(1)}) custom-call(bf16[640,768]{1,0:T(8,128)(2,1)S(1)} %get-tuple-element.92.grads, bf16[3,1024,256]{2,1,0:T(8,128)(2,1)S(1)} %copy-done), custom_call_target="tpu_custom_call" | custom-call | flops 1000000000 | bytes 5000000 | tf_op jit(solution)/shard_map/pallas_call | solution.py:459
  41.7 2.2 %collective-permute-start.8 = (bf16[272,640]{1,0:T(8,128)(2,1)S(1)}, bf16[272,640]{1,0:T(8,128)(2,1)S(1)}, u32[]{:S(2)}, u32[]{:S(2)}) collective-permute-start(bf16[272,640]{1,0:T(8,128)(2,1)S(1)} %get-tuple-element.84), channel_id=1, source_target_pairs={{0,64},{4,68},{8,72},{12,76},{16,80},{20,84},{24,88},{28,92},{32,9... | collective-permute-start | bytes 1044488 | tf_op jit(solution)/shard_map/ppermute | solution.py:31
  45.1 2.5 %collective-permute-start.15 = (bf16[144,1024]{1,0:T(8,128)(2,1)S(1)}, bf16[144,1024]{1,0:T(8,128)(2,1)S(1)}, u32[]{:S(2)}, u32[]{:S(2)}) collective-permute-start(bf16[144,1024]{1,0:T(8,128)(2,1)S(1)} %add_convert_fusion), channel_id=1, source_target_pairs={{0,2},{1,3},{2,0},{3,1},{4,6},{5,7},{6,4},{7,5},{8,10},{9,11},{10,... | collective-permute-start | bytes 884744 | tf_op jit(solution)/shard_map/ppermute | solution.py:31
  47.6 8.2 %collective-permute-done.10.refs_1_ = bf16[512,384]{1,0:T(8,128)(2,1)S(1)} collective-permute-done((bf16[512,384]{1,0:T(8,128)(2,1)S(1)}, bf16[512,384]{1,0:T(8,128)(2,1)S(1)}, u32[]{:S(2)}, u32[]{:S(2)}) %collective-permute-start.10) | collective-permute-done | bytes 393248 | tf_op jit(solution)/shard_map/ppermute | solution.py:31
  55.9 1.2 %collective-permute-start.11 = (bf16[128,384]{1,0:T(8,128)(2,1)S(1)}, bf16[128,384]{1,0:T(8,128)(2,1)S(1)}, u32[]{:S(2)}, u32[]{:S(2)}) collective-permute-start(bf16[128,384]{1,0:T(8,128)(2,1)S(1)} %get-tuple-element.89), channel_id=1, source_target_pairs={{0,32},{4,36},{8,40},{12,44},{16,48},{20,52},{24,56},{28,60},{32,6... | collective-permute-start | bytes 294920 | tf_op jit(solution)/shard_map/ppermute | solution.py:31
  57.0 4.3 %collective-permute-done.7.refs_1_ = bf16[272,640]{1,0:T(8,128)(2,1)S(1)} collective-permute-done((bf16[272,640]{1,0:T(8,128)(2,1)S(1)}, bf16[272,640]{1,0:T(8,128)(2,1)S(1)}, u32[]{:S(2)}, u32[]{:S(2)}) %collective-permute-start.7) | collective-permute-done | bytes 348192 | tf_op jit(solution)/shard_map/ppermute | solution.py:31
  62.9 4.6 %collective-permute-done.12.refs_6_ = bf16[128,384]{1,0:T(8,128)(2,1)S(1)} collective-permute-done((bf16[128,384]{1,0:T(8,128)(2,1)S(1)}, bf16[128,384]{1,0:T(8,128)(2,1)S(1)}, u32[]{:S(2)}, u32[]{:S(2)}) %collective-permute-start.12) | collective-permute-done | bytes 98336 | tf_op jit(solution)/shard_map/ppermute | solution.py:31
  67.9 1.6 %collective-permute-start.17 = (bf16[80,1024]{1,0:T(8,128)(2,1)S(1)}, bf16[80,1024]{1,0:T(8,128)(2,1)S(1)}, u32[]{:S(2)}, u32[]{:S(2)}) collective-permute-start(bf16[80,1024]{1,0:T(8,128)(2,1)S(1)} %get-tuple-element.107), channel_id=1, source_target_pairs={{0,128},{4,132},{8,136},{12,140},{16,144},{20,148},{24,152},{28,15... | collective-permute-start | bytes 491528 | tf_op jit(solution)/shard_map/ppermute | solution.py:31
  69.5 2.0 %collective-permute-start.18 = (bf16[80,640]{1,0:T(8,128)(2,1)S(1)}, bf16[80,640]{1,0:T(8,128)(2,1)S(1)}, u32[]{:S(2)}, u32[]{:S(2)}) collective-permute-start(bf16[80,640]{1,0:T(8,128)(2,1)S(1)} %get-tuple-element.108), channel_id=1, source_target_pairs={{0,132},{4,128},{8,140},{12,136},{16,148},{20,144},{24,156},{28,15... | collective-permute-start | bytes 307208 | tf_op jit(solution)/shard_map/ppermute | solution.py:31
  71.5 2.7 %collective-permute-done.16.b = bf16[80,640]{1,0:T(8,128)(2,1)S(1)} collective-permute-done((bf16[80,640]{1,0:T(8,128)(2,1)S(1)}, bf16[80,640]{1,0:T(8,128)(2,1)S(1)}, u32[]{:S(2)}, u32[]{:S(2)}) %collective-permute-start.16) | collective-permute-done | bytes 102432 | tf_op jit(solution)/shard_map/ppermute | solution.py:31
  75.3 3.6 %collective-permute-done.19 = bf16[72,1024]{1,0:T(8,128)(2,1)S(1)} collective-permute-done((bf16[72,1024]{1,0:T(8,128)(2,1)S(1)}, bf16[72,1024]{1,0:T(8,128)(2,1)S(1)}, u32[]{:S(2)}, u32[]{:S(2)}) %collective-permute-start.19) | collective-permute-done | bytes 147488 | tf_op jit(solution)/shard_map/ppermute | solution.py:31
  79.1 4.3 %collective-permute-start.21 = (bf16[32,1024]{1,0:T(8,128)(2,1)S(1)}, bf16[32,1024]{1,0:T(8,128)(2,1)S(1)}, u32[]{:S(2)}, u32[]{:S(2)}) collective-permute-start(bf16[32,1024]{1,0:T(8,128)(2,1)S(1)} %get-tuple-element.116), channel_id=1, source_target_pairs={{0,16},{4,20},{8,24},{12,28},{16,0},{20,4},{24,8},{28,12},{32,48},... | collective-permute-start | bytes 196616 | tf_op jit(solution)/shard_map/ppermute | solution.py:31
  83.5 1.2 %reshape.31 = f32[6,12,2,1024]{3,2,1,0:T(2,128)} reshape(f32[144,1024]{1,0:T(8,128)S(1)} %pad_maximum_fusion) | data formatting | bytes 1179648 | tf_op jit(solution)/shard_map/reshape | solution.py:474
  85.5 2.7 %collective-permute-done.21.c = bf16[32,1024]{1,0:T(8,128)(2,1)S(1)} collective-permute-done((bf16[32,1024]{1,0:T(8,128)(2,1)S(1)}, bf16[32,1024]{1,0:T(8,128)(2,1)S(1)}, u32[]{:S(2)}, u32[]{:S(2)}) %collective-permute-start.21) | collective-permute-done | bytes 65568 | tf_op jit(solution)/shard_map/ppermute | solution.py:31
  88.2 1.1 %collective-permute-done.22.d = bf16[32,1024]{1,0:T(8,128)(2,1)S(1)} collective-permute-done((bf16[32,1024]{1,0:T(8,128)(2,1)S(1)}, bf16[32,1024]{1,0:T(8,128)(2,1)S(1)}, u32[]{:S(2)}, u32[]{:S(2)}) %collective-permute-start.22) | collective-permute-done | bytes 65568 | tf_op jit(solution)/shard_map/ppermute | solution.py:31
  (72 shorter events, 11.5 us)
Async XLA Ops:
  3.5 20.2 %copy-start = (bf16[3,1024,256]{2,1,0:T(8,128)(2,1)S(1)}, bf16[3,1024,256]{2,1,0:T(8,128)(2,1)}, u32[]{:S(2)}) copy-start(bf16[3,1024,256]{2,1,0:T(8,128)(2,1)} %weight.1) | copy-start | bytes 4718596
  4.8 15.0 %collective-permute-start = (bf16[152,1024]{1,0:T(8,128)(2,1)S(1)}, bf16[152,1024]{1,0:T(8,128)(2,1)S(1)}, u32[]{:S(2)}, u32[]{:S(2)}) collective-permute-start(bf16[152,1024]{1,0:T(8,128)(2,1)S(1)} %pad_maximum_fusion.2), channel_id=1, source_target_pairs={{0,252},{4,0},{8,4},{12,8},{16,12},{20,16},{24,20},{28,24},{32,28}... | collective-permute-start | bytes 933896 | tf_op jit(solution)/shard_map/ppermute | solution.py:31
  13.3 10.4 %collective-permute-start.3 = (bf16[152,1024]{1,0:T(8,128)(2,1)S(1)}, bf16[152,1024]{1,0:T(8,128)(2,1)S(1)}, u32[]{:S(2)}, u32[]{:S(2)}) collective-permute-start(bf16[152,1024]{1,0:T(8,128)(2,1)S(1)} %pad_maximum_fusion.1.m0.refs_0_), channel_id=1, source_target_pairs={{0,2},{1,3},{2,0},{3,1},{4,6},{5,7},{6,4},{7,5},{8,10},{9,11},{10,... | collective-permute-start | bytes 933896 | tf_op jit(solution)/shard_map/ppermute | solution.py:31
  15.8 7.9 %collective-permute-start.1 = (bf16[152,1024]{1,0:T(8,128)(2,1)S(1)}, bf16[152,1024]{1,0:T(8,128)(2,1)S(1)}, u32[]{:S(2)}, u32[]{:S(2)}) collective-permute-start(bf16[152,1024]{1,0:T(8,128)(2,1)S(1)} %pad_maximum_fusion.1.m0.refs_0_), channel_id=1, source_target_pairs={{0,1},{1,0},{2,3},{3,2},{4,5},{5,4},{6,7},{7,6},{8,9},{9,8},{10,11... | collective-permute-start | bytes 933896 | tf_op jit(solution)/shard_map/ppermute | solution.py:31
  19.8 3.9 %collective-permute-start.2 = (bf16[152,1024]{1,0:T(8,128)(2,1)S(1)}, bf16[152,1024]{1,0:T(8,128)(2,1)S(1)}, u32[]{:S(2)}, u32[]{:S(2)}) collective-permute-start(bf16[152,1024]{1,0:T(8,128)(2,1)S(1)} %collective-permute-done.m1.refs_1_), channel_id=1, source_target_pairs={{0,1},{1,0},{2,3},{3,2},{4,5},{5,4},{6,7},{7,6},{8,9},{9,8},{10,11... | collective-permute-start | bytes 933896 | tf_op jit(solution)/shard_map/ppermute | solution.py:31
  19.8 11.3 %collective-permute-start.4 = (bf16[152,1024]{1,0:T(8,128)(2,1)S(1)}, bf16[152,1024]{1,0:T(8,128)(2,1)S(1)}, u32[]{:S(2)}, u32[]{:S(2)}) collective-permute-start(bf16[152,1024]{1,0:T(8,128)(2,1)S(1)} %collective-permute-done.m1.refs_1_), channel_id=1, source_target_pairs={{0,2},{1,3},{2,0},{3,1},{4,6},{5,7},{6,4},{7,5},{8,10},{9,11},{10,... | collective-permute-start | bytes 933896 | tf_op jit(solution)/shard_map/ppermute | solution.py:31
  23.7 7.4 %collective-permute-start.5 = (bf16[152,1024]{1,0:T(8,128)(2,1)S(1)}, bf16[152,1024]{1,0:T(8,128)(2,1)S(1)}, u32[]{:S(2)}, u32[]{:S(2)}) collective-permute-start(bf16[152,1024]{1,0:T(8,128)(2,1)S(1)} %collective-permute-done.3.refs_4_), channel_id=1, source_target_pairs={{0,1},{1,0},{2,3},{3,2},{4,5},{5,4},{6,7},{7,6},{8,9},{9,8},{10,11... | collective-permute-start | bytes 933896 | tf_op jit(solution)/shard_map/ppermute | solution.py:31
  31.1 1.6 %collective-permute-start.6 = (bf16[152,1024]{1,0:T(8,128)(2,1)S(1)}, bf16[152,1024]{1,0:T(8,128)(2,1)S(1)}, u32[]{:S(2)}, u32[]{:S(2)}) collective-permute-start(bf16[152,1024]{1,0:T(8,128)(2,1)S(1)} %collective-permute-done.4.refs_5_), channel_id=1, source_target_pairs={{0,1},{1,0},{2,3},{3,2},{4,5},{5,4},{6,7},{7,6},{8,9},{9,8},{10,11... | collective-permute-start | bytes 933896 | tf_op jit(solution)/shard_map/ppermute | solution.py:31
  41.5 3.5 %collective-permute-start.14 = (bf16[288,1024]{1,0:T(8,128)(2,1)S(1)}, bf16[288,1024]{1,0:T(8,128)(2,1)S(1)}, u32[]{:S(2)}, u32[]{:S(2)}) collective-permute-start(bf16[288,1024]{1,0:T(8,128)(2,1)S(1)} %get-tuple-element.94), channel_id=1, source_target_pairs={{0,1},{1,0},{2,3},{3,2},{4,5},{5,4},{6,7},{7,6},{8,9},{9,8},{10,11... | collective-permute-start | bytes 1769480 | tf_op jit(solution)/shard_map/ppermute | solution.py:31
  41.7 19.7 %collective-permute-start.7 = (bf16[272,640]{1,0:T(8,128)(2,1)S(1)}, bf16[272,640]{1,0:T(8,128)(2,1)S(1)}, u32[]{:S(2)}, u32[]{:S(2)}) collective-permute-start(bf16[272,640]{1,0:T(8,128)(2,1)S(1)} %get-tuple-element.83), channel_id=1, source_target_pairs={{0,32},{4,36},{8,40},{12,44},{16,48},{20,52},{24,56},{28,60},{32,6... | collective-permute-start | bytes 1044488 | tf_op jit(solution)/shard_map/ppermute | solution.py:31
  41.7 19.7 %collective-permute-start.8 = (bf16[272,640]{1,0:T(8,128)(2,1)S(1)}, bf16[272,640]{1,0:T(8,128)(2,1)S(1)}, u32[]{:S(2)}, u32[]{:S(2)}) collective-permute-start(bf16[272,640]{1,0:T(8,128)(2,1)S(1)} %get-tuple-element.84), channel_id=1, source_target_pairs={{0,64},{4,68},{8,72},{12,76},{16,80},{20,84},{24,88},{28,92},{32,9... | collective-permute-start | bytes 1044488 | tf_op jit(solution)/shard_map/ppermute | solution.py:31
  43.9 18.2 %collective-permute-start.9 = (bf16[272,640]{1,0:T(8,128)(2,1)S(1)}, bf16[272,640]{1,0:T(8,128)(2,1)S(1)}, u32[]{:S(2)}, u32[]{:S(2)}) collective-permute-start(bf16[272,640]{1,0:T(8,128)(2,1)S(1)} %get-tuple-element.85), channel_id=1, source_target_pairs={{0,96},{4,100},{8,104},{12,108},{16,112},{20,116},{24,120},{28,124... | collective-permute-start | bytes 1044488 | tf_op jit(solution)/shard_map/ppermute | solution.py:31
  45.0 10.8 %collective-permute-start.10 = (bf16[512,384]{1,0:T(8,128)(2,1)S(1)}, bf16[512,384]{1,0:T(8,128)(2,1)S(1)}, u32[]{:S(2)}, u32[]{:S(2)}) collective-permute-start(bf16[512,384]{1,0:T(8,128)(2,1)S(1)} %get-tuple-element.87), channel_id=1, source_target_pairs={{0,4},{4,0},{8,12},{12,8},{16,20},{20,16},{24,28},{28,24},{32,36},... | collective-permute-start | bytes 1179656 | tf_op jit(solution)/shard_map/ppermute | solution.py:31
  45.1 22.4 %collective-permute-start.15 = (bf16[144,1024]{1,0:T(8,128)(2,1)S(1)}, bf16[144,1024]{1,0:T(8,128)(2,1)S(1)}, u32[]{:S(2)}, u32[]{:S(2)}) collective-permute-start(bf16[144,1024]{1,0:T(8,128)(2,1)S(1)} %add_convert_fusion), channel_id=1, source_target_pairs={{0,2},{1,3},{2,0},{3,1},{4,6},{5,7},{6,4},{7,5},{8,10},{9,11},{10,... | collective-permute-start | bytes 884744 | tf_op jit(solution)/shard_map/ppermute | solution.py:31
  55.9 7.0 %collective-permute-start.11 = (bf16[128,384]{1,0:T(8,128)(2,1)S(1)}, bf16[128,384]{1,0:T(8,128)(2,1)S(1)}, u32[]{:S(2)}, u32[]{:S(2)}) collective-permute-start(bf16[128,384]{1,0:T(8,128)(2,1)S(1)} %get-tuple-element.89), channel_id=1, source_target_pairs={{0,32},{4,36},{8,40},{12,44},{16,48},{20,52},{24,56},{28,60},{32,6... | collective-permute-start | bytes 294920 | tf_op jit(solution)/shard_map/ppermute | solution.py:31
  61.4 6.1 %collective-permute-start.12 = (bf16[128,384]{1,0:T(8,128)(2,1)S(1)}, bf16[128,384]{1,0:T(8,128)(2,1)S(1)}, u32[]{:S(2)}, u32[]{:S(2)}) collective-permute-start(bf16[128,384]{1,0:T(8,128)(2,1)S(1)} %get-tuple-element.90), channel_id=1, source_target_pairs={{0,64},{4,68},{8,72},{12,76},{16,80},{20,84},{24,88},{28,92},{32,9... | collective-permute-start | bytes 294920 | tf_op jit(solution)/shard_map/ppermute | solution.py:31
  61.4 6.1 %collective-permute-start.13 = (bf16[128,384]{1,0:T(8,128)(2,1)S(1)}, bf16[128,384]{1,0:T(8,128)(2,1)S(1)}, u32[]{:S(2)}, u32[]{:S(2)}) collective-permute-start(bf16[128,384]{1,0:T(8,128)(2,1)S(1)} %get-tuple-element.91), channel_id=1, source_target_pairs={{0,96},{4,100},{8,104},{12,108},{16,112},{20,116},{24,120},{28,124... | collective-permute-start | bytes 294920 | tf_op jit(solution)/shard_map/ppermute | solution.py:31
  67.9 11.0 %collective-permute-start.17 = (bf16[80,1024]{1,0:T(8,128)(2,1)S(1)}, bf16[80,1024]{1,0:T(8,128)(2,1)S(1)}, u32[]{:S(2)}, u32[]{:S(2)}) collective-permute-start(bf16[80,1024]{1,0:T(8,128)(2,1)S(1)} %get-tuple-element.107), channel_id=1, source_target_pairs={{0,128},{4,132},{8,136},{12,140},{16,144},{20,148},{24,152},{28,15... | collective-permute-start | bytes 491528 | tf_op jit(solution)/shard_map/ppermute | solution.py:31
  69.5 9.4 %collective-permute-start.19 = (bf16[72,1024]{1,0:T(8,128)(2,1)S(1)}, bf16[72,1024]{1,0:T(8,128)(2,1)S(1)}, u32[]{:S(2)}, u32[]{:S(2)}) collective-permute-start(bf16[72,1024]{1,0:T(8,128)(2,1)S(1)} %get-tuple-element.109), channel_id=1, source_target_pairs={{0,4},{4,8},{8,12},{12,16},{16,20},{20,24},{24,28},{28,32},{32,36}... | collective-permute-start | bytes 442376 | tf_op jit(solution)/shard_map/ppermute | solution.py:31
  69.5 4.7 %collective-permute-start.16 = (bf16[80,640]{1,0:T(8,128)(2,1)S(1)}, bf16[80,640]{1,0:T(8,128)(2,1)S(1)}, u32[]{:S(2)}, u32[]{:S(2)}) collective-permute-start(bf16[80,640]{1,0:T(8,128)(2,1)S(1)} %get-tuple-element.106), channel_id=1, source_target_pairs={{0,4},{4,0},{8,12},{12,8},{16,20},{20,16},{24,28},{28,24},{32,36},... | collective-permute-start | bytes 307208 | tf_op jit(solution)/shard_map/ppermute | solution.py:31
  69.5 5.7 %collective-permute-start.18 = (bf16[80,640]{1,0:T(8,128)(2,1)S(1)}, bf16[80,640]{1,0:T(8,128)(2,1)S(1)}, u32[]{:S(2)}, u32[]{:S(2)}) collective-permute-start(bf16[80,640]{1,0:T(8,128)(2,1)S(1)} %get-tuple-element.108), channel_id=1, source_target_pairs={{0,132},{4,128},{8,140},{12,136},{16,148},{20,144},{24,156},{28,15... | collective-permute-start | bytes 307208 | tf_op jit(solution)/shard_map/ppermute | solution.py:31
  79.1 6.4 %collective-permute-start.20 = (bf16[32,1024]{1,0:T(8,128)(2,1)S(1)}, bf16[32,1024]{1,0:T(8,128)(2,1)S(1)}, u32[]{:S(2)}, u32[]{:S(2)}) collective-permute-start(bf16[32,1024]{1,0:T(8,128)(2,1)S(1)} %get-tuple-element.115), channel_id=1, source_target_pairs={{0,8},{4,12},{8,16},{12,20},{16,24},{20,28},{24,0},{28,4},{32,40},... | collective-permute-start | bytes 196616 | tf_op jit(solution)/shard_map/ppermute | solution.py:31
  79.1 9.1 %collective-permute-start.21 = (bf16[32,1024]{1,0:T(8,128)(2,1)S(1)}, bf16[32,1024]{1,0:T(8,128)(2,1)S(1)}, u32[]{:S(2)}, u32[]{:S(2)}) collective-permute-start(bf16[32,1024]{1,0:T(8,128)(2,1)S(1)} %get-tuple-element.116), channel_id=1, source_target_pairs={{0,16},{4,20},{8,24},{12,28},{16,0},{20,4},{24,8},{28,12},{32,48},... | collective-permute-start | bytes 196616 | tf_op jit(solution)/shard_map/ppermute | solution.py:31
  83.4 5.9 %collective-permute-start.22 = (bf16[32,1024]{1,0:T(8,128)(2,1)S(1)}, bf16[32,1024]{1,0:T(8,128)(2,1)S(1)}, u32[]{:S(2)}, u32[]{:S(2)}) collective-permute-start(bf16[32,1024]{1,0:T(8,128)(2,1)S(1)} %get-tuple-element.117), channel_id=1, source_target_pairs={{0,24},{4,28},{8,0},{12,4},{16,8},{20,12},{24,16},{28,20},{32,56},... | collective-permute-start | bytes 196616 | tf_op jit(solution)/shard_map/ppermute | solution.py:31
  (7 other events, 60.4 us)

commit v6 on v5

--- a/solution.py
+++ b/solution.py
@@ -178,10 +178,50 @@
     return y.astype(BF16)
 
 
-def early_kernel(m0, m1, m2, m3, weight, wo, proj, tall, gall):
-    stacked((m0, m1, m2, m3), tall, gall)
+def attended(marks, q, k, v, d, bias):
+    same = lax.dot_general(marks, marks, TN, preferred_element_type=F32)[:WT, :WT] > 0.5
+    same = jnp.where(same, 0.0, -jnp.inf)
+    q = by_head(q * jnp.asarray(0.125, BF16))
+    d = by_head(d)
+    s = lax.dot_general(q, k, NT, preferred_element_type=F32).reshape(HEADS, WT, WT)
+    dp = lax.dot_general(d, v, NT, preferred_element_type=F32).reshape(HEADS, WT, WT)
+    s = s + bias + same[None]
+    e = jnp.exp(s - jnp.max(s, axis=2, keepdims=True))
+    pr = e * (1.0 / jnp.sum(e, axis=2, keepdims=True))
+    ds = pr * (dp - jnp.sum(pr * dp, axis=2, keepdims=True))
+    prb = pr.astype(BF16).reshape(HEADS * WT, WT)
+    dsb = ds.astype(BF16).reshape(HEADS * WT, WT)
+    dq = own_columns(jnp.dot(dsb, k, preferred_element_type=F32)) * 0.125
+    dk = lax.dot_general(dsb, q, TN, preferred_element_type=F32)
+    dv = lax.dot_general(prb, d, TN, preferred_element_type=F32)
+    return (dq, dk, dv, own_columns(jnp.dot(prb, v, preferred_element_type=F32))), ds
+
+
+def marked(pieces, p):
+    return sum(pieces[2 * p + r][64:80, :WIDTH].astype(F32)[8:16] for r in range(2))
+
+
+def early_kernel(m0, m1, m2, m3, weight, wo, bias, proj, done, sums, tall, gall, rows, win):
+    pieces = (m0, m1, m2, m3)
+    stacked(pieces, tall, gall)
+    odd = lax.bitwise_and(lax.axis_index("head"), 1)
+    first = eastern(WIDTH)
     for m in range(4):
-        proj[m] = projected(m, tall, gall, weight, wo)
+        y = projected(m, tall, gall, weight, wo)
+        proj[m] = y
+        rows[...] = y.astype(F32)
+        for r in range(2):
+            a = rows[pl.ds(pl.multiple_of(odd * 160 + r * ROWS, 8), 72), :]
+            b = rows[pl.ds(pl.multiple_of(160 - odd * 160 + r * ROWS, 8), 72), :]
+            win[m, r * 72 : (r + 1) * 72, :] = jnp.where(first, b, a)
+    here, there = marked(pieces, 0), marked(pieces, 1)
+    here, there = jnp.where(odd == 1, there, here), jnp.where(odd == 1, here, there)
+    row = lax.broadcasted_iota(jnp.int32, (8, WIDTH), 0)
+    marks = jnp.where(row < 4, here + pltpu.roll(there, 4, 0), 0.0).astype(BF16)
+    results, ds = attended(marks, *(win[m].astype(BF16) for m in range(4)), bias[...])
+    for m in range(4):
+        done[m] = results[m]
+    sums[...] = ds
 
 
 def segment_sums(sums, highs, lows):
@@ -213,16 +253,16 @@
 
 def band_kernel(*refs):
     pieces = refs[:8]
-    weight, wo, bias, early, high_rows, low_rows, grads = refs[8:15]
-    ways, pairs = refs[15:19], refs[19:21]
-    tall, gall, qkv, rows, wins, outs, sums, att, labels, full = refs[21:]
+    weight, wo, bias, early, done, early_sums, high_rows, low_rows, grads = refs[8:17]
+    ways, pairs = refs[17:21], refs[21:23]
+    tall, gall, qkv, rows, wins, outs, sums, att, labels, full = refs[23:]
     own = lax.axis_index("head")
     labels[...] = jnp.zeros_like(labels)
     row = lax.broadcasted_iota(jnp.int32, (8, WIDTH), 0)
     for p in range(4):
         shard = lax.bitwise_xor(own, p)
         before = lax.rem(shard + 3, 4)
-        marks = sum(pieces[2 * p + r][64:80, :WIDTH].astype(F32)[8:16] for r in range(2))
+        marks = marked(pieces, p)
         labels[shard] += jnp.where(row < 4, marks, 0.0)
         labels[before] += jnp.where(row < 4, pltpu.roll(marks, 4, 0), 0.0)
     stacked(pieces[:4], tall.at[:HALF, :], gall.at[:HALF, :])
@@ -233,27 +273,17 @@
         to_windows(rows, wins, own)
         if m < 3:
             qkv[m] = wins[...].astype(BF16)
-    for w in range(4):
+    near = lax.bitwise_and(own, 2)
+    for m in range(4):
+        outs[m, near] = done[m]
+    sums[...] = early_sums[...]
+    for i in range(1, 4):
+        w = lax.rem(near + i, 4)
         marks = labels[w].astype(BF16)
-        same = lax.dot_general(marks, marks, TN, preferred_element_type=F32)[:WT, :WT] > 0.5
-        same = jnp.where(same, 0.0, -jnp.inf)
-        q = by_head(qkv[0, w] * jnp.asarray(0.125, BF16))
-        k = qkv[1, w]
-        v = qkv[2, w]
-        d = by_head(wins[w].astype(BF16))
-        s = lax.dot_general(q, k, NT, preferred_element_type=F32).reshape(HEADS, WT, WT)
-        dp = lax.dot_general(d, v, NT, preferred_element_type=F32).reshape(HEADS, WT, WT)
-        s = s + bias[...] + same[None]
-        e = jnp.exp(s - jnp.max(s, axis=2, keepdims=True))
-        pr = e * (1.0 / jnp.sum(e, axis=2, keepdims=True))
-        ds = pr * (dp - jnp.sum(pr * dp, axis=2, keepdims=True))
-        sums[...] = ds if w == 0 else sums[...] + ds
-        prb = pr.astype(BF16).reshape(HEADS * WT, WT)
-        dsb = ds.astype(BF16).reshape(HEADS * WT, WT)
-        outs[0, w] = own_columns(jnp.dot(dsb, k, preferred_element_type=F32)) * 0.125
-        outs[1, w] = lax.dot_general(dsb, q, TN, preferred_element_type=F32)
-        outs[2, w] = lax.dot_general(prb, d, TN, preferred_element_type=F32)
-        outs[3, w] = own_columns(jnp.dot(prb, v, preferred_element_type=F32))
+        results, ds = attended(marks, qkv[0, w], qkv[1, w], qkv[2, w], wins[w].astype(BF16), bias[...])
+        sums[...] += ds
+        for m in range(4):
+            outs[m, w] = results[m]
     for m in range(4):
         from_windows(outs.at[m], rows, own)
         if m < 3:
@@ -388,7 +418,7 @@
         in_specs=[pl.BlockSpec(memory_space=pl.ANY)] * 3,
         out_specs=[pl.BlockSpec(memory_space=pltpu.VMEM)] * 3,
         scratch_shapes=[pltpu.SemaphoreType.DMA((3,))],
-        compiler_params=pltpu.CompilerParams(vmem_limit_bytes=8 * 2**20),
+        compiler_params=pltpu.CompilerParams(vmem_limit_bytes=56 * 2**20),
     )(*inputs)
 
     def message(r):
@@ -413,15 +443,20 @@
     far_low = across(low)
     near = (high, low, core(high), core(low))
 
-    early = call(
+    early, done, sums = call(
         early_kernel,
-        shape((4, HALF, WIDTH), BF16),
-        [pltpu.VMEM((HALF, D), BF16), pltpu.VMEM((HALF, D), BF16)],
+        (shape((4, HALF, WIDTH), BF16), shape((4, WT, WIDTH), F32), shape((HEADS, WT, WT), F32)),
+        [
+            pltpu.VMEM((HALF, D), BF16),
+            pltpu.VMEM((HALF, D), BF16),
+            pltpu.VMEM((HALF, WIDTH), F32),
+            pltpu.VMEM((4, WT, WIDTH), F32),
+        ],
         10**9,
         5 * 10**6,
-        8,
-    )(*near, qkv_weight, out_weight)
-    far_low, early = lax.optimization_barrier((far_low, early))
+        16,
+    )(*near, qkv_weight, out_weight, bias)
+    far_low, early, done, sums = lax.optimization_barrier((far_low, early, done, sums))
     far = (far_high, far_low, core(far_high), core(far_low))
 
     grads, *blocks = call(
@@ -444,7 +479,7 @@
         3 * 10**9,
         10**7,
         24,
-    )(*near, *far, qkv_weight, out_weight, bias, early, high_rows, low_rows)
+    )(*near, *far, qkv_weight, out_weight, bias, early, done, sums, high_rows, low_rows)
 
     def by_y(parts):
         far = sent(parts[2], "lat", moved(0, 2, 0))

time: 90.9 us -> 91.6 us (level)
  Pallas kernels: 13.5 us -> 15.6 us
    unnamed x16 -> x10, local copies, waits for them, and re-layouts: 2.63 us -> 0.03 us
    pallas_call x1, Pallas kernels: 0.15 us -> 1.93 us  [shards(): pl.pallas_call(load_kernel, out_shape=[shape(x.shape, x.dtype) for x in i...]
    slice x1, local copies, waits for them, and re-layouts: 0.49 us -> 1.68 us  [message(): t, g = (x[rows].reshape(72, D) for x in loaded[:2])]
    pallas_call x1, Pallas kernels: 0.84 us -> 1.85 us  [shards(): call(early_kernel, (shape((4, HALF, WIDTH), BF16), shape((4, WT, WIDTH),...]
  transfers between devices with their start and end apart: 23 -> 23, of which waited for: 15 -> 15; matrix products, arithmetic and copies ran while one was open for 2% -> 2% of each run, Pallas kernels for 3% -> 5%
where the time goes in v6:
time: 91.6 us; the launch traced here: 90.9 us
  waiting for transfers between devices  41.5 us (45%)
  starting transfers between devices  28.2 us (31%)
  Pallas kernels  15.6 us (17%)
  local copies, waits for them, and re-layouts  4.27 us (5%)
    ppermute x23, waiting for transfers between devices, sent(): return lax.ppermute(x, axis, [(i, to(i)) for i in range(size)])  41.5 us
    ppermute x23, starting transfers between devices, sent(): return lax.ppermute(x, axis, [(i, to(i)) for i in range(size)])  28.2 us
    pallas_call x1, Pallas kernels, shards(): call(band_kernel, (shape((ALL, 3 * WIDTH), BF16),) + (shape((272, 640), B...  6.98 us
    pallas_call x1, Pallas kernels, shards(): call(bias_kernel, (shape((HEADS, WT, WT), F32), shape((88, 16, 256), BF16...  2.14 us
    pallas_call x1, Pallas kernels, shards(): pl.pallas_call(load_kernel, out_shape=[shape(x.shape, x.dtype) for x in i...  1.93 us
    pallas_call x1, Pallas kernels, shards(): call(early_kernel, (shape((4, HALF, WIDTH), BF16), shape((4, WT, WIDTH),...  1.85 us
  transfers between devices with their start and end apart: 23, of which 15 were waited for; matrix products, arithmetic and copies ran while one was open for 2% of the time, Pallas kernels for 5%

profile of v6, /device:TPU:2, one launch (start us, length us, event | category | flops | bytes accessed | tf_op | source)
XLA Modules:
  0.0 90.9 jit_solution(2329534899138568587)
XLA Ops:
  0.7 1.9 %shard_map.111 = (bf16[6,12,2,1024]{3,2,1,0:T(2,128)(2,1)}, bf16[6,12,2,1024]{3,2,1,0:T(2,128)(2,1)}, s32[6,2,12]{2,1,0:T(2,128)}) custom-call(bf16[6,12,2,1024]{3,2,1,0:T(2,128)(2,1)} %bitcast.11, bf16[6,12,2,1024]{3,2,1,0:T(2,128)(2,1)} %bitcast.12, s32[6,2,12]{2,1,0:T(2,128)} %refs_2_.1), custom_call_target="tpu_custom_call" | custom-call | tf_op jit(solution)/shard_map/pallas_call | solution.py:415
  2.7 1.7 %fusion.3 = (bf16[3,12,2,1024]{3,2,1,0:T(2,128)(2,1)S(1)}, bf16[3,12,2,1024]{3,2,1,0:T(2,128)(2,1)S(1)}, bf16[3,12,2,1024]{3,2,1,0:T(2,128)(2,1)S(1)}, bf16[3,12,2,1024]{3,2,1,0:T(2,128)(2,1)S(1)}) fusion(bf16[6,12,2,1024]{3,2,1,0:T(2,128)(2,1)} %get-tuple-element.71, bf16[6,12,2,1024]{3,2,1,0:T(2,128)(2,1)} %get-tuple-element.73), kind=kLoop, calls=%fused_computation.21 | loop fusion | bytes 1179648 | tf_op jit(solution)/shard_map/slice | solution.py:426
  5.8 8.4 %collective-permute-start = (bf16[152,1024]{1,0:T(8,128)(2,1)S(1)}, bf16[152,1024]{1,0:T(8,128)(2,1)S(1)}, u32[]{:S(2)}, u32[]{:S(2)}) collective-permute-start(bf16[152,1024]{1,0:T(8,128)(2,1)S(1)} %pad_maximum_fusion.2), channel_id=1, source_target_pairs={{0,252},{4,0},{8,4},{12,8},{16,12},{20,16},{24,20},{28,24},{32,28}... | collective-permute-start | bytes 933896 | tf_op jit(solution)/shard_map/ppermute | solution.py:31
  14.4 2.5 %collective-permute-start.3 = (bf16[152,1024]{1,0:T(8,128)(2,1)S(1)}, bf16[152,1024]{1,0:T(8,128)(2,1)S(1)}, u32[]{:S(2)}, u32[]{:S(2)}) collective-permute-start(bf16[152,1024]{1,0:T(8,128)(2,1)S(1)} %pad_maximum_fusion.1.m0.refs_0_), channel_id=1, source_target_pairs={{0,2},{1,3},{2,0},{3,1},{4,6},{5,7},{6,4},{7,5},{8,10},{9,11},{10,... | collective-permute-start | bytes 933896 | tf_op jit(solution)/shard_map/ppermute | solution.py:31
  16.9 2.1 %shard_map.112 = (f32[4,144,144]{2,1,0:T(8,128)S(1)}, bf16[88,16,256]{2,1,0:T(8,128)(2,1)S(1)}, bf16[88,48,256]{2,1,0:T(8,128)(2,1)S(1)}) custom-call(f32[4,768]{1,0:T(4,128)S(1)} %pad.22.table, s32[144,144]{1,0:T(8,128)S(1)} %copy-done.2, bf16[144,144]{1,0:T(8,128)(2,1)S(1)} %copy-done.3), custom_call_target="tpu_custom_call" | custom-call | flops 100000000 | bytes 4000000 | tf_op jit(solution)/shard_map/pallas_call | solution.py:435
  19.0 1.8 %collective-permute-done.m1.refs_1_ = bf16[152,1024]{1,0:T(8,128)(2,1)S(1)} collective-permute-done((bf16[152,1024]{1,0:T(8,128)(2,1)S(1)}, bf16[152,1024]{1,0:T(8,128)(2,1)S(1)}, u32[]{:S(2)}, u32[]{:S(2)}) %collective-permute-start) | collective-permute-done | bytes 311328 | tf_op jit(solution)/shard_map/ppermute | solution.py:31
  20.9 2.4 %collective-permute-start.4 = (bf16[152,1024]{1,0:T(8,128)(2,1)S(1)}, bf16[152,1024]{1,0:T(8,128)(2,1)S(1)}, u32[]{:S(2)}, u32[]{:S(2)}) collective-permute-start(bf16[152,1024]{1,0:T(8,128)(2,1)S(1)} %collective-permute-done.m1.refs_1_), channel_id=1, source_target_pairs={{0,2},{1,3},{2,0},{3,1},{4,6},{5,7},{6,4},{7,5},{8,10},{9,11},{10,... | collective-permute-start | bytes 933896 | tf_op jit(solution)/shard_map/ppermute | solution.py:31
  23.3 1.5 %collective-permute-done.3.refs_4_ = bf16[152,1024]{1,0:T(8,128)(2,1)S(1)} collective-permute-done((bf16[152,1024]{1,0:T(8,128)(2,1)S(1)}, bf16[152,1024]{1,0:T(8,128)(2,1)S(1)}, u32[]{:S(2)}, u32[]{:S(2)}) %collective-permute-start.3) | collective-permute-done | bytes 311328 | tf_op jit(solution)/shard_map/ppermute | solution.py:31
  24.8 1.8 %shard_map.113 = (bf16[4,320,256]{2,1,0:T(8,128)(2,1)S(1)}, f32[4,144,256]{2,1,0:T(8,128)S(1)}, f32[4,144,144]{2,1,0:T(8,128)S(1)}) custom-call(bf16[152,1024]{1,0:T(8,128)(2,1)S(1)} %pad_maximum_fusion.1.m0.refs_0_, bf16[152,1024]{1,0:T(8,128)(2,1)S(1)} %collective-permute-done.m1.refs_1_, bf16[152,1024]{1,0:T(8,128)(2,1)S(1)} %collective-permute-done.1.m2.refs_2_, ...), custom_call_target="tpu_custom_call" | custom-call | flops 1000000000 | bytes 5000000 | tf_op jit(solution)/shard_map/pallas_call | solution.py:446
  26.7 5.5 %collective-permute-done.4.refs_5_ = bf16[152,1024]{1,0:T(8,128)(2,1)S(1)} collective-permute-done((bf16[152,1024]{1,0:T(8,128)(2,1)S(1)}, bf16[152,1024]{1,0:T(8,128)(2,1)S(1)}, u32[]{:S(2)}, u32[]{:S(2)}) %collective-permute-start.4) | collective-permute-done | bytes 311328 | tf_op jit(solution)/shard_map/ppermute | solution.py:31
  32.1 1.6 %collective-permute-done.6.refs_7_ = bf16[152,1024]{1,0:T(8,128)(2,1)S(1)} collective-permute-done((bf16[152,1024]{1,0:T(8,128)(2,1)S(1)}, bf16[152,1024]{1,0:T(8,128)(2,1)S(1)}, u32[]{:S(2)}, u32[]{:S(2)}) %collective-permute-start.6) | collective-permute-done | bytes 311328 | tf_op jit(solution)/shard_map/ppermute | solution.py:31
  33.7 7.0 %shard_map.114 = (bf16[640,768]{1,0:T(8,128)(2,1)S(1)}, bf16[272,640]{1,0:T(8,128)(2,1)S(1)}, bf16[272,640]{1,0:T(8,128)(2,1)S(1)}, bf16[272,640]{1,0:T(8,128)(2...) custom-call(bf16[152,1024]{1,0:T(8,128)(2,1)S(1)} %pad_maximum_fusion.1.m0.refs_0_, ...), custom_call_target="tpu_custom_call" | custom-call | flops 3000000000 | bytes 10000000 | tf_op jit(solution)/shard_map/pallas_call | solution.py:462
  42.2 2.2 %collective-permute-start.8 = (bf16[272,640]{1,0:T(8,128)(2,1)S(1)}, bf16[272,640]{1,0:T(8,128)(2,1)S(1)}, u32[]{:S(2)}, u32[]{:S(2)}) collective-permute-start(bf16[272,640]{1,0:T(8,128)(2,1)S(1)} %get-tuple-element.94), channel_id=1, source_target_pairs={{0,64},{4,68},{8,72},{12,76},{16,80},{20,84},{24,88},{28,92},{32,9... | collective-permute-start | bytes 1044488 | tf_op jit(solution)/shard_map/ppermute | solution.py:31
  45.5 2.5 %collective-permute-start.15 = (bf16[144,1024]{1,0:T(8,128)(2,1)S(1)}, bf16[144,1024]{1,0:T(8,128)(2,1)S(1)}, u32[]{:S(2)}, u32[]{:S(2)}) collective-permute-start(bf16[144,1024]{1,0:T(8,128)(2,1)S(1)} %add_convert_fusion), channel_id=1, source_target_pairs={{0,2},{1,3},{2,0},{3,1},{4,6},{5,7},{6,4},{7,5},{8,10},{9,11},{10,... | collective-permute-start | bytes 884744 | tf_op jit(solution)/shard_map/ppermute | solution.py:31
  48.0 8.2 %collective-permute-done.10.refs_1_ = bf16[512,384]{1,0:T(8,128)(2,1)S(1)} collective-permute-done((bf16[512,384]{1,0:T(8,128)(2,1)S(1)}, bf16[512,384]{1,0:T(8,128)(2,1)S(1)}, u32[]{:S(2)}, u32[]{:S(2)}) %collective-permute-start.10) | collective-permute-done | bytes 393248 | tf_op jit(solution)/shard_map/ppermute | solution.py:31
  57.3 4.5 %collective-permute-done.7.refs_1_ = bf16[272,640]{1,0:T(8,128)(2,1)S(1)} collective-permute-done((bf16[272,640]{1,0:T(8,128)(2,1)S(1)}, bf16[272,640]{1,0:T(8,128)(2,1)S(1)}, u32[]{:S(2)}, u32[]{:S(2)}) %collective-permute-start.7) | collective-permute-done | bytes 348192 | tf_op jit(solution)/shard_map/ppermute | solution.py:31
  63.4 4.6 %collective-permute-done.12.refs_6_ = bf16[128,384]{1,0:T(8,128)(2,1)S(1)} collective-permute-done((bf16[128,384]{1,0:T(8,128)(2,1)S(1)}, bf16[128,384]{1,0:T(8,128)(2,1)S(1)}, u32[]{:S(2)}, u32[]{:S(2)}) %collective-permute-start.12) | collective-permute-done | bytes 98336 | tf_op jit(solution)/shard_map/ppermute | solution.py:31
  68.4 1.6 %collective-permute-start.17 = (bf16[80,1024]{1,0:T(8,128)(2,1)S(1)}, bf16[80,1024]{1,0:T(8,128)(2,1)S(1)}, u32[]{:S(2)}, u32[]{:S(2)}) collective-permute-start(bf16[80,1024]{1,0:T(8,128)(2,1)S(1)} %get-tuple-element.117), channel_id=1, source_target_pairs={{0,128},{4,132},{8,136},{12,140},{16,144},{20,148},{24,152},{28,15... | collective-permute-start | bytes 491528 | tf_op jit(solution)/shard_map/ppermute | solution.py:31
  70.0 2.0 %collective-permute-start.18 = (bf16[80,640]{1,0:T(8,128)(2,1)S(1)}, bf16[80,640]{1,0:T(8,128)(2,1)S(1)}, u32[]{:S(2)}, u32[]{:S(2)}) collective-permute-start(bf16[80,640]{1,0:T(8,128)(2,1)S(1)} %get-tuple-element.118), channel_id=1, source_target_pairs={{0,132},{4,128},{8,140},{12,136},{16,148},{20,144},{24,156},{28,15... | collective-permute-start | bytes 307208 | tf_op jit(solution)/shard_map/ppermute | solution.py:31
  72.0 2.7 %collective-permute-done.16.b = bf16[80,640]{1,0:T(8,128)(2,1)S(1)} collective-permute-done((bf16[80,640]{1,0:T(8,128)(2,1)S(1)}, bf16[80,640]{1,0:T(8,128)(2,1)S(1)}, u32[]{:S(2)}, u32[]{:S(2)}) %collective-permute-start.16) | collective-permute-done | bytes 102432 | tf_op jit(solution)/shard_map/ppermute | solution.py:31
  75.7 3.6 %collective-permute-done.19 = bf16[72,1024]{1,0:T(8,128)(2,1)S(1)} collective-permute-done((bf16[72,1024]{1,0:T(8,128)(2,1)S(1)}, bf16[72,1024]{1,0:T(8,128)(2,1)S(1)}, u32[]{:S(2)}, u32[]{:S(2)}) %collective-permute-start.19) | collective-permute-done | bytes 147488 | tf_op jit(solution)/shard_map/ppermute | solution.py:31
  79.6 4.3 %collective-permute-start.21 = (bf16[32,1024]{1,0:T(8,128)(2,1)S(1)}, bf16[32,1024]{1,0:T(8,128)(2,1)S(1)}, u32[]{:S(2)}, u32[]{:S(2)}) collective-permute-start(bf16[32,1024]{1,0:T(8,128)(2,1)S(1)} %get-tuple-element.126), channel_id=1, source_target_pairs={{0,16},{4,20},{8,24},{12,28},{16,0},{20,4},{24,8},{28,12},{32,48},... | collective-permute-start | bytes 196616 | tf_op jit(solution)/shard_map/ppermute | solution.py:31
  86.0 2.7 %collective-permute-done.21.c = bf16[32,1024]{1,0:T(8,128)(2,1)S(1)} collective-permute-done((bf16[32,1024]{1,0:T(8,128)(2,1)S(1)}, bf16[32,1024]{1,0:T(8,128)(2,1)S(1)}, u32[]{:S(2)}, u32[]{:S(2)}) %collective-permute-start.21) | collective-permute-done | bytes 65568 | tf_op jit(solution)/shard_map/ppermute | solution.py:31
  88.7 1.4 %collective-permute-done.22.d = bf16[32,1024]{1,0:T(8,128)(2,1)S(1)} collective-permute-done((bf16[32,1024]{1,0:T(8,128)(2,1)S(1)}, bf16[32,1024]{1,0:T(8,128)(2,1)S(1)}, u32[]{:S(2)}, u32[]{:S(2)}) %collective-permute-start.22) | collective-permute-done | bytes 65568 | tf_op jit(solution)/shard_map/ppermute | solution.py:31
  (66 shorter events, 11.4 us)
Async XLA Ops:
  2.7 22.1 %copy-start = (bf16[3,1024,256]{2,1,0:T(8,128)(2,1)S(1)}, bf16[3,1024,256]{2,1,0:T(8,128)(2,1)}, u32[]{:S(2)}) copy-start(bf16[3,1024,256]{2,1,0:T(8,128)(2,1)} %weight.1) | copy-start | bytes 4718596
  5.8 15.0 %collective-permute-start = (bf16[152,1024]{1,0:T(8,128)(2,1)S(1)}, bf16[152,1024]{1,0:T(8,128)(2,1)S(1)}, u32[]{:S(2)}, u32[]{:S(2)}) collective-permute-start(bf16[152,1024]{1,0:T(8,128)(2,1)S(1)} %pad_maximum_fusion.2), channel_id=1, source_target_pairs={{0,252},{4,0},{8,4},{12,8},{16,12},{20,16},{24,20},{28,24},{32,28}... | collective-permute-start | bytes 933896 | tf_op jit(solution)/shard_map/ppermute | solution.py:31
  14.4 10.4 %collective-permute-start.3 = (bf16[152,1024]{1,0:T(8,128)(2,1)S(1)}, bf16[152,1024]{1,0:T(8,128)(2,1)S(1)}, u32[]{:S(2)}, u32[]{:S(2)}) collective-permute-start(bf16[152,1024]{1,0:T(8,128)(2,1)S(1)} %pad_maximum_fusion.1.m0.refs_0_), channel_id=1, source_target_pairs={{0,2},{1,3},{2,0},{3,1},{4,6},{5,7},{6,4},{7,5},{8,10},{9,11},{10,... | collective-permute-start | bytes 933896 | tf_op jit(solution)/shard_map/ppermute | solution.py:31
  16.9 7.9 %collective-permute-start.1 = (bf16[152,1024]{1,0:T(8,128)(2,1)S(1)}, bf16[152,1024]{1,0:T(8,128)(2,1)S(1)}, u32[]{:S(2)}, u32[]{:S(2)}) collective-permute-start(bf16[152,1024]{1,0:T(8,128)(2,1)S(1)} %pad_maximum_fusion.1.m0.refs_0_), channel_id=1, source_target_pairs={{0,1},{1,0},{2,3},{3,2},{4,5},{5,4},{6,7},{7,6},{8,9},{9,8},{10,11... | collective-permute-start | bytes 933896 | tf_op jit(solution)/shard_map/ppermute | solution.py:31
  20.8 3.9 %collective-permute-start.2 = (bf16[152,1024]{1,0:T(8,128)(2,1)S(1)}, bf16[152,1024]{1,0:T(8,128)(2,1)S(1)}, u32[]{:S(2)}, u32[]{:S(2)}) collective-permute-start(bf16[152,1024]{1,0:T(8,128)(2,1)S(1)} %collective-permute-done.m1.refs_1_), channel_id=1, source_target_pairs={{0,1},{1,0},{2,3},{3,2},{4,5},{5,4},{6,7},{7,6},{8,9},{9,8},{10,11... | collective-permute-start | bytes 933896 | tf_op jit(solution)/shard_map/ppermute | solution.py:31
  20.9 11.3 %collective-permute-start.4 = (bf16[152,1024]{1,0:T(8,128)(2,1)S(1)}, bf16[152,1024]{1,0:T(8,128)(2,1)S(1)}, u32[]{:S(2)}, u32[]{:S(2)}) collective-permute-start(bf16[152,1024]{1,0:T(8,128)(2,1)S(1)} %collective-permute-done.m1.refs_1_), channel_id=1, source_target_pairs={{0,2},{1,3},{2,0},{3,1},{4,6},{5,7},{6,4},{7,5},{8,10},{9,11},{10,... | collective-permute-start | bytes 933896 | tf_op jit(solution)/shard_map/ppermute | solution.py:31
  24.8 7.4 %collective-permute-start.5 = (bf16[152,1024]{1,0:T(8,128)(2,1)S(1)}, bf16[152,1024]{1,0:T(8,128)(2,1)S(1)}, u32[]{:S(2)}, u32[]{:S(2)}) collective-permute-start(bf16[152,1024]{1,0:T(8,128)(2,1)S(1)} %collective-permute-done.3.refs_4_), channel_id=1, source_target_pairs={{0,1},{1,0},{2,3},{3,2},{4,5},{5,4},{6,7},{7,6},{8,9},{9,8},{10,11... | collective-permute-start | bytes 933896 | tf_op jit(solution)/shard_map/ppermute | solution.py:31
  32.1 1.6 %collective-permute-start.6 = (bf16[152,1024]{1,0:T(8,128)(2,1)S(1)}, bf16[152,1024]{1,0:T(8,128)(2,1)S(1)}, u32[]{:S(2)}, u32[]{:S(2)}) collective-permute-start(bf16[152,1024]{1,0:T(8,128)(2,1)S(1)} %collective-permute-done.4.refs_5_), channel_id=1, source_target_pairs={{0,1},{1,0},{2,3},{3,2},{4,5},{5,4},{6,7},{7,6},{8,9},{9,8},{10,11... | collective-permute-start | bytes 933896 | tf_op jit(solution)/shard_map/ppermute | solution.py:31
  42.0 3.5 %collective-permute-start.14 = (bf16[288,1024]{1,0:T(8,128)(2,1)S(1)}, bf16[288,1024]{1,0:T(8,128)(2,1)S(1)}, u32[]{:S(2)}, u32[]{:S(2)}) collective-permute-start(bf16[288,1024]{1,0:T(8,128)(2,1)S(1)} %get-tuple-element.104), channel_id=1, source_target_pairs={{0,1},{1,0},{2,3},{3,2},{4,5},{5,4},{6,7},{7,6},{8,9},{9,8},{10,11... | collective-permute-start | bytes 1769480 | tf_op jit(solution)/shard_map/ppermute | solution.py:31
  42.2 19.7 %collective-permute-start.7 = (bf16[272,640]{1,0:T(8,128)(2,1)S(1)}, bf16[272,640]{1,0:T(8,128)(2,1)S(1)}, u32[]{:S(2)}, u32[]{:S(2)}) collective-permute-start(bf16[272,640]{1,0:T(8,128)(2,1)S(1)} %get-tuple-element.93), channel_id=1, source_target_pairs={{0,32},{4,36},{8,40},{12,44},{16,48},{20,52},{24,56},{28,60},{32,6... | collective-permute-start | bytes 1044488 | tf_op jit(solution)/shard_map/ppermute | solution.py:31
  42.2 19.7 %collective-permute-start.8 = (bf16[272,640]{1,0:T(8,128)(2,1)S(1)}, bf16[272,640]{1,0:T(8,128)(2,1)S(1)}, u32[]{:S(2)}, u32[]{:S(2)}) collective-permute-start(bf16[272,640]{1,0:T(8,128)(2,1)S(1)} %get-tuple-element.94), channel_id=1, source_target_pairs={{0,64},{4,68},{8,72},{12,76},{16,80},{20,84},{24,88},{28,92},{32,9... | collective-permute-start | bytes 1044488 | tf_op jit(solution)/shard_map/ppermute | solution.py:31
  44.4 18.2 %collective-permute-start.9 = (bf16[272,640]{1,0:T(8,128)(2,1)S(1)}, bf16[272,640]{1,0:T(8,128)(2,1)S(1)}, u32[]{:S(2)}, u32[]{:S(2)}) collective-permute-start(bf16[272,640]{1,0:T(8,128)(2,1)S(1)} %get-tuple-element.95), channel_id=1, source_target_pairs={{0,96},{4,100},{8,104},{12,108},{16,112},{20,116},{24,120},{28,124... | collective-permute-start | bytes 1044488 | tf_op jit(solution)/shard_map/ppermute | solution.py:31
  45.5 10.8 %collective-permute-start.10 = (bf16[512,384]{1,0:T(8,128)(2,1)S(1)}, bf16[512,384]{1,0:T(8,128)(2,1)S(1)}, u32[]{:S(2)}, u32[]{:S(2)}) collective-permute-start(bf16[512,384]{1,0:T(8,128)(2,1)S(1)} %get-tuple-element.97), channel_id=1, source_target_pairs={{0,4},{4,0},{8,12},{12,8},{16,20},{20,16},{24,28},{28,24},{32,36},... | collective-permute-start | bytes 1179656 | tf_op jit(solution)/shard_map/ppermute | solution.py:31
  45.5 22.4 %collective-permute-start.15 = (bf16[144,1024]{1,0:T(8,128)(2,1)S(1)}, bf16[144,1024]{1,0:T(8,128)(2,1)S(1)}, u32[]{:S(2)}, u32[]{:S(2)}) collective-permute-start(bf16[144,1024]{1,0:T(8,128)(2,1)S(1)} %add_convert_fusion), channel_id=1, source_target_pairs={{0,2},{1,3},{2,0},{3,1},{4,6},{5,7},{6,4},{7,5},{8,10},{9,11},{10,... | collective-permute-start | bytes 884744 | tf_op jit(solution)/shard_map/ppermute | solution.py:31
  56.4 7.0 %collective-permute-start.11 = (bf16[128,384]{1,0:T(8,128)(2,1)S(1)}, bf16[128,384]{1,0:T(8,128)(2,1)S(1)}, u32[]{:S(2)}, u32[]{:S(2)}) collective-permute-start(bf16[128,384]{1,0:T(8,128)(2,1)S(1)} %get-tuple-element.99), channel_id=1, source_target_pairs={{0,32},{4,36},{8,40},{12,44},{16,48},{20,52},{24,56},{28,60},{32,6... | collective-permute-start | bytes 294920 | tf_op jit(solution)/shard_map/ppermute | solution.py:31
  61.8 6.1 %collective-permute-start.12 = (bf16[128,384]{1,0:T(8,128)(2,1)S(1)}, bf16[128,384]{1,0:T(8,128)(2,1)S(1)}, u32[]{:S(2)}, u32[]{:S(2)}) collective-permute-start(bf16[128,384]{1,0:T(8,128)(2,1)S(1)} %get-tuple-element.100), channel_id=1, source_target_pairs={{0,64},{4,68},{8,72},{12,76},{16,80},{20,84},{24,88},{28,92},{32,9... | collective-permute-start | bytes 294920 | tf_op jit(solution)/shard_map/ppermute | solution.py:31
  61.8 6.1 %collective-permute-start.13 = (bf16[128,384]{1,0:T(8,128)(2,1)S(1)}, bf16[128,384]{1,0:T(8,128)(2,1)S(1)}, u32[]{:S(2)}, u32[]{:S(2)}) collective-permute-start(bf16[128,384]{1,0:T(8,128)(2,1)S(1)} %get-tuple-element.101), channel_id=1, source_target_pairs={{0,96},{4,100},{8,104},{12,108},{16,112},{20,116},{24,120},{28,124... | collective-permute-start | bytes 294920 | tf_op jit(solution)/shard_map/ppermute | solution.py:31
  68.4 10.9 %collective-permute-start.17 = (bf16[80,1024]{1,0:T(8,128)(2,1)S(1)}, bf16[80,1024]{1,0:T(8,128)(2,1)S(1)}, u32[]{:S(2)}, u32[]{:S(2)}) collective-permute-start(bf16[80,1024]{1,0:T(8,128)(2,1)S(1)} %get-tuple-element.117), channel_id=1, source_target_pairs={{0,128},{4,132},{8,136},{12,140},{16,144},{20,148},{24,152},{28,15... | collective-permute-start | bytes 491528 | tf_op jit(solution)/shard_map/ppermute | solution.py:31
  70.0 9.4 %collective-permute-start.19 = (bf16[72,1024]{1,0:T(8,128)(2,1)S(1)}, bf16[72,1024]{1,0:T(8,128)(2,1)S(1)}, u32[]{:S(2)}, u32[]{:S(2)}) collective-permute-start(bf16[72,1024]{1,0:T(8,128)(2,1)S(1)} %get-tuple-element.119), channel_id=1, source_target_pairs={{0,4},{4,8},{8,12},{12,16},{16,20},{20,24},{24,28},{28,32},{32,36}... | collective-permute-start | bytes 442376 | tf_op jit(solution)/shard_map/ppermute | solution.py:31
  70.0 4.7 %collective-permute-start.16 = (bf16[80,640]{1,0:T(8,128)(2,1)S(1)}, bf16[80,640]{1,0:T(8,128)(2,1)S(1)}, u32[]{:S(2)}, u32[]{:S(2)}) collective-permute-start(bf16[80,640]{1,0:T(8,128)(2,1)S(1)} %get-tuple-element.116), channel_id=1, source_target_pairs={{0,4},{4,0},{8,12},{12,8},{16,20},{20,16},{24,28},{28,24},{32,36},... | collective-permute-start | bytes 307208 | tf_op jit(solution)/shard_map/ppermute | solution.py:31
  70.0 5.7 %collective-permute-start.18 = (bf16[80,640]{1,0:T(8,128)(2,1)S(1)}, bf16[80,640]{1,0:T(8,128)(2,1)S(1)}, u32[]{:S(2)}, u32[]{:S(2)}) collective-permute-start(bf16[80,640]{1,0:T(8,128)(2,1)S(1)} %get-tuple-element.118), channel_id=1, source_target_pairs={{0,132},{4,128},{8,140},{12,136},{16,148},{20,144},{24,156},{28,15... | collective-permute-start | bytes 307208 | tf_op jit(solution)/shard_map/ppermute | solution.py:31
  79.5 6.4 %collective-permute-start.20 = (bf16[32,1024]{1,0:T(8,128)(2,1)S(1)}, bf16[32,1024]{1,0:T(8,128)(2,1)S(1)}, u32[]{:S(2)}, u32[]{:S(2)}) collective-permute-start(bf16[32,1024]{1,0:T(8,128)(2,1)S(1)} %get-tuple-element.125), channel_id=1, source_target_pairs={{0,8},{4,12},{8,16},{12,20},{16,24},{20,28},{24,0},{28,4},{32,40},... | collective-permute-start | bytes 196616 | tf_op jit(solution)/shard_map/ppermute | solution.py:31
  79.6 9.1 %collective-permute-start.21 = (bf16[32,1024]{1,0:T(8,128)(2,1)S(1)}, bf16[32,1024]{1,0:T(8,128)(2,1)S(1)}, u32[]{:S(2)}, u32[]{:S(2)}) collective-permute-start(bf16[32,1024]{1,0:T(8,128)(2,1)S(1)} %get-tuple-element.126), channel_id=1, source_target_pairs={{0,16},{4,20},{8,24},{12,28},{16,0},{20,4},{24,8},{28,12},{32,48},... | collective-permute-start | bytes 196616 | tf_op jit(solution)/shard_map/ppermute | solution.py:31
  83.9 6.2 %collective-permute-start.22 = (bf16[32,1024]{1,0:T(8,128)(2,1)S(1)}, bf16[32,1024]{1,0:T(8,128)(2,1)S(1)}, u32[]{:S(2)}, u32[]{:S(2)}) collective-permute-start(bf16[32,1024]{1,0:T(8,128)(2,1)S(1)} %get-tuple-element.127), channel_id=1, source_target_pairs={{0,24},{4,28},{8,0},{12,4},{16,8},{20,12},{24,16},{28,20},{32,56},... | collective-permute-start | bytes 196616 | tf_op jit(solution)/shard_map/ppermute | solution.py:31
  (4 other events, 70.7 us)

commit v7 on v6

--- a/solution.py
+++ b/solution.py
@@ -418,7 +418,7 @@
         in_specs=[pl.BlockSpec(memory_space=pl.ANY)] * 3,
         out_specs=[pl.BlockSpec(memory_space=pltpu.VMEM)] * 3,
         scratch_shapes=[pltpu.SemaphoreType.DMA((3,))],
-        compiler_params=pltpu.CompilerParams(vmem_limit_bytes=56 * 2**20),
+        compiler_params=pltpu.CompilerParams(vmem_limit_bytes=8 * 2**20),
     )(*inputs)
 
     def message(r):

time: 91.6 us -> 90.5 us (0.988)
  Pallas kernels: 15.6 us -> 13.9 us
    unnamed x10 -> x16, local copies, waits for them, and re-layouts: 0.03 us -> 2.63 us
    pallas_call x1, Pallas kernels: 1.93 us -> 0.15 us  [shards(): pl.pallas_call(load_kernel, out_shape=[shape(x.shape, x.dtype) for x in i...]
    slice x1, local copies, waits for them, and re-layouts: 1.68 us -> 0.49 us  [message(): t, g = (x[rows].reshape(72, D) for x in loaded[:2])]
where the time goes in v7:
time: 90.5 us; the launch traced here: 89.8 us
  waiting for transfers between devices  41.5 us (46%)
  starting transfers between devices  28.2 us (31%)
  Pallas kernels  13.9 us (15%)
  local copies, waits for them, and re-layouts  4.98 us (6%)
    ppermute x23, waiting for transfers between devices, sent(): return lax.ppermute(x, axis, [(i, to(i)) for i in range(size)])  41.5 us
    ppermute x23, starting transfers between devices, sent(): return lax.ppermute(x, axis, [(i, to(i)) for i in range(size)])  28.2 us
    pallas_call x1, Pallas kernels, shards(): call(band_kernel, (shape((ALL, 3 * WIDTH), BF16),) + (shape((272, 640), B...  6.98 us
    unnamed x16, local copies, waits for them, and re-layouts  2.63 us
    pallas_call x1, Pallas kernels, shards(): call(bias_kernel, (shape((HEADS, WT, WT), F32), shape((88, 16, 256), BF16...  2.14 us
    pallas_call x1, Pallas kernels, shards(): call(early_kernel, (shape((4, HALF, WIDTH), BF16), shape((4, WT, WIDTH),...  1.85 us
  transfers between devices with their start and end apart: 23, of which 15 were waited for; matrix products, arithmetic and copies ran while one was open for 2% of the time, Pallas kernels for 5%

profile of v7, /device:TPU:2, one launch (start us, length us, event | category | flops | bytes accessed | tf_op | source)
XLA Modules:
  0.0 89.8 jit_solution(4468387256841717602)
XLA Ops:
  4.8 8.4 %collective-permute-start = (bf16[152,1024]{1,0:T(8,128)(2,1)S(1)}, bf16[152,1024]{1,0:T(8,128)(2,1)S(1)}, u32[]{:S(2)}, u32[]{:S(2)}) collective-permute-start(bf16[152,1024]{1,0:T(8,128)(2,1)S(1)} %pad_maximum_fusion.2), channel_id=1, source_target_pairs={{0,252},{4,0},{8,4},{12,8},{16,12},{20,16},{24,20},{28,24},{32,28}... | collective-permute-start | bytes 933896 | tf_op jit(solution)/shard_map/ppermute | solution.py:31
  13.3 2.5 %collective-permute-start.3 = (bf16[152,1024]{1,0:T(8,128)(2,1)S(1)}, bf16[152,1024]{1,0:T(8,128)(2,1)S(1)}, u32[]{:S(2)}, u32[]{:S(2)}) collective-permute-start(bf16[152,1024]{1,0:T(8,128)(2,1)S(1)} %pad_maximum_fusion.1.m0.refs_0_), channel_id=1, source_target_pairs={{0,2},{1,3},{2,0},{3,1},{4,6},{5,7},{6,4},{7,5},{8,10},{9,11},{10,... | collective-permute-start | bytes 933896 | tf_op jit(solution)/shard_map/ppermute | solution.py:31
  15.8 2.1 %shard_map.112 = (f32[4,144,144]{2,1,0:T(8,128)S(1)}, bf16[88,16,256]{2,1,0:T(8,128)(2,1)S(1)}, bf16[88,48,256]{2,1,0:T(8,128)(2,1)S(1)}) custom-call(f32[4,768]{1,0:T(4,128)S(1)} %pad.22.table, s32[144,144]{1,0:T(8,128)S(1)} %copy-done.5, bf16[144,144]{1,0:T(8,128)(2,1)S(1)} %copy-done.6), custom_call_target="tpu_custom_call" | custom-call | flops 100000000 | bytes 4000000 | tf_op jit(solution)/shard_map/pallas_call | solution.py:435
  18.0 1.8 %collective-permute-done.m1.refs_1_ = bf16[152,1024]{1,0:T(8,128)(2,1)S(1)} collective-permute-done((bf16[152,1024]{1,0:T(8,128)(2,1)S(1)}, bf16[152,1024]{1,0:T(8,128)(2,1)S(1)}, u32[]{:S(2)}, u32[]{:S(2)}) %collective-permute-start) | collective-permute-done | bytes 311328 | tf_op jit(solution)/shard_map/ppermute | solution.py:31
  19.8 2.4 %collective-permute-start.4 = (bf16[152,1024]{1,0:T(8,128)(2,1)S(1)}, bf16[152,1024]{1,0:T(8,128)(2,1)S(1)}, u32[]{:S(2)}, u32[]{:S(2)}) collective-permute-start(bf16[152,1024]{1,0:T(8,128)(2,1)S(1)} %collective-permute-done.m1.refs_1_), channel_id=1, source_target_pairs={{0,2},{1,3},{2,0},{3,1},{4,6},{5,7},{6,4},{7,5},{8,10},{9,11},{10,... | collective-permute-start | bytes 933896 | tf_op jit(solution)/shard_map/ppermute | solution.py:31
  22.2 1.5 %collective-permute-done.3.refs_4_ = bf16[152,1024]{1,0:T(8,128)(2,1)S(1)} collective-permute-done((bf16[152,1024]{1,0:T(8,128)(2,1)S(1)}, bf16[152,1024]{1,0:T(8,128)(2,1)S(1)}, u32[]{:S(2)}, u32[]{:S(2)}) %collective-permute-start.3) | collective-permute-done | bytes 311328 | tf_op jit(solution)/shard_map/ppermute | solution.py:31
  23.7 1.8 %shard_map.113 = (bf16[4,320,256]{2,1,0:T(8,128)(2,1)S(1)}, f32[4,144,256]{2,1,0:T(8,128)S(1)}, f32[4,144,144]{2,1,0:T(8,128)S(1)}) custom-call(bf16[152,1024]{1,0:T(8,128)(2,1)S(1)} %pad_maximum_fusion.1.m0.refs_0_, bf16[152,1024]{1,0:T(8,128)(2,1)S(1)} %collective-permute-done.m1.refs_1_, bf16[152,1024]{1,0:T(8,128)(2,1)S(1)} %collective-permute-done.1.m2.refs_2_, ...), custom_call_target="tpu_custom_call" | custom-call | flops 1000000000 | bytes 5000000 | tf_op jit(solution)/shard_map/pallas_call | solution.py:446
  25.6 5.5 %collective-permute-done.4.refs_5_ = bf16[152,1024]{1,0:T(8,128)(2,1)S(1)} collective-permute-done((bf16[152,1024]{1,0:T(8,128)(2,1)S(1)}, bf16[152,1024]{1,0:T(8,128)(2,1)S(1)}, u32[]{:S(2)}, u32[]{:S(2)}) %collective-permute-start.4) | collective-permute-done | bytes 311328 | tf_op jit(solution)/shard_map/ppermute | solution.py:31
  31.1 1.6 %collective-permute-done.6.refs_7_ = bf16[152,1024]{1,0:T(8,128)(2,1)S(1)} collective-permute-done((bf16[152,1024]{1,0:T(8,128)(2,1)S(1)}, bf16[152,1024]{1,0:T(8,128)(2,1)S(1)}, u32[]{:S(2)}, u32[]{:S(2)}) %collective-permute-start.6) | collective-permute-done | bytes 311328 | tf_op jit(solution)/shard_map/ppermute | solution.py:31
  32.7 7.0 %shard_map.114 = (bf16[640,768]{1,0:T(8,128)(2,1)S(1)}, bf16[272,640]{1,0:T(8,128)(2,1)S(1)}, bf16[272,640]{1,0:T(8,128)(2,1)S(1)}, bf16[272,640]{1,0:T(8,128)(2...) custom-call(bf16[152,1024]{1,0:T(8,128)(2,1)S(1)} %pad_maximum_fusion.1.m0.refs_0_, ...), custom_call_target="tpu_custom_call" | custom-call | flops 3000000000 | bytes 10000000 | tf_op jit(solution)/shard_map/pallas_call | solution.py:462
  39.7 1.2 %shard_map.116 = (bf16[144,1024]{1,0:T(8,128)(2,1)S(1)}, bf16[144,1024]{1,0:T(8,128)(2,1)S(1)}, bf16[288,1024]{1,0:T(8,128)(2,1)S(1)}) custom-call(bf16[640,768]{1,0:T(8,128)(2,1)S(1)} %get-tuple-element.102.grads, bf16[3,1024,256]{2,1,0:T(8,128)(2,1)S(1)} %copy-done), custom_call_target="tpu_custom_call" | custom-call | flops 1000000000 | bytes 5000000 | tf_op jit(solution)/shard_map/pallas_call | solution.py:494
  41.1 2.2 %collective-permute-start.8 = (bf16[272,640]{1,0:T(8,128)(2,1)S(1)}, bf16[272,640]{1,0:T(8,128)(2,1)S(1)}, u32[]{:S(2)}, u32[]{:S(2)}) collective-permute-start(bf16[272,640]{1,0:T(8,128)(2,1)S(1)} %get-tuple-element.94), channel_id=1, source_target_pairs={{0,64},{4,68},{8,72},{12,76},{16,80},{20,84},{24,88},{28,92},{32,9... | collective-permute-start | bytes 1044488 | tf_op jit(solution)/shard_map/ppermute | solution.py:31
  44.5 2.5 %collective-permute-start.15 = (bf16[144,1024]{1,0:T(8,128)(2,1)S(1)}, bf16[144,1024]{1,0:T(8,128)(2,1)S(1)}, u32[]{:S(2)}, u32[]{:S(2)}) collective-permute-start(bf16[144,1024]{1,0:T(8,128)(2,1)S(1)} %add_convert_fusion), channel_id=1, source_target_pairs={{0,2},{1,3},{2,0},{3,1},{4,6},{5,7},{6,4},{7,5},{8,10},{9,11},{10,... | collective-permute-start | bytes 884744 | tf_op jit(solution)/shard_map/ppermute | solution.py:31
  47.0 8.2 %collective-permute-done.10.refs_1_ = bf16[512,384]{1,0:T(8,128)(2,1)S(1)} collective-permute-done((bf16[512,384]{1,0:T(8,128)(2,1)S(1)}, bf16[512,384]{1,0:T(8,128)(2,1)S(1)}, u32[]{:S(2)}, u32[]{:S(2)}) %collective-permute-start.10) | collective-permute-done | bytes 393248 | tf_op jit(solution)/shard_map/ppermute | solution.py:31
  56.2 4.5 %collective-permute-done.7.refs_1_ = bf16[272,640]{1,0:T(8,128)(2,1)S(1)} collective-permute-done((bf16[272,640]{1,0:T(8,128)(2,1)S(1)}, bf16[272,640]{1,0:T(8,128)(2,1)S(1)}, u32[]{:S(2)}, u32[]{:S(2)}) %collective-permute-start.7) | collective-permute-done | bytes 348192 | tf_op jit(solution)/shard_map/ppermute | solution.py:31
  62.3 4.6 %collective-permute-done.12.refs_6_ = bf16[128,384]{1,0:T(8,128)(2,1)S(1)} collective-permute-done((bf16[128,384]{1,0:T(8,128)(2,1)S(1)}, bf16[128,384]{1,0:T(8,128)(2,1)S(1)}, u32[]{:S(2)}, u32[]{:S(2)}) %collective-permute-start.12) | collective-permute-done | bytes 98336 | tf_op jit(solution)/shard_map/ppermute | solution.py:31
  67.4 1.6 %collective-permute-start.17 = (bf16[80,1024]{1,0:T(8,128)(2,1)S(1)}, bf16[80,1024]{1,0:T(8,128)(2,1)S(1)}, u32[]{:S(2)}, u32[]{:S(2)}) collective-permute-start(bf16[80,1024]{1,0:T(8,128)(2,1)S(1)} %get-tuple-element.117), channel_id=1, source_target_pairs={{0,128},{4,132},{8,136},{12,140},{16,144},{20,148},{24,152},{28,15... | collective-permute-start | bytes 491528 | tf_op jit(solution)/shard_map/ppermute | solution.py:31
  68.9 2.0 %collective-permute-start.18 = (bf16[80,640]{1,0:T(8,128)(2,1)S(1)}, bf16[80,640]{1,0:T(8,128)(2,1)S(1)}, u32[]{:S(2)}, u32[]{:S(2)}) collective-permute-start(bf16[80,640]{1,0:T(8,128)(2,1)S(1)} %get-tuple-element.118), channel_id=1, source_target_pairs={{0,132},{4,128},{8,140},{12,136},{16,148},{20,144},{24,156},{28,15... | collective-permute-start | bytes 307208 | tf_op jit(solution)/shard_map/ppermute | solution.py:31
  70.9 2.7 %collective-permute-done.16.b = bf16[80,640]{1,0:T(8,128)(2,1)S(1)} collective-permute-done((bf16[80,640]{1,0:T(8,128)(2,1)S(1)}, bf16[80,640]{1,0:T(8,128)(2,1)S(1)}, u32[]{:S(2)}, u32[]{:S(2)}) %collective-permute-start.16) | collective-permute-done | bytes 102432 | tf_op jit(solution)/shard_map/ppermute | solution.py:31
  74.7 3.6 %collective-permute-done.19 = bf16[72,1024]{1,0:T(8,128)(2,1)S(1)} collective-permute-done((bf16[72,1024]{1,0:T(8,128)(2,1)S(1)}, bf16[72,1024]{1,0:T(8,128)(2,1)S(1)}, u32[]{:S(2)}, u32[]{:S(2)}) %collective-permute-start.19) | collective-permute-done | bytes 147488 | tf_op jit(solution)/shard_map/ppermute | solution.py:31
  78.5 4.3 %collective-permute-start.21 = (bf16[32,1024]{1,0:T(8,128)(2,1)S(1)}, bf16[32,1024]{1,0:T(8,128)(2,1)S(1)}, u32[]{:S(2)}, u32[]{:S(2)}) collective-permute-start(bf16[32,1024]{1,0:T(8,128)(2,1)S(1)} %get-tuple-element.126), channel_id=1, source_target_pairs={{0,16},{4,20},{8,24},{12,28},{16,0},{20,4},{24,8},{28,12},{32,48},... | collective-permute-start | bytes 196616 | tf_op jit(solution)/shard_map/ppermute | solution.py:31
  82.9 1.2 %reshape.31 = f32[6,12,2,1024]{3,2,1,0:T(2,128)} reshape(f32[144,1024]{1,0:T(8,128)S(1)} %pad_maximum_fusion) | data formatting | bytes 1179648 | tf_op jit(solution)/shard_map/reshape | solution.py:509
  84.9 2.7 %collective-permute-done.21.c = bf16[32,1024]{1,0:T(8,128)(2,1)S(1)} collective-permute-done((bf16[32,1024]{1,0:T(8,128)(2,1)S(1)}, bf16[32,1024]{1,0:T(8,128)(2,1)S(1)}, u32[]{:S(2)}, u32[]{:S(2)}) %collective-permute-start.21) | collective-permute-done | bytes 65568 | tf_op jit(solution)/shard_map/ppermute | solution.py:31
  87.6 1.4 %collective-permute-done.22.d = bf16[32,1024]{1,0:T(8,128)(2,1)S(1)} collective-permute-done((bf16[32,1024]{1,0:T(8,128)(2,1)S(1)}, bf16[32,1024]{1,0:T(8,128)(2,1)S(1)}, u32[]{:S(2)}, u32[]{:S(2)}) %collective-permute-start.22) | collective-permute-done | bytes 65568 | tf_op jit(solution)/shard_map/ppermute | solution.py:31
  (72 shorter events, 11.6 us)
Async XLA Ops:
  3.5 20.2 %copy-start = (bf16[3,1024,256]{2,1,0:T(8,128)(2,1)S(1)}, bf16[3,1024,256]{2,1,0:T(8,128)(2,1)}, u32[]{:S(2)}) copy-start(bf16[3,1024,256]{2,1,0:T(8,128)(2,1)} %weight.1) | copy-start | bytes 4718596
  4.8 15.0 %collective-permute-start = (bf16[152,1024]{1,0:T(8,128)(2,1)S(1)}, bf16[152,1024]{1,0:T(8,128)(2,1)S(1)}, u32[]{:S(2)}, u32[]{:S(2)}) collective-permute-start(bf16[152,1024]{1,0:T(8,128)(2,1)S(1)} %pad_maximum_fusion.2), channel_id=1, source_target_pairs={{0,252},{4,0},{8,4},{12,8},{16,12},{20,16},{24,20},{28,24},{32,28}... | collective-permute-start | bytes 933896 | tf_op jit(solution)/shard_map/ppermute | solution.py:31
  13.3 10.4 %collective-permute-start.3 = (bf16[152,1024]{1,0:T(8,128)(2,1)S(1)}, bf16[152,1024]{1,0:T(8,128)(2,1)S(1)}, u32[]{:S(2)}, u32[]{:S(2)}) collective-permute-start(bf16[152,1024]{1,0:T(8,128)(2,1)S(1)} %pad_maximum_fusion.1.m0.refs_0_), channel_id=1, source_target_pairs={{0,2},{1,3},{2,0},{3,1},{4,6},{5,7},{6,4},{7,5},{8,10},{9,11},{10,... | collective-permute-start | bytes 933896 | tf_op jit(solution)/shard_map/ppermute | solution.py:31
  15.8 7.9 %collective-permute-start.1 = (bf16[152,1024]{1,0:T(8,128)(2,1)S(1)}, bf16[152,1024]{1,0:T(8,128)(2,1)S(1)}, u32[]{:S(2)}, u32[]{:S(2)}) collective-permute-start(bf16[152,1024]{1,0:T(8,128)(2,1)S(1)} %pad_maximum_fusion.1.m0.refs_0_), channel_id=1, source_target_pairs={{0,1},{1,0},{2,3},{3,2},{4,5},{5,4},{6,7},{7,6},{8,9},{9,8},{10,11... | collective-permute-start | bytes 933896 | tf_op jit(solution)/shard_map/ppermute | solution.py:31
  19.8 3.9 %collective-permute-start.2 = (bf16[152,1024]{1,0:T(8,128)(2,1)S(1)}, bf16[152,1024]{1,0:T(8,128)(2,1)S(1)}, u32[]{:S(2)}, u32[]{:S(2)}) collective-permute-start(bf16[152,1024]{1,0:T(8,128)(2,1)S(1)} %collective-permute-done.m1.refs_1_), channel_id=1, source_target_pairs={{0,1},{1,0},{2,3},{3,2},{4,5},{5,4},{6,7},{7,6},{8,9},{9,8},{10,11... | collective-permute-start | bytes 933896 | tf_op jit(solution)/shard_map/ppermute | solution.py:31
  19.8 11.3 %collective-permute-start.4 = (bf16[152,1024]{1,0:T(8,128)(2,1)S(1)}, bf16[152,1024]{1,0:T(8,128)(2,1)S(1)}, u32[]{:S(2)}, u32[]{:S(2)}) collective-permute-start(bf16[152,1024]{1,0:T(8,128)(2,1)S(1)} %collective-permute-done.m1.refs_1_), channel_id=1, source_target_pairs={{0,2},{1,3},{2,0},{3,1},{4,6},{5,7},{6,4},{7,5},{8,10},{9,11},{10,... | collective-permute-start | bytes 933896 | tf_op jit(solution)/shard_map/ppermute | solution.py:31
  23.7 7.4 %collective-permute-start.5 = (bf16[152,1024]{1,0:T(8,128)(2,1)S(1)}, bf16[152,1024]{1,0:T(8,128)(2,1)S(1)}, u32[]{:S(2)}, u32[]{:S(2)}) collective-permute-start(bf16[152,1024]{1,0:T(8,128)(2,1)S(1)} %collective-permute-done.3.refs_4_), channel_id=1, source_target_pairs={{0,1},{1,0},{2,3},{3,2},{4,5},{5,4},{6,7},{7,6},{8,9},{9,8},{10,11... | collective-permute-start | bytes 933896 | tf_op jit(solution)/shard_map/ppermute | solution.py:31
  31.1 1.6 %collective-permute-start.6 = (bf16[152,1024]{1,0:T(8,128)(2,1)S(1)}, bf16[152,1024]{1,0:T(8,128)(2,1)S(1)}, u32[]{:S(2)}, u32[]{:S(2)}) collective-permute-start(bf16[152,1024]{1,0:T(8,128)(2,1)S(1)} %collective-permute-done.4.refs_5_), channel_id=1, source_target_pairs={{0,1},{1,0},{2,3},{3,2},{4,5},{5,4},{6,7},{7,6},{8,9},{9,8},{10,11... | collective-permute-start | bytes 933896 | tf_op jit(solution)/shard_map/ppermute | solution.py:31
  40.9 3.5 %collective-permute-start.14 = (bf16[288,1024]{1,0:T(8,128)(2,1)S(1)}, bf16[288,1024]{1,0:T(8,128)(2,1)S(1)}, u32[]{:S(2)}, u32[]{:S(2)}) collective-permute-start(bf16[288,1024]{1,0:T(8,128)(2,1)S(1)} %get-tuple-element.104), channel_id=1, source_target_pairs={{0,1},{1,0},{2,3},{3,2},{4,5},{5,4},{6,7},{7,6},{8,9},{9,8},{10,11... | collective-permute-start | bytes 1769480 | tf_op jit(solution)/shard_map/ppermute | solution.py:31
  41.1 19.7 %collective-permute-start.7 = (bf16[272,640]{1,0:T(8,128)(2,1)S(1)}, bf16[272,640]{1,0:T(8,128)(2,1)S(1)}, u32[]{:S(2)}, u32[]{:S(2)}) collective-permute-start(bf16[272,640]{1,0:T(8,128)(2,1)S(1)} %get-tuple-element.93), channel_id=1, source_target_pairs={{0,32},{4,36},{8,40},{12,44},{16,48},{20,52},{24,56},{28,60},{32,6... | collective-permute-start | bytes 1044488 | tf_op jit(solution)/shard_map/ppermute | solution.py:31
  41.1 19.7 %collective-permute-start.8 = (bf16[272,640]{1,0:T(8,128)(2,1)S(1)}, bf16[272,640]{1,0:T(8,128)(2,1)S(1)}, u32[]{:S(2)}, u32[]{:S(2)}) collective-permute-start(bf16[272,640]{1,0:T(8,128)(2,1)S(1)} %get-tuple-element.94), channel_id=1, source_target_pairs={{0,64},{4,68},{8,72},{12,76},{16,80},{20,84},{24,88},{28,92},{32,9... | collective-permute-start | bytes 1044488 | tf_op jit(solution)/shard_map/ppermute | solution.py:31
  43.3 18.2 %collective-permute-start.9 = (bf16[272,640]{1,0:T(8,128)(2,1)S(1)}, bf16[272,640]{1,0:T(8,128)(2,1)S(1)}, u32[]{:S(2)}, u32[]{:S(2)}) collective-permute-start(bf16[272,640]{1,0:T(8,128)(2,1)S(1)} %get-tuple-element.95), channel_id=1, source_target_pairs={{0,96},{4,100},{8,104},{12,108},{16,112},{20,116},{24,120},{28,124... | collective-permute-start | bytes 1044488 | tf_op jit(solution)/shard_map/ppermute | solution.py:31
  44.4 10.8 %collective-permute-start.10 = (bf16[512,384]{1,0:T(8,128)(2,1)S(1)}, bf16[512,384]{1,0:T(8,128)(2,1)S(1)}, u32[]{:S(2)}, u32[]{:S(2)}) collective-permute-start(bf16[512,384]{1,0:T(8,128)(2,1)S(1)} %get-tuple-element.97), channel_id=1, source_target_pairs={{0,4},{4,0},{8,12},{12,8},{16,20},{20,16},{24,28},{28,24},{32,36},... | collective-permute-start | bytes 1179656 | tf_op jit(solution)/shard_map/ppermute | solution.py:31
  44.5 22.4 %collective-permute-start.15 = (bf16[144,1024]{1,0:T(8,128)(2,1)S(1)}, bf16[144,1024]{1,0:T(8,128)(2,1)S(1)}, u32[]{:S(2)}, u32[]{:S(2)}) collective-permute-start(bf16[144,1024]{1,0:T(8,128)(2,1)S(1)} %add_convert_fusion), channel_id=1, source_target_pairs={{0,2},{1,3},{2,0},{3,1},{4,6},{5,7},{6,4},{7,5},{8,10},{9,11},{10,... | collective-permute-start | bytes 884744 | tf_op jit(solution)/shard_map/ppermute | solution.py:31
  55.3 7.0 %collective-permute-start.11 = (bf16[128,384]{1,0:T(8,128)(2,1)S(1)}, bf16[128,384]{1,0:T(8,128)(2,1)S(1)}, u32[]{:S(2)}, u32[]{:S(2)}) collective-permute-start(bf16[128,384]{1,0:T(8,128)(2,1)S(1)} %get-tuple-element.99), channel_id=1, source_target_pairs={{0,32},{4,36},{8,40},{12,44},{16,48},{20,52},{24,56},{28,60},{32,6... | collective-permute-start | bytes 294920 | tf_op jit(solution)/shard_map/ppermute | solution.py:31
  60.8 6.1 %collective-permute-start.12 = (bf16[128,384]{1,0:T(8,128)(2,1)S(1)}, bf16[128,384]{1,0:T(8,128)(2,1)S(1)}, u32[]{:S(2)}, u32[]{:S(2)}) collective-permute-start(bf16[128,384]{1,0:T(8,128)(2,1)S(1)} %get-tuple-element.100), channel_id=1, source_target_pairs={{0,64},{4,68},{8,72},{12,76},{16,80},{20,84},{24,88},{28,92},{32,9... | collective-permute-start | bytes 294920 | tf_op jit(solution)/shard_map/ppermute | solution.py:31
  60.8 6.1 %collective-permute-start.13 = (bf16[128,384]{1,0:T(8,128)(2,1)S(1)}, bf16[128,384]{1,0:T(8,128)(2,1)S(1)}, u32[]{:S(2)}, u32[]{:S(2)}) collective-permute-start(bf16[128,384]{1,0:T(8,128)(2,1)S(1)} %get-tuple-element.101), channel_id=1, source_target_pairs={{0,96},{4,100},{8,104},{12,108},{16,112},{20,116},{24,120},{28,124... | collective-permute-start | bytes 294920 | tf_op jit(solution)/shard_map/ppermute | solution.py:31
  67.4 10.9 %collective-permute-start.17 = (bf16[80,1024]{1,0:T(8,128)(2,1)S(1)}, bf16[80,1024]{1,0:T(8,128)(2,1)S(1)}, u32[]{:S(2)}, u32[]{:S(2)}) collective-permute-start(bf16[80,1024]{1,0:T(8,128)(2,1)S(1)} %get-tuple-element.117), channel_id=1, source_target_pairs={{0,128},{4,132},{8,136},{12,140},{16,144},{20,148},{24,152},{28,15... | collective-permute-start | bytes 491528 | tf_op jit(solution)/shard_map/ppermute | solution.py:31
  68.9 9.4 %collective-permute-start.19 = (bf16[72,1024]{1,0:T(8,128)(2,1)S(1)}, bf16[72,1024]{1,0:T(8,128)(2,1)S(1)}, u32[]{:S(2)}, u32[]{:S(2)}) collective-permute-start(bf16[72,1024]{1,0:T(8,128)(2,1)S(1)} %get-tuple-element.119), channel_id=1, source_target_pairs={{0,4},{4,8},{8,12},{12,16},{16,20},{20,24},{24,28},{28,32},{32,36}... | collective-permute-start | bytes 442376 | tf_op jit(solution)/shard_map/ppermute | solution.py:31
  68.9 4.7 %collective-permute-start.16 = (bf16[80,640]{1,0:T(8,128)(2,1)S(1)}, bf16[80,640]{1,0:T(8,128)(2,1)S(1)}, u32[]{:S(2)}, u32[]{:S(2)}) collective-permute-start(bf16[80,640]{1,0:T(8,128)(2,1)S(1)} %get-tuple-element.116), channel_id=1, source_target_pairs={{0,4},{4,0},{8,12},{12,8},{16,20},{20,16},{24,28},{28,24},{32,36},... | collective-permute-start | bytes 307208 | tf_op jit(solution)/shard_map/ppermute | solution.py:31
  68.9 5.7 %collective-permute-start.18 = (bf16[80,640]{1,0:T(8,128)(2,1)S(1)}, bf16[80,640]{1,0:T(8,128)(2,1)S(1)}, u32[]{:S(2)}, u32[]{:S(2)}) collective-permute-start(bf16[80,640]{1,0:T(8,128)(2,1)S(1)} %get-tuple-element.118), channel_id=1, source_target_pairs={{0,132},{4,128},{8,140},{12,136},{16,148},{20,144},{24,156},{28,15... | collective-permute-start | bytes 307208 | tf_op jit(solution)/shard_map/ppermute | solution.py:31
  78.5 6.4 %collective-permute-start.20 = (bf16[32,1024]{1,0:T(8,128)(2,1)S(1)}, bf16[32,1024]{1,0:T(8,128)(2,1)S(1)}, u32[]{:S(2)}, u32[]{:S(2)}) collective-permute-start(bf16[32,1024]{1,0:T(8,128)(2,1)S(1)} %get-tuple-element.125), channel_id=1, source_target_pairs={{0,8},{4,12},{8,16},{12,20},{16,24},{20,28},{24,0},{28,4},{32,40},... | collective-permute-start | bytes 196616 | tf_op jit(solution)/shard_map/ppermute | solution.py:31
  78.5 9.1 %collective-permute-start.21 = (bf16[32,1024]{1,0:T(8,128)(2,1)S(1)}, bf16[32,1024]{1,0:T(8,128)(2,1)S(1)}, u32[]{:S(2)}, u32[]{:S(2)}) collective-permute-start(bf16[32,1024]{1,0:T(8,128)(2,1)S(1)} %get-tuple-element.126), channel_id=1, source_target_pairs={{0,16},{4,20},{8,24},{12,28},{16,0},{20,4},{24,8},{28,12},{32,48},... | collective-permute-start | bytes 196616 | tf_op jit(solution)/shard_map/ppermute | solution.py:31
  82.8 6.1 %collective-permute-start.22 = (bf16[32,1024]{1,0:T(8,128)(2,1)S(1)}, bf16[32,1024]{1,0:T(8,128)(2,1)S(1)}, u32[]{:S(2)}, u32[]{:S(2)}) collective-permute-start(bf16[32,1024]{1,0:T(8,128)(2,1)S(1)} %get-tuple-element.127), channel_id=1, source_target_pairs={{0,24},{4,28},{8,0},{12,4},{16,8},{20,12},{24,16},{28,20},{32,56},... | collective-permute-start | bytes 196616 | tf_op jit(solution)/shard_map/ppermute | solution.py:31
  (7 other events, 60.4 us)

commit v8 on v7

--- a/solution.py
+++ b/solution.py
@@ -345,10 +345,7 @@
 
 
 def second_kernel(*refs):
-    ways, late, (near, given, more), outs, (high, low) = refs[:4], refs[4:8], refs[8:11], refs[11:15], refs[15:]
-    total = near[...].astype(F32) + given[...].astype(F32) + more[...].astype(F32)
-    high[...] = total[:72]
-    low[...] = total[72:].astype(BF16)
+    ways, late, outs = refs[:4], refs[4:8], refs[8:]
     x, _, z = place()
     found = bias_rows(bias_sum(stage_rows(ways, pl.ds(256, 16), slice(0, 512))))
     for i, out in enumerate(outs):
@@ -364,7 +361,10 @@
             out[64:, 640:] = jnp.zeros((16, 384), BF16)
 
 
-def third_kernel(a, b, c, d, *outs):
+def third_kernel(a, b, c, d, near, given, more, high, low, *outs):
+    total = near[...].astype(F32) + given[...].astype(F32) + more[...].astype(F32)
+    high[...] = total[:72]
+    low[...] = total[72:].astype(BF16)
     z = place()[2] // 2
     found = bias_rows(bias_sum(stage_rows((a, b, c, d), pl.ds(64, 16), slice(0, 512))))
     for e, out in enumerate(outs):
@@ -499,15 +499,19 @@
     more = across(far)
     parts = call(after_pairs_kernel, (shape((128, 384), BF16),) * 4, (), 10**6, 10**6, 8)(*pairs)
     late = by_y(parts)
-    ways, late, more = lax.optimization_barrier((ways, late, more))
     full, part = shape((80, D), BF16), shape((80, 640), BF16)
-    *parts, near, low = call(
-        second_kernel, (full, part, full, part, shape((72, D), F32), shape((72, D), BF16)), (), 10**6, 4 * 10**6, 8
-    )(*ways, *late, near, given[:WT], more)
+    parts = call(second_kernel, (full, part, full, part), (), 10**6, 4 * 10**6, 8)(*ways, *late)
     parts = [parts[0]] + [sent(parts[i], "lat", paired(i // 2, i % 2)) for i in range(1, 4)]
-    parts, low = lax.optimization_barrier((parts, onward(low)))
+    near, low, *parts = call(
+        third_kernel,
+        (shape((72, D), F32), shape((72, D), BF16)) + (shape((32, D), BF16),) * 4,
+        (),
+        10**6,
+        2 * 10**6,
+        8,
+    )(*parts, near, given[:WT], more)
+    low = onward(low)
     input_grad = jnp.concatenate([low.astype(F32), near]).reshape(6, 12, 2, D).transpose(0, 2, 1, 3)
-    parts = call(third_kernel, (shape((32, D), BF16),) * 4, (), 10**6, 10**6, 8)(*parts)
     far = sent(parts[2], "lat", moved(0, 0, 4))
     got = [parts[0], sent(parts[1], "lat", moved(0, 0, 2)), far, sent(parts[3], "lat", moved(0, 0, 6))]
     got, input_grad = lax.optimization_barrier((got, input_grad))

time: 90.5 us -> 91.4 us (level)
  starting transfers between devices: 28.2 us -> 30.1 us
  waiting for transfers between devices: 41.5 us -> 39.8 us
    ppermute x23, starting transfers between devices: 28.2 us -> 30.1 us  [sent(): return lax.ppermute(x, axis, [(i, to(i)) for i in range(size)])]
    ppermute x23, waiting for transfers between devices: 41.5 us -> 39.8 us  [sent(): return lax.ppermute(x, axis, [(i, to(i)) for i in range(size)])]
  transfers between devices with their start and end apart: 23 -> 23, of which waited for: 15 -> 13; matrix products, arithmetic and copies ran while one was open for 2% -> 2% of each run, Pallas kernels for 5% -> 5%
where the time goes in v8:
time: 91.4 us; the launch traced here: 90 us
  waiting for transfers between devices  39.8 us (44%)
  starting transfers between devices  30.1 us (33%)
  Pallas kernels  13.8 us (15%)
  local copies, waits for them, and re-layouts  4.98 us (5%)
    ppermute x23, waiting for transfers between devices, sent(): return lax.ppermute(x, axis, [(i, to(i)) for i in range(size)])  39.8 us
    ppermute x23, starting transfers between devices, sent(): return lax.ppermute(x, axis, [(i, to(i)) for i in range(size)])  30.1 us
    pallas_call x1, Pallas kernels, shards(): call(band_kernel, (shape((ALL, 3 * WIDTH), BF16),) + (shape((272, 640), B...  6.98 us
    unnamed x16, local copies, waits for them, and re-layouts  2.63 us
    pallas_call x1, Pallas kernels, shards(): call(bias_kernel, (shape((HEADS, WT, WT), F32), shape((88, 16, 256), BF16...  2.14 us
    pallas_call x1, Pallas kernels, shards(): call(early_kernel, (shape((4, HALF, WIDTH), BF16), shape((4, WT, WIDTH),...  1.85 us
  transfers between devices with their start and end apart: 23, of which 13 were waited for; matrix products, arithmetic and copies ran while one was open for 2% of the time, Pallas kernels for 5%

profile of v8, /device:TPU:2, one launch (start us, length us, event | category | flops | bytes accessed | tf_op | source)
XLA Modules:
  0.0 90.0 jit_solution(14747419466048247680)
XLA Ops:
  4.8 8.4 %collective-permute-start = (bf16[152,1024]{1,0:T(8,128)(2,1)S(1)}, bf16[152,1024]{1,0:T(8,128)(2,1)S(1)}, u32[]{:S(2)}, u32[]{:S(2)}) collective-permute-start(bf16[152,1024]{1,0:T(8,128)(2,1)S(1)} %pad_maximum_fusion.2), channel_id=1, source_target_pairs={{0,252},{4,0},{8,4},{12,8},{16,12},{20,16},{24,20},{28,24},{32,28}... | collective-permute-start | bytes 933896 | tf_op jit(solution)/shard_map/ppermute | solution.py:31
  13.3 2.5 %collective-permute-start.3 = (bf16[152,1024]{1,0:T(8,128)(2,1)S(1)}, bf16[152,1024]{1,0:T(8,128)(2,1)S(1)}, u32[]{:S(2)}, u32[]{:S(2)}) collective-permute-start(bf16[152,1024]{1,0:T(8,128)(2,1)S(1)} %pad_maximum_fusion.1.m0.refs_0_), channel_id=1, source_target_pairs={{0,2},{1,3},{2,0},{3,1},{4,6},{5,7},{6,4},{7,5},{8,10},{9,11},{10,... | collective-permute-start | bytes 933896 | tf_op jit(solution)/shard_map/ppermute | solution.py:31
  15.8 2.1 %shard_map.112 = (f32[4,144,144]{2,1,0:T(8,128)S(1)}, bf16[88,16,256]{2,1,0:T(8,128)(2,1)S(1)}, bf16[88,48,256]{2,1,0:T(8,128)(2,1)S(1)}) custom-call(f32[4,768]{1,0:T(4,128)S(1)} %pad.22.table, s32[144,144]{1,0:T(8,128)S(1)} %copy-done.5, bf16[144,144]{1,0:T(8,128)(2,1)S(1)} %copy-done.6), custom_call_target="tpu_custom_call" | custom-call | flops 100000000 | bytes 4000000 | tf_op jit(solution)/shard_map/pallas_call | solution.py:435
  18.0 1.8 %collective-permute-done.m1.refs_1_ = bf16[152,1024]{1,0:T(8,128)(2,1)S(1)} collective-permute-done((bf16[152,1024]{1,0:T(8,128)(2,1)S(1)}, bf16[152,1024]{1,0:T(8,128)(2,1)S(1)}, u32[]{:S(2)}, u32[]{:S(2)}) %collective-permute-start) | collective-permute-done | bytes 311328 | tf_op jit(solution)/shard_map/ppermute | solution.py:31
  19.8 2.4 %collective-permute-start.4 = (bf16[152,1024]{1,0:T(8,128)(2,1)S(1)}, bf16[152,1024]{1,0:T(8,128)(2,1)S(1)}, u32[]{:S(2)}, u32[]{:S(2)}) collective-permute-start(bf16[152,1024]{1,0:T(8,128)(2,1)S(1)} %collective-permute-done.m1.refs_1_), channel_id=1, source_target_pairs={{0,2},{1,3},{2,0},{3,1},{4,6},{5,7},{6,4},{7,5},{8,10},{9,11},{10,... | collective-permute-start | bytes 933896 | tf_op jit(solution)/shard_map/ppermute | solution.py:31
  22.2 1.5 %collective-permute-done.3.refs_4_ = bf16[152,1024]{1,0:T(8,128)(2,1)S(1)} collective-permute-done((bf16[152,1024]{1,0:T(8,128)(2,1)S(1)}, bf16[152,1024]{1,0:T(8,128)(2,1)S(1)}, u32[]{:S(2)}, u32[]{:S(2)}) %collective-permute-start.3) | collective-permute-done | bytes 311328 | tf_op jit(solution)/shard_map/ppermute | solution.py:31
  23.7 1.8 %shard_map.113 = (bf16[4,320,256]{2,1,0:T(8,128)(2,1)S(1)}, f32[4,144,256]{2,1,0:T(8,128)S(1)}, f32[4,144,144]{2,1,0:T(8,128)S(1)}) custom-call(bf16[152,1024]{1,0:T(8,128)(2,1)S(1)} %pad_maximum_fusion.1.m0.refs_0_, bf16[152,1024]{1,0:T(8,128)(2,1)S(1)} %collective-permute-done.m1.refs_1_, bf16[152,1024]{1,0:T(8,128)(2,1)S(1)} %collective-permute-done.1.m2.refs_2_, ...), custom_call_target="tpu_custom_call" | custom-call | flops 1000000000 | bytes 5000000 | tf_op jit(solution)/shard_map/pallas_call | solution.py:446
  25.6 5.5 %collective-permute-done.4.refs_5_ = bf16[152,1024]{1,0:T(8,128)(2,1)S(1)} collective-permute-done((bf16[152,1024]{1,0:T(8,128)(2,1)S(1)}, bf16[152,1024]{1,0:T(8,128)(2,1)S(1)}, u32[]{:S(2)}, u32[]{:S(2)}) %collective-permute-start.4) | collective-permute-done | bytes 311328 | tf_op jit(solution)/shard_map/ppermute | solution.py:31
  31.1 1.6 %collective-permute-done.6.refs_7_ = bf16[152,1024]{1,0:T(8,128)(2,1)S(1)} collective-permute-done((bf16[152,1024]{1,0:T(8,128)(2,1)S(1)}, bf16[152,1024]{1,0:T(8,128)(2,1)S(1)}, u32[]{:S(2)}, u32[]{:S(2)}) %collective-permute-start.6) | collective-permute-done | bytes 311328 | tf_op jit(solution)/shard_map/ppermute | solution.py:31
  32.7 7.0 %shard_map.114 = (bf16[640,768]{1,0:T(8,128)(2,1)S(1)}, bf16[272,640]{1,0:T(8,128)(2,1)S(1)}, bf16[272,640]{1,0:T(8,128)(2,1)S(1)}, bf16[272,640]{1,0:T(8,128)(2...) custom-call(bf16[152,1024]{1,0:T(8,128)(2,1)S(1)} %pad_maximum_fusion.1.m0.refs_0_, ...), custom_call_target="tpu_custom_call" | custom-call | flops 3000000000 | bytes 10000000 | tf_op jit(solution)/shard_map/pallas_call | solution.py:462
  39.7 1.2 %shard_map.117 = (bf16[144,1024]{1,0:T(8,128)(2,1)S(1)}, bf16[144,1024]{1,0:T(8,128)(2,1)S(1)}, bf16[288,1024]{1,0:T(8,128)(2,1)S(1)}) custom-call(bf16[640,768]{1,0:T(8,128)(2,1)S(1)} %get-tuple-element.92.grads, bf16[3,1024,256]{2,1,0:T(8,128)(2,1)S(1)} %copy-done), custom_call_target="tpu_custom_call" | custom-call | flops 1000000000 | bytes 5000000 | tf_op jit(solution)/shard_map/pallas_call | solution.py:494
  41.2 2.2 %collective-permute-start.8 = (bf16[272,640]{1,0:T(8,128)(2,1)S(1)}, bf16[272,640]{1,0:T(8,128)(2,1)S(1)}, u32[]{:S(2)}, u32[]{:S(2)}) collective-permute-start(bf16[272,640]{1,0:T(8,128)(2,1)S(1)} %get-tuple-element.80), channel_id=1, source_target_pairs={{0,64},{4,68},{8,72},{12,76},{16,80},{20,84},{24,88},{28,92},{32,9... | collective-permute-start | bytes 1044488 | tf_op jit(solution)/shard_map/ppermute | solution.py:31
  43.4 1.1 %collective-permute-start.9 = (bf16[272,640]{1,0:T(8,128)(2,1)S(1)}, bf16[272,640]{1,0:T(8,128)(2,1)S(1)}, u32[]{:S(2)}, u32[]{:S(2)}) collective-permute-start(bf16[272,640]{1,0:T(8,128)(2,1)S(1)} %get-tuple-element.81), channel_id=1, source_target_pairs={{0,96},{4,100},{8,104},{12,108},{16,112},{20,116},{24,120},{28,124... | collective-permute-start | bytes 1044488 | tf_op jit(solution)/shard_map/ppermute | solution.py:31
  44.5 2.5 %collective-permute-start.18 = (bf16[144,1024]{1,0:T(8,128)(2,1)S(1)}, bf16[144,1024]{1,0:T(8,128)(2,1)S(1)}, u32[]{:S(2)}, u32[]{:S(2)}) collective-permute-start(bf16[144,1024]{1,0:T(8,128)(2,1)S(1)} %add_convert_fusion), channel_id=1, source_target_pairs={{0,2},{1,3},{2,0},{3,1},{4,6},{5,7},{6,4},{7,5},{8,10},{9,11},{10,... | collective-permute-start | bytes 884744 | tf_op jit(solution)/shard_map/ppermute | solution.py:31
  47.0 5.5 %collective-permute-done.10.refs_1_ = bf16[512,384]{1,0:T(8,128)(2,1)S(1)} collective-permute-done((bf16[512,384]{1,0:T(8,128)(2,1)S(1)}, bf16[512,384]{1,0:T(8,128)(2,1)S(1)}, u32[]{:S(2)}, u32[]{:S(2)}) %collective-permute-start.10) | collective-permute-done | bytes 393248 | tf_op jit(solution)/shard_map/ppermute | solution.py:31
  52.7 8.1 %collective-permute-done.7.refs_1_ = bf16[272,640]{1,0:T(8,128)(2,1)S(1)} collective-permute-done((bf16[272,640]{1,0:T(8,128)(2,1)S(1)}, bf16[272,640]{1,0:T(8,128)(2,1)S(1)}, u32[]{:S(2)}, u32[]{:S(2)}) %collective-permute-start.7) | collective-permute-done | bytes 348192 | tf_op jit(solution)/shard_map/ppermute | solution.py:31
  62.3 4.6 %collective-permute-done.12.refs_6_ = bf16[128,384]{1,0:T(8,128)(2,1)S(1)} collective-permute-done((bf16[128,384]{1,0:T(8,128)(2,1)S(1)}, bf16[128,384]{1,0:T(8,128)(2,1)S(1)}, u32[]{:S(2)}, u32[]{:S(2)}) %collective-permute-start.12) | collective-permute-done | bytes 98336 | tf_op jit(solution)/shard_map/ppermute | solution.py:31
  67.2 1.6 %collective-permute-start.15 = (bf16[80,1024]{1,0:T(8,128)(2,1)S(1)}, bf16[80,1024]{1,0:T(8,128)(2,1)S(1)}, u32[]{:S(2)}, u32[]{:S(2)}) collective-permute-start(bf16[80,1024]{1,0:T(8,128)(2,1)S(1)} %get-tuple-element.90), channel_id=1, source_target_pairs={{0,128},{4,132},{8,136},{12,140},{16,144},{20,148},{24,152},{28,15... | collective-permute-start | bytes 491528 | tf_op jit(solution)/shard_map/ppermute | solution.py:31
  68.8 2.0 %collective-permute-start.14 = (bf16[80,640]{1,0:T(8,128)(2,1)S(1)}, bf16[80,640]{1,0:T(8,128)(2,1)S(1)}, u32[]{:S(2)}, u32[]{:S(2)}) collective-permute-start(bf16[80,640]{1,0:T(8,128)(2,1)S(1)} %get-tuple-element.89), channel_id=1, source_target_pairs={{0,4},{4,0},{8,12},{12,8},{16,20},{20,16},{24,28},{28,24},{32,36},... | collective-permute-start | bytes 307208 | tf_op jit(solution)/shard_map/ppermute | solution.py:31
  70.9 2.6 %collective-permute-done.14.b = bf16[80,640]{1,0:T(8,128)(2,1)S(1)} collective-permute-done((bf16[80,640]{1,0:T(8,128)(2,1)S(1)}, bf16[80,640]{1,0:T(8,128)(2,1)S(1)}, u32[]{:S(2)}, u32[]{:S(2)}) %collective-permute-start.14) | collective-permute-done | bytes 102432 | tf_op jit(solution)/shard_map/ppermute | solution.py:31
  73.5 2.9 %collective-permute-done.16.d = bf16[80,640]{1,0:T(8,128)(2,1)S(1)} collective-permute-done((bf16[80,640]{1,0:T(8,128)(2,1)S(1)}, bf16[80,640]{1,0:T(8,128)(2,1)S(1)}, u32[]{:S(2)}, u32[]{:S(2)}) %collective-permute-start.16) | collective-permute-done | bytes 102432 | tf_op jit(solution)/shard_map/ppermute | solution.py:31
  77.2 6.6 %collective-permute-start.20 = (bf16[32,1024]{1,0:T(8,128)(2,1)S(1)}, bf16[32,1024]{1,0:T(8,128)(2,1)S(1)}, u32[]{:S(2)}, u32[]{:S(2)}) collective-permute-start(bf16[32,1024]{1,0:T(8,128)(2,1)S(1)} %get-tuple-element.98), channel_id=1, source_target_pairs={{0,16},{4,20},{8,24},{12,28},{16,0},{20,4},{24,8},{28,12},{32,48},... | collective-permute-start | bytes 196616 | tf_op jit(solution)/shard_map/ppermute | solution.py:31
  83.8 3.5 %collective-permute-done.22 = bf16[72,1024]{1,0:T(8,128)(2,1)S(1)} collective-permute-done((bf16[72,1024]{1,0:T(8,128)(2,1)S(1)}, bf16[72,1024]{1,0:T(8,128)(2,1)S(1)}, u32[]{:S(2)}, u32[]{:S(2)}) %collective-permute-start.22) | collective-permute-done | bytes 147488 | tf_op jit(solution)/shard_map/ppermute | solution.py:31
  87.4 1.2 %reshape.31 = f32[6,12,2,1024]{3,2,1,0:T(2,128)} reshape(f32[144,1024]{1,0:T(8,128)S(1)} %pad_maximum_fusion) | data formatting | bytes 1179648 | tf_op jit(solution)/shard_map/reshape | solution.py:514
  (72 shorter events, 8.8 us)
Async XLA Ops:
  3.5 20.2 %copy-start = (bf16[3,1024,256]{2,1,0:T(8,128)(2,1)S(1)}, bf16[3,1024,256]{2,1,0:T(8,128)(2,1)}, u32[]{:S(2)}) copy-start(bf16[3,1024,256]{2,1,0:T(8,128)(2,1)} %weight.1) | copy-start | bytes 4718596
  4.8 15.0 %collective-permute-start = (bf16[152,1024]{1,0:T(8,128)(2,1)S(1)}, bf16[152,1024]{1,0:T(8,128)(2,1)S(1)}, u32[]{:S(2)}, u32[]{:S(2)}) collective-permute-start(bf16[152,1024]{1,0:T(8,128)(2,1)S(1)} %pad_maximum_fusion.2), channel_id=1, source_target_pairs={{0,252},{4,0},{8,4},{12,8},{16,12},{20,16},{24,20},{28,24},{32,28}... | collective-permute-start | bytes 933896 | tf_op jit(solution)/shard_map/ppermute | solution.py:31
  13.3 10.4 %collective-permute-start.3 = (bf16[152,1024]{1,0:T(8,128)(2,1)S(1)}, bf16[152,1024]{1,0:T(8,128)(2,1)S(1)}, u32[]{:S(2)}, u32[]{:S(2)}) collective-permute-start(bf16[152,1024]{1,0:T(8,128)(2,1)S(1)} %pad_maximum_fusion.1.m0.refs_0_), channel_id=1, source_target_pairs={{0,2},{1,3},{2,0},{3,1},{4,6},{5,7},{6,4},{7,5},{8,10},{9,11},{10,... | collective-permute-start | bytes 933896 | tf_op jit(solution)/shard_map/ppermute | solution.py:31
  15.8 7.9 %collective-permute-start.1 = (bf16[152,1024]{1,0:T(8,128)(2,1)S(1)}, bf16[152,1024]{1,0:T(8,128)(2,1)S(1)}, u32[]{:S(2)}, u32[]{:S(2)}) collective-permute-start(bf16[152,1024]{1,0:T(8,128)(2,1)S(1)} %pad_maximum_fusion.1.m0.refs_0_), channel_id=1, source_target_pairs={{0,1},{1,0},{2,3},{3,2},{4,5},{5,4},{6,7},{7,6},{8,9},{9,8},{10,11... | collective-permute-start | bytes 933896 | tf_op jit(solution)/shard_map/ppermute | solution.py:31
  19.8 3.9 %collective-permute-start.2 = (bf16[152,1024]{1,0:T(8,128)(2,1)S(1)}, bf16[152,1024]{1,0:T(8,128)(2,1)S(1)}, u32[]{:S(2)}, u32[]{:S(2)}) collective-permute-start(bf16[152,1024]{1,0:T(8,128)(2,1)S(1)} %collective-permute-done.m1.refs_1_), channel_id=1, source_target_pairs={{0,1},{1,0},{2,3},{3,2},{4,5},{5,4},{6,7},{7,6},{8,9},{9,8},{10,11... | collective-permute-start | bytes 933896 | tf_op jit(solution)/shard_map/ppermute | solution.py:31
  19.8 11.3 %collective-permute-start.4 = (bf16[152,1024]{1,0:T(8,128)(2,1)S(1)}, bf16[152,1024]{1,0:T(8,128)(2,1)S(1)}, u32[]{:S(2)}, u32[]{:S(2)}) collective-permute-start(bf16[152,1024]{1,0:T(8,128)(2,1)S(1)} %collective-permute-done.m1.refs_1_), channel_id=1, source_target_pairs={{0,2},{1,3},{2,0},{3,1},{4,6},{5,7},{6,4},{7,5},{8,10},{9,11},{10,... | collective-permute-start | bytes 933896 | tf_op jit(solution)/shard_map/ppermute | solution.py:31
  23.7 7.4 %collective-permute-start.5 = (bf16[152,1024]{1,0:T(8,128)(2,1)S(1)}, bf16[152,1024]{1,0:T(8,128)(2,1)S(1)}, u32[]{:S(2)}, u32[]{:S(2)}) collective-permute-start(bf16[152,1024]{1,0:T(8,128)(2,1)S(1)} %collective-permute-done.3.refs_4_), channel_id=1, source_target_pairs={{0,1},{1,0},{2,3},{3,2},{4,5},{5,4},{6,7},{7,6},{8,9},{9,8},{10,11... | collective-permute-start | bytes 933896 | tf_op jit(solution)/shard_map/ppermute | solution.py:31
  31.1 1.6 %collective-permute-start.6 = (bf16[152,1024]{1,0:T(8,128)(2,1)S(1)}, bf16[152,1024]{1,0:T(8,128)(2,1)S(1)}, u32[]{:S(2)}, u32[]{:S(2)}) collective-permute-start(bf16[152,1024]{1,0:T(8,128)(2,1)S(1)} %collective-permute-done.4.refs_5_), channel_id=1, source_target_pairs={{0,1},{1,0},{2,3},{3,2},{4,5},{5,4},{6,7},{7,6},{8,9},{9,8},{10,11... | collective-permute-start | bytes 933896 | tf_op jit(solution)/shard_map/ppermute | solution.py:31
  40.9 3.5 %collective-permute-start.17 = (bf16[288,1024]{1,0:T(8,128)(2,1)S(1)}, bf16[288,1024]{1,0:T(8,128)(2,1)S(1)}, u32[]{:S(2)}, u32[]{:S(2)}) collective-permute-start(bf16[288,1024]{1,0:T(8,128)(2,1)S(1)} %get-tuple-element.94), channel_id=1, source_target_pairs={{0,1},{1,0},{2,3},{3,2},{4,5},{5,4},{6,7},{7,6},{8,9},{9,8},{10,11... | collective-permute-start | bytes 1769480 | tf_op jit(solution)/shard_map/ppermute | solution.py:31
  41.1 11.4 %collective-permute-start.10 = (bf16[512,384]{1,0:T(8,128)(2,1)S(1)}, bf16[512,384]{1,0:T(8,128)(2,1)S(1)}, u32[]{:S(2)}, u32[]{:S(2)}) collective-permute-start(bf16[512,384]{1,0:T(8,128)(2,1)S(1)} %get-tuple-element.83), channel_id=1, source_target_pairs={{0,4},{4,0},{8,12},{12,8},{16,20},{20,16},{24,28},{28,24},{32,36},... | collective-permute-start | bytes 1179656 | tf_op jit(solution)/shard_map/ppermute | solution.py:31
  41.1 19.7 %collective-permute-start.7 = (bf16[272,640]{1,0:T(8,128)(2,1)S(1)}, bf16[272,640]{1,0:T(8,128)(2,1)S(1)}, u32[]{:S(2)}, u32[]{:S(2)}) collective-permute-start(bf16[272,640]{1,0:T(8,128)(2,1)S(1)} %get-tuple-element.79), channel_id=1, source_target_pairs={{0,32},{4,36},{8,40},{12,44},{16,48},{20,52},{24,56},{28,60},{32,6... | collective-permute-start | bytes 1044488 | tf_op jit(solution)/shard_map/ppermute | solution.py:31
  41.2 19.6 %collective-permute-start.8 = (bf16[272,640]{1,0:T(8,128)(2,1)S(1)}, bf16[272,640]{1,0:T(8,128)(2,1)S(1)}, u32[]{:S(2)}, u32[]{:S(2)}) collective-permute-start(bf16[272,640]{1,0:T(8,128)(2,1)S(1)} %get-tuple-element.80), channel_id=1, source_target_pairs={{0,64},{4,68},{8,72},{12,76},{16,80},{20,84},{24,88},{28,92},{32,9... | collective-permute-start | bytes 1044488 | tf_op jit(solution)/shard_map/ppermute | solution.py:31
  43.4 18.4 %collective-permute-start.9 = (bf16[272,640]{1,0:T(8,128)(2,1)S(1)}, bf16[272,640]{1,0:T(8,128)(2,1)S(1)}, u32[]{:S(2)}, u32[]{:S(2)}) collective-permute-start(bf16[272,640]{1,0:T(8,128)(2,1)S(1)} %get-tuple-element.81), channel_id=1, source_target_pairs={{0,96},{4,100},{8,104},{12,108},{16,112},{20,116},{24,120},{28,124... | collective-permute-start | bytes 1044488 | tf_op jit(solution)/shard_map/ppermute | solution.py:31
  44.5 31.9 %collective-permute-start.18 = (bf16[144,1024]{1,0:T(8,128)(2,1)S(1)}, bf16[144,1024]{1,0:T(8,128)(2,1)S(1)}, u32[]{:S(2)}, u32[]{:S(2)}) collective-permute-start(bf16[144,1024]{1,0:T(8,128)(2,1)S(1)} %add_convert_fusion), channel_id=1, source_target_pairs={{0,2},{1,3},{2,0},{3,1},{4,6},{5,7},{6,4},{7,5},{8,10},{9,11},{10,... | collective-permute-start | bytes 884744 | tf_op jit(solution)/shard_map/ppermute | solution.py:31
  52.6 9.7 %collective-permute-start.11 = (bf16[128,384]{1,0:T(8,128)(2,1)S(1)}, bf16[128,384]{1,0:T(8,128)(2,1)S(1)}, u32[]{:S(2)}, u32[]{:S(2)}) collective-permute-start(bf16[128,384]{1,0:T(8,128)(2,1)S(1)} %get-tuple-element.85), channel_id=1, source_target_pairs={{0,32},{4,36},{8,40},{12,44},{16,48},{20,52},{24,56},{28,60},{32,6... | collective-permute-start | bytes 294920 | tf_op jit(solution)/shard_map/ppermute | solution.py:31
  60.8 6.1 %collective-permute-start.12 = (bf16[128,384]{1,0:T(8,128)(2,1)S(1)}, bf16[128,384]{1,0:T(8,128)(2,1)S(1)}, u32[]{:S(2)}, u32[]{:S(2)}) collective-permute-start(bf16[128,384]{1,0:T(8,128)(2,1)S(1)} %get-tuple-element.86), channel_id=1, source_target_pairs={{0,64},{4,68},{8,72},{12,76},{16,80},{20,84},{24,88},{28,92},{32,9... | collective-permute-start | bytes 294920 | tf_op jit(solution)/shard_map/ppermute | solution.py:31
  60.8 6.1 %collective-permute-start.13 = (bf16[128,384]{1,0:T(8,128)(2,1)S(1)}, bf16[128,384]{1,0:T(8,128)(2,1)S(1)}, u32[]{:S(2)}, u32[]{:S(2)}) collective-permute-start(bf16[128,384]{1,0:T(8,128)(2,1)S(1)} %get-tuple-element.87), channel_id=1, source_target_pairs={{0,96},{4,100},{8,104},{12,108},{16,112},{20,116},{24,120},{28,124... | collective-permute-start | bytes 294920 | tf_op jit(solution)/shard_map/ppermute | solution.py:31
  67.2 9.2 %collective-permute-start.15 = (bf16[80,1024]{1,0:T(8,128)(2,1)S(1)}, bf16[80,1024]{1,0:T(8,128)(2,1)S(1)}, u32[]{:S(2)}, u32[]{:S(2)}) collective-permute-start(bf16[80,1024]{1,0:T(8,128)(2,1)S(1)} %get-tuple-element.90), channel_id=1, source_target_pairs={{0,128},{4,132},{8,136},{12,140},{16,144},{20,148},{24,152},{28,15... | collective-permute-start | bytes 491528 | tf_op jit(solution)/shard_map/ppermute | solution.py:31
  68.8 4.7 %collective-permute-start.14 = (bf16[80,640]{1,0:T(8,128)(2,1)S(1)}, bf16[80,640]{1,0:T(8,128)(2,1)S(1)}, u32[]{:S(2)}, u32[]{:S(2)}) collective-permute-start(bf16[80,640]{1,0:T(8,128)(2,1)S(1)} %get-tuple-element.89), channel_id=1, source_target_pairs={{0,4},{4,0},{8,12},{12,8},{16,20},{20,16},{24,28},{28,24},{32,36},... | collective-permute-start | bytes 307208 | tf_op jit(solution)/shard_map/ppermute | solution.py:31
  70.8 5.6 %collective-permute-start.16 = (bf16[80,640]{1,0:T(8,128)(2,1)S(1)}, bf16[80,640]{1,0:T(8,128)(2,1)S(1)}, u32[]{:S(2)}, u32[]{:S(2)}) collective-permute-start(bf16[80,640]{1,0:T(8,128)(2,1)S(1)} %get-tuple-element.91), channel_id=1, source_target_pairs={{0,132},{4,128},{8,140},{12,136},{16,148},{20,144},{24,156},{28,15... | collective-permute-start | bytes 307208 | tf_op jit(solution)/shard_map/ppermute | solution.py:31
  76.7 10.7 %collective-permute-start.22 = (bf16[72,1024]{1,0:T(8,128)(2,1)S(1)}, bf16[72,1024]{1,0:T(8,128)(2,1)S(1)}, u32[]{:S(2)}, u32[]{:S(2)}) collective-permute-start(bf16[72,1024]{1,0:T(8,128)(2,1)S(1)} %get-tuple-element.100), channel_id=1, source_target_pairs={{0,4},{4,8},{8,12},{12,16},{16,20},{20,24},{24,28},{28,32},{32,36}... | collective-permute-start | bytes 442376 | tf_op jit(solution)/shard_map/ppermute | solution.py:31
  77.2 11.4 %collective-permute-start.19 = (bf16[32,1024]{1,0:T(8,128)(2,1)S(1)}, bf16[32,1024]{1,0:T(8,128)(2,1)S(1)}, u32[]{:S(2)}, u32[]{:S(2)}) collective-permute-start(bf16[32,1024]{1,0:T(8,128)(2,1)S(1)} %get-tuple-element.97), channel_id=1, source_target_pairs={{0,8},{4,12},{8,16},{12,20},{16,24},{20,28},{24,0},{28,4},{32,40},... | collective-permute-start | bytes 196616 | tf_op jit(solution)/shard_map/ppermute | solution.py:31
  77.2 11.4 %collective-permute-start.20 = (bf16[32,1024]{1,0:T(8,128)(2,1)S(1)}, bf16[32,1024]{1,0:T(8,128)(2,1)S(1)}, u32[]{:S(2)}, u32[]{:S(2)}) collective-permute-start(bf16[32,1024]{1,0:T(8,128)(2,1)S(1)} %get-tuple-element.98), channel_id=1, source_target_pairs={{0,16},{4,20},{8,24},{12,28},{16,0},{20,4},{24,8},{28,12},{32,48},... | collective-permute-start | bytes 196616 | tf_op jit(solution)/shard_map/ppermute | solution.py:31
  83.8 5.4 %collective-permute-start.21 = (bf16[32,1024]{1,0:T(8,128)(2,1)S(1)}, bf16[32,1024]{1,0:T(8,128)(2,1)S(1)}, u32[]{:S(2)}, u32[]{:S(2)}) collective-permute-start(bf16[32,1024]{1,0:T(8,128)(2,1)S(1)} %get-tuple-element.99), channel_id=1, source_target_pairs={{0,24},{4,28},{8,0},{12,4},{16,8},{20,12},{24,16},{28,20},{32,56},... | collective-permute-start | bytes 196616 | tf_op jit(solution)/shard_map/ppermute | solution.py:31
  (7 other events, 60.4 us)
